TPU v7x, 128 devices: a whole 4x4x4 slice. The times are simulated.
128 devices in a mesh: hst: 8 (over x, core), wide: 16 (over z, y).
Axes of the slice: x: 4, y: 4, z: 4, core: 2. Of those that a mesh axis runs over, the one named last changes fastest.
Arguments:
- dense_out: bfloat16 [32768, 128], P(('hst', 'wide')), may hold values from -6 to 6
- pooled: bfloat16 [32768, 8192], P(('hst', 'wide')), may hold values from -6 to 6
- dense_cot: bfloat16 [32768, 128], P(('hst', 'wide')), may hold values from -6 to 6
- pair_cot: bfloat16 [32768, 2080], P(('hst', 'wide')), may hold values from -0.75 to 0.75
- bag_ids: int32 [64, 8, 32768], P(None, None, ('hst', 'wide')), may hold values from 0 to 4095
- weights: float32 [64, 4096, 128], P('wide', 'hst'), may hold values from -3 to 3
- accum: float32 [64, 4096], P('wide', 'hst'), may hold values from 50 to 2000
Outputs:
- d_dense: bfloat16 [32768, 128], P(('hst', 'wide'))
- new_weights: float32 [64, 4096, 128], P('wide', 'hst')
- new_accum: float32 [64, 4096], P('wide', 'hst')
Inputs may be any that keep to these rules, and one draw needn't show every extreme that they name: `bag_ids`: each id names a row of its table.
All inputs are finite; a program needn't handle non-finite values.
Results may differ from a plain program's by a relative error of at most 0.0059.
Values may be sent and summed in bfloat16 or wider, within the bound.
No kernel may reach another device: no remote copies, remote signals or barrier semaphores. Data moves between devices by JAX's collectives and lax.ppermute only.
A program may use at most 192 MiB of HBM per device.

v0:
```python
import jax
import jax.numpy as jnp
from jax import lax
from jax.sharding import PartitionSpec as P

LEARN_RATE = 0.5
EPSILON = 1e-08


def pair_selector(num_pairs, num_feat):
    column = jnp.arange(num_feat * num_feat, dtype=jnp.int32)
    first = column // num_feat
    second = column % num_feat
    upper = jnp.maximum(first, second)
    lower = jnp.minimum(first, second)
    slots = upper * (upper - 1) // 2 + lower
    valid = first != second
    matches = (jnp.arange(num_pairs, dtype=jnp.int32)[:, None] == slots[None, :]) & valid[None, :]
    return matches.astype(jnp.bfloat16)


def window_sums(grads, ids_sample, length):
    block_rows = 512
    block_count = length // block_rows
    slot_count = ids_sample.shape[2]
    results = []
    for table in range(grads.shape[1]):
        grads_table = grads[:, table]
        ids_table = ids_sample[:, table]

        def one_block(start):
            positions = start + jnp.arange(block_rows, dtype=jnp.int32)
            counts = jnp.zeros((block_rows, ids_table.shape[0]), jnp.bfloat16)
            for slot in range(slot_count):
                counts = counts + (positions[:, None] == ids_table[None, :, slot]).astype(
                    jnp.bfloat16
                )
            return jnp.dot(counts, grads_table, preferred_element_type=jnp.float32)

        starts = jnp.arange(block_count, dtype=jnp.int32) * block_rows
        summed = lax.map(one_block, starts)
        results.append(summed.reshape(length, grads.shape[2]))
    return jnp.stack(results, 0)


def local(dense_out, pooled, dense_cot, pair_cot, bag_ids, weights, accum):
    samples = dense_out.shape[0]
    width = dense_out.shape[1]
    tables = bag_ids.shape[0]
    per_owner = weights.shape[0]
    row_block = weights.shape[1]
    wide_count = lax.axis_size("wide")
    num_feat = tables + 1
    features = jnp.concatenate([dense_out[:, None, :], pooled.reshape(samples, tables, width)], 1)
    selector = pair_selector(pair_cot.shape[1], num_feat)
    pair_grad = jnp.dot(pair_cot, selector, preferred_element_type=jnp.float32).astype(jnp.bfloat16)
    pair_grad = pair_grad.reshape(samples, num_feat, num_feat)
    feat_grads = jnp.einsum("bij,bje->bie", pair_grad, features, preferred_element_type=jnp.float32)
    d_dense = (feat_grads[:, 0] + dense_cot).astype(jnp.bfloat16)
    bag_grads = feat_grads[:, 1:].astype(jnp.bfloat16)
    received = lax.all_to_all(
        bag_grads.reshape(samples, wide_count, per_owner * width),
        "wide",
        split_axis=1,
        concat_axis=0,
        tiled=True,
    )
    received = received.reshape(wide_count * samples, per_owner, width)
    ids_received = lax.all_to_all(
        bag_ids.reshape(wide_count, per_owner, bag_ids.shape[1], samples),
        "wide",
        split_axis=0,
        concat_axis=3,
        tiled=True,
    )
    ids_sample = ids_received.reshape(per_owner, bag_ids.shape[1], wide_count * samples).transpose(
        2, 0, 1
    )
    summed = window_sums(received, ids_sample, row_block * lax.axis_size("hst"))
    row_grads = lax.psum_scatter(
        summed.transpose(1, 0, 2)
        .reshape(row_block * lax.axis_size("hst"), per_owner * width)
        .astype(jnp.bfloat16),
        "hst",
        scatter_dimension=0,
        tiled=True,
    ).astype(jnp.float32)
    row_grads = row_grads.reshape(row_block, per_owner, width).transpose(1, 0, 2)
    new_accum = accum + jnp.mean(row_grads * row_grads, -1)
    new_weights = weights - LEARN_RATE * row_grads / (jnp.sqrt(new_accum)[..., None] + EPSILON)
    return (d_dense, new_weights, new_accum)


def solution(mesh):
    in_specs = (
        P(("hst", "wide"), None),
        P(("hst", "wide"), None),
        P(("hst", "wide"), None),
        P(("hst", "wide"), None),
        P(None, None, ("hst", "wide")),
        P("wide", "hst", None),
        P("wide", "hst"),
    )
    out_specs = (P(("hst", "wide"), None), P("wide", "hst", None), P("wide", "hst"))
    return jax.shard_map(local, mesh=mesh, in_specs=in_specs, out_specs=out_specs, check_vma=False)
```

profile of v0, /device:TPU:0, one launch (start us, length us, event | category | flops | bytes accessed | tf_op | source)
XLA Modules:
  0.0 489.5 jit_solution(6332930653595601746)
XLA Ops:
  7.2 8.3 %all-to-all-start = ((s32[16,4,8,256]{3,2,1,0:T(8,128)}), s32[16,4,8,256]{3,2,1,0:T(8,128)}, u32[]{:S(2)}, u32[]{:S(2)}) async-start(s32[16,4,8,256]{3,2,1,0:T(8,128)} %bitcast.210), calls=%async_computation | async-start | bytes 1048576 | tf_op jit(solution)/shard_map/all_to_all | solution.py:69
  15.6 11.9 %fusion.72 = bf16[256,4225]{0,1:T(8,128)(2,1)} fusion(bf16[256,2080]{0,1:T(8,128)(2,1)S(1)} %copy-done, s32[4225]{0:T(1024)S(1)} %fusion.86, pred[4225]{0:T(1024)(128)(4,1)S(1)} %fusion.87), kind=kOutput, calls=%fused_computation.87 | convolution fusion | flops 4518113280 | bytes 3249285 | tf_op jit(solution)/shard_map/dot_general | solution.py:56
  30.7 5.3 %copy.41 = bf16[256,65,65]{2,1,0:T(8,128)(2,1)} copy(bf16[256,65,65]{0,2,1:T(8,128)(2,1)S(1)} %reshape.122) | data formatting | bytes 4326400 | tf_op jit(solution)/shard_map/reshape | solution.py:57
  42.4 3.7 copy-done.2
  49.5 7.0 %copy.55 = bf16[256,64,128]{0,2,1:T(8,128)(2,1)} copy(bf16[256,64,128]{2,1,0:T(8,128)(2,1)} %slice.156) | data formatting | bytes 8388608 | tf_op jit(solution)/shard_map/reshape | solution.py:62
  56.4 7.2 %all-to-all-start.1 = ((bf16[256,16,512]{0,2,1:T(8,128)(2,1)}), bf16[256,16,512]{0,2,1:T(8,128)(2,1)}, u32[]{:S(2)}, u32[]{:S(2)}) async-start(bf16[256,16,512]{0,2,1:T(8,128)(2,1)} %bitcast.200), calls=%async_computation.1 | async-start | bytes 8388608 | tf_op jit(solution)/shard_map/all_to_all | solution.py:61
  66.0 59.1 %all-to-all-done.1 = bf16[256,16,512]{0,2,1:T(8,128)(2,1)} async-done(((bf16[256,16,512]{0,2,1:T(8,128)(2,1)}), bf16[256,16,512]{0,2,1:T(8,128)(2,1)}, u32[]{:S(2)}, u32[]{:S(2)}) %all-to-all-start.1) | async-done | bytes 4194336 | tf_op jit(solution)/shard_map/all_to_all | solution.py:61
  125.2 6.5 %copy.44 = bf16[16,256,1,512]{1,0,3,2:T(8,128)(2,1)} copy(bf16[16,256,1,512]{1,3,0,2:T(8,128)(2,1)} %bitcast.50) | data formatting | bytes 8388608 | tf_op jit(solution)/shard_map/all_to_all | solution.py:61
  131.7 7.4 %reshape.127 = bf16[4096,4,128]{0,2,1:T(8,128)(2,1)} reshape(bf16[16,256,1,512]{1,0,3,2:T(8,128)(2,1)} %copy.44) | data formatting | bytes 8388608 | tf_op jit(solution)/shard_map/reshape | solution.py:68
  139.0 3.9 slice_bitcast_fusion.3
  143.8 62.3 %while.40 = (s32[]{:T(128)}, bf16[8,512,128]{2,1,0:T(8,128)(2,1)S(1)}, s32[8]{0:T(128)S(1)}, s32[4096,8]{0,1:T(8,128)S(1)}, bf16[4096,128]{1,0:T(8,128)(2,1)S(1)}, /*index=5*/s32[]{:T(128)}) while((s32[]{:T(128)}, bf16[8,512,128]{2,1,0:T(8,128)(2,1)S(1)}, s32[8]{0:T(128)S(1)}, s32[4096,8]{0,1:T(8,128)S(1)}, bf16[4096,128]{1,0:T(8,128)(2,1)S(1)}, ...), condition=%wide.region_1.2_spmd, body=%wide.region_0.1_spmd.sunk | while | flops 585105920 | bytes 1708121 | solution.py:41
  145.0 6.5 %fusion.122 = bf16[8,512,128]{2,1,0:T(8,128)(2,1)S(1)} fusion(bf16[8,512,128]{2,1,0:T(8,128)(2,1)S(1)} %get-tuple-element.515, s32[]{:T(128)} %get-tuple-element.514, bf16[4096,128]{1,0:T(8,128)(2,1)S(1)} %get-tuple-element.524, s32[4096]{0:T(1024)S(1)} %bitcast.213, s32[4096]{0:T(1024)S(1)} %bitcast.214, s32[4096]{0:T(1024)S(1)} %bitcast.215, ...), kind=kOutput, calls=%fused_computation.18.clone.1 | convolution fusion | flops 585105408 | bytes 1443844 | tf_op jit(solution)/shard_map/while/body/eval_jaxpr/dot_general | solution.py:38
  152.8 6.5 %fusion.122 = bf16[8,512,128]{2,1,0:T(8,128)(2,1)S(1)} fusion(bf16[8,512,128]{2,1,0:T(8,128)(2,1)S(1)} %get-tuple-element.515, s32[]{:T(128)} %get-tuple-element.514, bf16[4096,128]{1,0:T(8,128)(2,1)S(1)} %get-tuple-element.524, s32[4096]{0:T(1024)S(1)} %bitcast.213, s32[4096]{0:T(1024)S(1)} %bitcast.214, s32[4096]{0:T(1024)S(1)} %bitcast.215, ...), kind=kOutput, calls=%fused_computation.18.clone.1 | convolution fusion | flops 585105408 | bytes 1443844 | tf_op jit(solution)/shard_map/while/body/eval_jaxpr/dot_general | solution.py:38
  160.6 6.5 %fusion.122 = bf16[8,512,128]{2,1,0:T(8,128)(2,1)S(1)} fusion(bf16[8,512,128]{2,1,0:T(8,128)(2,1)S(1)} %get-tuple-element.515, s32[]{:T(128)} %get-tuple-element.514, bf16[4096,128]{1,0:T(8,128)(2,1)S(1)} %get-tuple-element.524, s32[4096]{0:T(1024)S(1)} %bitcast.213, s32[4096]{0:T(1024)S(1)} %bitcast.214, s32[4096]{0:T(1024)S(1)} %bitcast.215, ...), kind=kOutput, calls=%fused_computation.18.clone.1 | convolution fusion | flops 585105408 | bytes 1443844 | tf_op jit(solution)/shard_map/while/body/eval_jaxpr/dot_general | solution.py:38
  168.4 6.5 %fusion.122 = bf16[8,512,128]{2,1,0:T(8,128)(2,1)S(1)} fusion(bf16[8,512,128]{2,1,0:T(8,128)(2,1)S(1)} %get-tuple-element.515, s32[]{:T(128)} %get-tuple-element.514, bf16[4096,128]{1,0:T(8,128)(2,1)S(1)} %get-tuple-element.524, s32[4096]{0:T(1024)S(1)} %bitcast.213, s32[4096]{0:T(1024)S(1)} %bitcast.214, s32[4096]{0:T(1024)S(1)} %bitcast.215, ...), kind=kOutput, calls=%fused_computation.18.clone.1 | convolution fusion | flops 585105408 | bytes 1443844 | tf_op jit(solution)/shard_map/while/body/eval_jaxpr/dot_general | solution.py:38
  176.2 6.5 %fusion.122 = bf16[8,512,128]{2,1,0:T(8,128)(2,1)S(1)} fusion(bf16[8,512,128]{2,1,0:T(8,128)(2,1)S(1)} %get-tuple-element.515, s32[]{:T(128)} %get-tuple-element.514, bf16[4096,128]{1,0:T(8,128)(2,1)S(1)} %get-tuple-element.524, s32[4096]{0:T(1024)S(1)} %bitcast.213, s32[4096]{0:T(1024)S(1)} %bitcast.214, s32[4096]{0:T(1024)S(1)} %bitcast.215, ...), kind=kOutput, calls=%fused_computation.18.clone.1 | convolution fusion | flops 585105408 | bytes 1443844 | tf_op jit(solution)/shard_map/while/body/eval_jaxpr/dot_general | solution.py:38
  184.0 6.5 %fusion.122 = bf16[8,512,128]{2,1,0:T(8,128)(2,1)S(1)} fusion(bf16[8,512,128]{2,1,0:T(8,128)(2,1)S(1)} %get-tuple-element.515, s32[]{:T(128)} %get-tuple-element.514, bf16[4096,128]{1,0:T(8,128)(2,1)S(1)} %get-tuple-element.524, s32[4096]{0:T(1024)S(1)} %bitcast.213, s32[4096]{0:T(1024)S(1)} %bitcast.214, s32[4096]{0:T(1024)S(1)} %bitcast.215, ...), kind=kOutput, calls=%fused_computation.18.clone.1 | convolution fusion | flops 585105408 | bytes 1443844 | tf_op jit(solution)/shard_map/while/body/eval_jaxpr/dot_general | solution.py:38
  191.7 6.5 %fusion.122 = bf16[8,512,128]{2,1,0:T(8,128)(2,1)S(1)} fusion(bf16[8,512,128]{2,1,0:T(8,128)(2,1)S(1)} %get-tuple-element.515, s32[]{:T(128)} %get-tuple-element.514, bf16[4096,128]{1,0:T(8,128)(2,1)S(1)} %get-tuple-element.524, s32[4096]{0:T(1024)S(1)} %bitcast.213, s32[4096]{0:T(1024)S(1)} %bitcast.214, s32[4096]{0:T(1024)S(1)} %bitcast.215, ...), kind=kOutput, calls=%fused_computation.18.clone.1 | convolution fusion | flops 585105408 | bytes 1443844 | tf_op jit(solution)/shard_map/while/body/eval_jaxpr/dot_general | solution.py:38
  199.5 6.5 %fusion.122 = bf16[8,512,128]{2,1,0:T(8,128)(2,1)S(1)} fusion(bf16[8,512,128]{2,1,0:T(8,128)(2,1)S(1)} %get-tuple-element.515, s32[]{:T(128)} %get-tuple-element.514, bf16[4096,128]{1,0:T(8,128)(2,1)S(1)} %get-tuple-element.524, s32[4096]{0:T(1024)S(1)} %bitcast.213, s32[4096]{0:T(1024)S(1)} %bitcast.214, s32[4096]{0:T(1024)S(1)} %bitcast.215, ...), kind=kOutput, calls=%fused_computation.18.clone.1 | convolution fusion | flops 585105408 | bytes 1443844 | tf_op jit(solution)/shard_map/while/body/eval_jaxpr/dot_general | solution.py:38
  209.0 72.3 %while.41 = (s32[]{:T(128)}, bf16[8,512,128]{2,1,0:T(8,128)(2,1)S(1)}, s32[8]{0:T(128)S(1)}, s32[4096,8]{0,1:T(8,128)S(1)}, bf16[4096,128]{1,0:T(8,128)(2,1)}, /*index=5*/s32[]{:T(128)}) while((s32[]{:T(128)}, bf16[8,512,128]{2,1,0:T(8,128)(2,1)S(1)}, s32[8]{0:T(128)S(1)}, s32[4096,8]{0,1:T(8,128)S(1)}, bf16[4096,128]{1,0:T(8,128)(2,1)}, ...), condition=%wide.region_3.4_spmd, body=%wide.region_2.3_spmd.sunk | while | flops 585105920 | bytes 1708121 | solution.py:41
  210.5 7.7 %fusion.126 = bf16[8,512,128]{2,1,0:T(8,128)(2,1)S(1)} fusion(bf16[8,512,128]{2,1,0:T(8,128)(2,1)S(1)} %get-tuple-element.497, s32[]{:T(128)} %get-tuple-element.496, bf16[4096,128]{1,0:T(8,128)(2,1)} %get-tuple-element.506, s32[4096]{0:T(1024)S(1)} %bitcast.221, s32[4096]{0:T(1024)S(1)} %bitcast.222, s32[4096]{0:T(1024)S(1)} %bitcast.223, ...), kind=kOutput, calls=%fused_computation.38.clone.1 | convolution fusion | flops 585105408 | bytes 1443844 | tf_op jit(solution)/shard_map/while/body/eval_jaxpr/dot_general | solution.py:38
  219.5 7.7 %fusion.126 = bf16[8,512,128]{2,1,0:T(8,128)(2,1)S(1)} fusion(bf16[8,512,128]{2,1,0:T(8,128)(2,1)S(1)} %get-tuple-element.497, s32[]{:T(128)} %get-tuple-element.496, bf16[4096,128]{1,0:T(8,128)(2,1)} %get-tuple-element.506, s32[4096]{0:T(1024)S(1)} %bitcast.221, s32[4096]{0:T(1024)S(1)} %bitcast.222, s32[4096]{0:T(1024)S(1)} %bitcast.223, ...), kind=kOutput, calls=%fused_computation.38.clone.1 | convolution fusion | flops 585105408 | bytes 1443844 | tf_op jit(solution)/shard_map/while/body/eval_jaxpr/dot_general | solution.py:38
  228.5 7.7 %fusion.126 = bf16[8,512,128]{2,1,0:T(8,128)(2,1)S(1)} fusion(bf16[8,512,128]{2,1,0:T(8,128)(2,1)S(1)} %get-tuple-element.497, s32[]{:T(128)} %get-tuple-element.496, bf16[4096,128]{1,0:T(8,128)(2,1)} %get-tuple-element.506, s32[4096]{0:T(1024)S(1)} %bitcast.221, s32[4096]{0:T(1024)S(1)} %bitcast.222, s32[4096]{0:T(1024)S(1)} %bitcast.223, ...), kind=kOutput, calls=%fused_computation.38.clone.1 | convolution fusion | flops 585105408 | bytes 1443844 | tf_op jit(solution)/shard_map/while/body/eval_jaxpr/dot_general | solution.py:38
  237.5 7.7 %fusion.126 = bf16[8,512,128]{2,1,0:T(8,128)(2,1)S(1)} fusion(bf16[8,512,128]{2,1,0:T(8,128)(2,1)S(1)} %get-tuple-element.497, s32[]{:T(128)} %get-tuple-element.496, bf16[4096,128]{1,0:T(8,128)(2,1)} %get-tuple-element.506, s32[4096]{0:T(1024)S(1)} %bitcast.221, s32[4096]{0:T(1024)S(1)} %bitcast.222, s32[4096]{0:T(1024)S(1)} %bitcast.223, ...), kind=kOutput, calls=%fused_computation.38.clone.1 | convolution fusion | flops 585105408 | bytes 1443844 | tf_op jit(solution)/shard_map/while/body/eval_jaxpr/dot_general | solution.py:38
  246.5 7.7 %fusion.126 = bf16[8,512,128]{2,1,0:T(8,128)(2,1)S(1)} fusion(bf16[8,512,128]{2,1,0:T(8,128)(2,1)S(1)} %get-tuple-element.497, s32[]{:T(128)} %get-tuple-element.496, bf16[4096,128]{1,0:T(8,128)(2,1)} %get-tuple-element.506, s32[4096]{0:T(1024)S(1)} %bitcast.221, s32[4096]{0:T(1024)S(1)} %bitcast.222, s32[4096]{0:T(1024)S(1)} %bitcast.223, ...), kind=kOutput, calls=%fused_computation.38.clone.1 | convolution fusion | flops 585105408 | bytes 1443844 | tf_op jit(solution)/shard_map/while/body/eval_jaxpr/dot_general | solution.py:38
  255.6 7.7 %fusion.126 = bf16[8,512,128]{2,1,0:T(8,128)(2,1)S(1)} fusion(bf16[8,512,128]{2,1,0:T(8,128)(2,1)S(1)} %get-tuple-element.497, s32[]{:T(128)} %get-tuple-element.496, bf16[4096,128]{1,0:T(8,128)(2,1)} %get-tuple-element.506, s32[4096]{0:T(1024)S(1)} %bitcast.221, s32[4096]{0:T(1024)S(1)} %bitcast.222, s32[4096]{0:T(1024)S(1)} %bitcast.223, ...), kind=kOutput, calls=%fused_computation.38.clone.1 | convolution fusion | flops 585105408 | bytes 1443844 | tf_op jit(solution)/shard_map/while/body/eval_jaxpr/dot_general | solution.py:38
  264.6 7.7 %fusion.126 = bf16[8,512,128]{2,1,0:T(8,128)(2,1)S(1)} fusion(bf16[8,512,128]{2,1,0:T(8,128)(2,1)S(1)} %get-tuple-element.497, s32[]{:T(128)} %get-tuple-element.496, bf16[4096,128]{1,0:T(8,128)(2,1)} %get-tuple-element.506, s32[4096]{0:T(1024)S(1)} %bitcast.221, s32[4096]{0:T(1024)S(1)} %bitcast.222, s32[4096]{0:T(1024)S(1)} %bitcast.223, ...), kind=kOutput, calls=%fused_computation.38.clone.1 | convolution fusion | flops 585105408 | bytes 1443844 | tf_op jit(solution)/shard_map/while/body/eval_jaxpr/dot_general | solution.py:38
  273.6 7.7 %fusion.126 = bf16[8,512,128]{2,1,0:T(8,128)(2,1)S(1)} fusion(bf16[8,512,128]{2,1,0:T(8,128)(2,1)S(1)} %get-tuple-element.497, s32[]{:T(128)} %get-tuple-element.496, bf16[4096,128]{1,0:T(8,128)(2,1)} %get-tuple-element.506, s32[4096]{0:T(1024)S(1)} %bitcast.221, s32[4096]{0:T(1024)S(1)} %bitcast.222, s32[4096]{0:T(1024)S(1)} %bitcast.223, ...), kind=kOutput, calls=%fused_computation.38.clone.1 | convolution fusion | flops 585105408 | bytes 1443844 | tf_op jit(solution)/shard_map/while/body/eval_jaxpr/dot_general | solution.py:38
  285.1 74.1 %while.42 = (s32[]{:T(128)}, bf16[8,512,128]{2,1,0:T(8,128)(2,1)S(1)}, s32[8]{0:T(128)S(1)}, s32[4096,8]{0,1:T(8,128)S(1)}, bf16[4096,128]{1,0:T(8,128)(2,1)}, /*index=5*/s32[]{:T(128)}) while((s32[]{:T(128)}, bf16[8,512,128]{2,1,0:T(8,128)(2,1)S(1)}, s32[8]{0:T(128)S(1)}, s32[4096,8]{0,1:T(8,128)S(1)}, bf16[4096,128]{1,0:T(8,128)(2,1)}, ...), condition=%wide.region_5.6_spmd, body=%wide.region_4.5_spmd.sunk | while | flops 585105920 | bytes 1708121 | solution.py:41
  286.8 7.7 %fusion.130 = bf16[8,512,128]{2,1,0:T(8,128)(2,1)S(1)} fusion(bf16[8,512,128]{2,1,0:T(8,128)(2,1)S(1)} %get-tuple-element.479, s32[]{:T(128)} %get-tuple-element.478, bf16[4096,128]{1,0:T(8,128)(2,1)} %get-tuple-element.488, s32[4096]{0:T(1024)S(1)} %bitcast.229, s32[4096]{0:T(1024)S(1)} %bitcast.230, s32[4096]{0:T(1024)S(1)} %bitcast.231, ...), kind=kOutput, calls=%fused_computation.58.clone.1 | convolution fusion | flops 585105408 | bytes 1443844 | tf_op jit(solution)/shard_map/while/body/eval_jaxpr/dot_general | solution.py:38
  296.0 7.7 %fusion.130 = bf16[8,512,128]{2,1,0:T(8,128)(2,1)S(1)} fusion(bf16[8,512,128]{2,1,0:T(8,128)(2,1)S(1)} %get-tuple-element.479, s32[]{:T(128)} %get-tuple-element.478, bf16[4096,128]{1,0:T(8,128)(2,1)} %get-tuple-element.488, s32[4096]{0:T(1024)S(1)} %bitcast.229, s32[4096]{0:T(1024)S(1)} %bitcast.230, s32[4096]{0:T(1024)S(1)} %bitcast.231, ...), kind=kOutput, calls=%fused_computation.58.clone.1 | convolution fusion | flops 585105408 | bytes 1443844 | tf_op jit(solution)/shard_map/while/body/eval_jaxpr/dot_general | solution.py:38
  305.3 7.7 %fusion.130 = bf16[8,512,128]{2,1,0:T(8,128)(2,1)S(1)} fusion(bf16[8,512,128]{2,1,0:T(8,128)(2,1)S(1)} %get-tuple-element.479, s32[]{:T(128)} %get-tuple-element.478, bf16[4096,128]{1,0:T(8,128)(2,1)} %get-tuple-element.488, s32[4096]{0:T(1024)S(1)} %bitcast.229, s32[4096]{0:T(1024)S(1)} %bitcast.230, s32[4096]{0:T(1024)S(1)} %bitcast.231, ...), kind=kOutput, calls=%fused_computation.58.clone.1 | convolution fusion | flops 585105408 | bytes 1443844 | tf_op jit(solution)/shard_map/while/body/eval_jaxpr/dot_general | solution.py:38
  314.5 7.7 %fusion.130 = bf16[8,512,128]{2,1,0:T(8,128)(2,1)S(1)} fusion(bf16[8,512,128]{2,1,0:T(8,128)(2,1)S(1)} %get-tuple-element.479, s32[]{:T(128)} %get-tuple-element.478, bf16[4096,128]{1,0:T(8,128)(2,1)} %get-tuple-element.488, s32[4096]{0:T(1024)S(1)} %bitcast.229, s32[4096]{0:T(1024)S(1)} %bitcast.230, s32[4096]{0:T(1024)S(1)} %bitcast.231, ...), kind=kOutput, calls=%fused_computation.58.clone.1 | convolution fusion | flops 585105408 | bytes 1443844 | tf_op jit(solution)/shard_map/while/body/eval_jaxpr/dot_general | solution.py:38
  323.7 7.7 %fusion.130 = bf16[8,512,128]{2,1,0:T(8,128)(2,1)S(1)} fusion(bf16[8,512,128]{2,1,0:T(8,128)(2,1)S(1)} %get-tuple-element.479, s32[]{:T(128)} %get-tuple-element.478, bf16[4096,128]{1,0:T(8,128)(2,1)} %get-tuple-element.488, s32[4096]{0:T(1024)S(1)} %bitcast.229, s32[4096]{0:T(1024)S(1)} %bitcast.230, s32[4096]{0:T(1024)S(1)} %bitcast.231, ...), kind=kOutput, calls=%fused_computation.58.clone.1 | convolution fusion | flops 585105408 | bytes 1443844 | tf_op jit(solution)/shard_map/while/body/eval_jaxpr/dot_general | solution.py:38
  333.0 7.7 %fusion.130 = bf16[8,512,128]{2,1,0:T(8,128)(2,1)S(1)} fusion(bf16[8,512,128]{2,1,0:T(8,128)(2,1)S(1)} %get-tuple-element.479, s32[]{:T(128)} %get-tuple-element.478, bf16[4096,128]{1,0:T(8,128)(2,1)} %get-tuple-element.488, s32[4096]{0:T(1024)S(1)} %bitcast.229, s32[4096]{0:T(1024)S(1)} %bitcast.230, s32[4096]{0:T(1024)S(1)} %bitcast.231, ...), kind=kOutput, calls=%fused_computation.58.clone.1 | convolution fusion | flops 585105408 | bytes 1443844 | tf_op jit(solution)/shard_map/while/body/eval_jaxpr/dot_general | solution.py:38
  342.2 7.7 %fusion.130 = bf16[8,512,128]{2,1,0:T(8,128)(2,1)S(1)} fusion(bf16[8,512,128]{2,1,0:T(8,128)(2,1)S(1)} %get-tuple-element.479, s32[]{:T(128)} %get-tuple-element.478, bf16[4096,128]{1,0:T(8,128)(2,1)} %get-tuple-element.488, s32[4096]{0:T(1024)S(1)} %bitcast.229, s32[4096]{0:T(1024)S(1)} %bitcast.230, s32[4096]{0:T(1024)S(1)} %bitcast.231, ...), kind=kOutput, calls=%fused_computation.58.clone.1 | convolution fusion | flops 585105408 | bytes 1443844 | tf_op jit(solution)/shard_map/while/body/eval_jaxpr/dot_general | solution.py:38
  351.4 7.7 %fusion.130 = bf16[8,512,128]{2,1,0:T(8,128)(2,1)S(1)} fusion(bf16[8,512,128]{2,1,0:T(8,128)(2,1)S(1)} %get-tuple-element.479, s32[]{:T(128)} %get-tuple-element.478, bf16[4096,128]{1,0:T(8,128)(2,1)} %get-tuple-element.488, s32[4096]{0:T(1024)S(1)} %bitcast.229, s32[4096]{0:T(1024)S(1)} %bitcast.230, s32[4096]{0:T(1024)S(1)} %bitcast.231, ...), kind=kOutput, calls=%fused_computation.58.clone.1 | convolution fusion | flops 585105408 | bytes 1443844 | tf_op jit(solution)/shard_map/while/body/eval_jaxpr/dot_general | solution.py:38
  363.0 73.2 %while.43 = (s32[]{:T(128)}, bf16[8,512,128]{2,1,0:T(8,128)(2,1)S(1)}, s32[8]{0:T(128)S(1)}, s32[4096,8]{0,1:T(8,128)S(1)}, bf16[4096,128]{1,0:T(8,128)(2,1)}, /*index=5*/s32[]{:T(128)}) while((s32[]{:T(128)}, bf16[8,512,128]{2,1,0:T(8,128)(2,1)S(1)}, s32[8]{0:T(128)S(1)}, s32[4096,8]{0,1:T(8,128)S(1)}, bf16[4096,128]{1,0:T(8,128)(2,1)}, ...), condition=%wide.region_7.8_spmd, body=%wide.region_6.7_spmd.sunk | while | flops 585105920 | bytes 1708121 | solution.py:41
  364.6 7.7 %fusion.134 = bf16[8,512,128]{2,1,0:T(8,128)(2,1)S(1)} fusion(bf16[8,512,128]{2,1,0:T(8,128)(2,1)S(1)} %get-tuple-element.461, s32[]{:T(128)} %get-tuple-element.460, bf16[4096,128]{1,0:T(8,128)(2,1)} %get-tuple-element.470, s32[4096]{0:T(1024)S(1)} %bitcast.237, s32[4096]{0:T(1024)S(1)} %bitcast.238, s32[4096]{0:T(1024)S(1)} %bitcast.239, ...), kind=kOutput, calls=%fused_computation.78.clone.1 | convolution fusion | flops 585105408 | bytes 1443844 | tf_op jit(solution)/shard_map/while/body/eval_jaxpr/dot_general | solution.py:38
  373.7 7.7 %fusion.134 = bf16[8,512,128]{2,1,0:T(8,128)(2,1)S(1)} fusion(bf16[8,512,128]{2,1,0:T(8,128)(2,1)S(1)} %get-tuple-element.461, s32[]{:T(128)} %get-tuple-element.460, bf16[4096,128]{1,0:T(8,128)(2,1)} %get-tuple-element.470, s32[4096]{0:T(1024)S(1)} %bitcast.237, s32[4096]{0:T(1024)S(1)} %bitcast.238, s32[4096]{0:T(1024)S(1)} %bitcast.239, ...), kind=kOutput, calls=%fused_computation.78.clone.1 | convolution fusion | flops 585105408 | bytes 1443844 | tf_op jit(solution)/shard_map/while/body/eval_jaxpr/dot_general | solution.py:38
  382.8 7.7 %fusion.134 = bf16[8,512,128]{2,1,0:T(8,128)(2,1)S(1)} fusion(bf16[8,512,128]{2,1,0:T(8,128)(2,1)S(1)} %get-tuple-element.461, s32[]{:T(128)} %get-tuple-element.460, bf16[4096,128]{1,0:T(8,128)(2,1)} %get-tuple-element.470, s32[4096]{0:T(1024)S(1)} %bitcast.237, s32[4096]{0:T(1024)S(1)} %bitcast.238, s32[4096]{0:T(1024)S(1)} %bitcast.239, ...), kind=kOutput, calls=%fused_computation.78.clone.1 | convolution fusion | flops 585105408 | bytes 1443844 | tf_op jit(solution)/shard_map/while/body/eval_jaxpr/dot_general | solution.py:38
  391.9 7.7 %fusion.134 = bf16[8,512,128]{2,1,0:T(8,128)(2,1)S(1)} fusion(bf16[8,512,128]{2,1,0:T(8,128)(2,1)S(1)} %get-tuple-element.461, s32[]{:T(128)} %get-tuple-element.460, bf16[4096,128]{1,0:T(8,128)(2,1)} %get-tuple-element.470, s32[4096]{0:T(1024)S(1)} %bitcast.237, s32[4096]{0:T(1024)S(1)} %bitcast.238, s32[4096]{0:T(1024)S(1)} %bitcast.239, ...), kind=kOutput, calls=%fused_computation.78.clone.1 | convolution fusion | flops 585105408 | bytes 1443844 | tf_op jit(solution)/shard_map/while/body/eval_jaxpr/dot_general | solution.py:38
  401.1 7.7 %fusion.134 = bf16[8,512,128]{2,1,0:T(8,128)(2,1)S(1)} fusion(bf16[8,512,128]{2,1,0:T(8,128)(2,1)S(1)} %get-tuple-element.461, s32[]{:T(128)} %get-tuple-element.460, bf16[4096,128]{1,0:T(8,128)(2,1)} %get-tuple-element.470, s32[4096]{0:T(1024)S(1)} %bitcast.237, s32[4096]{0:T(1024)S(1)} %bitcast.238, s32[4096]{0:T(1024)S(1)} %bitcast.239, ...), kind=kOutput, calls=%fused_computation.78.clone.1 | convolution fusion | flops 585105408 | bytes 1443844 | tf_op jit(solution)/shard_map/while/body/eval_jaxpr/dot_general | solution.py:38
  410.2 7.7 %fusion.134 = bf16[8,512,128]{2,1,0:T(8,128)(2,1)S(1)} fusion(bf16[8,512,128]{2,1,0:T(8,128)(2,1)S(1)} %get-tuple-element.461, s32[]{:T(128)} %get-tuple-element.460, bf16[4096,128]{1,0:T(8,128)(2,1)} %get-tuple-element.470, s32[4096]{0:T(1024)S(1)} %bitcast.237, s32[4096]{0:T(1024)S(1)} %bitcast.238, s32[4096]{0:T(1024)S(1)} %bitcast.239, ...), kind=kOutput, calls=%fused_computation.78.clone.1 | convolution fusion | flops 585105408 | bytes 1443844 | tf_op jit(solution)/shard_map/while/body/eval_jaxpr/dot_general | solution.py:38
  419.3 7.7 %fusion.134 = bf16[8,512,128]{2,1,0:T(8,128)(2,1)S(1)} fusion(bf16[8,512,128]{2,1,0:T(8,128)(2,1)S(1)} %get-tuple-element.461, s32[]{:T(128)} %get-tuple-element.460, bf16[4096,128]{1,0:T(8,128)(2,1)} %get-tuple-element.470, s32[4096]{0:T(1024)S(1)} %bitcast.237, s32[4096]{0:T(1024)S(1)} %bitcast.238, s32[4096]{0:T(1024)S(1)} %bitcast.239, ...), kind=kOutput, calls=%fused_computation.78.clone.1 | convolution fusion | flops 585105408 | bytes 1443844 | tf_op jit(solution)/shard_map/while/body/eval_jaxpr/dot_general | solution.py:38
  428.4 7.8 %fusion.134 = bf16[8,512,128]{2,1,0:T(8,128)(2,1)S(1)} fusion(bf16[8,512,128]{2,1,0:T(8,128)(2,1)S(1)} %get-tuple-element.461, s32[]{:T(128)} %get-tuple-element.460, bf16[4096,128]{1,0:T(8,128)(2,1)} %get-tuple-element.470, s32[4096]{0:T(1024)S(1)} %bitcast.237, s32[4096]{0:T(1024)S(1)} %bitcast.238, s32[4096]{0:T(1024)S(1)} %bitcast.239, ...), kind=kOutput, calls=%fused_computation.78.clone.1 | convolution fusion | flops 585105408 | bytes 1443844 | tf_op jit(solution)/shard_map/while/body/eval_jaxpr/dot_general | solution.py:38
  436.7 3.5 pad_maximum_fusion
  442.8 34.9 %reduce-scatter.2.cloned.1.call-done = bf16[512,512]{0,1:T(8,128)(2,1)} async-done(((bf16[4096,512]{0,1:T(8,128)(2,1)}), bf16[512,512]{0,1:T(8,128)(2,1)}) %reduce-scatter.2.cloned.1.call-update) | async-done | bytes 524304 | tf_op jit(solution)/shard_map/reduce_scatter | solution.py:80
  (147 shorter events, 75.9 us)
Async XLA Ops:
  7.2 8.4 %copy-start = (bf16[256,2080]{0,1:T(8,128)(2,1)S(1)}, bf16[256,2080]{0,1:T(8,128)(2,1)}, u32[]{:S(2)}) copy-start(bf16[256,2080]{0,1:T(8,128)(2,1)} %param.18) | copy-start | bytes 3194884
  7.2 49.3 %all-to-all-start = ((s32[16,4,8,256]{3,2,1,0:T(8,128)}), s32[16,4,8,256]{3,2,1,0:T(8,128)}, u32[]{:S(2)}, u32[]{:S(2)}) async-start(s32[16,4,8,256]{3,2,1,0:T(8,128)} %bitcast.210), calls=%async_computation | async-start | bytes 1048576 | tf_op jit(solution)/shard_map/all_to_all | solution.py:69
  36.0 3.5 copy-start.6
  36.0 3.7 copy-start.3
  42.4 3.7 copy-start.2
  56.4 68.7 %all-to-all-start.1 = ((bf16[256,16,512]{0,2,1:T(8,128)(2,1)}), bf16[256,16,512]{0,2,1:T(8,128)(2,1)}, u32[]{:S(2)}, u32[]{:S(2)}) async-start(bf16[256,16,512]{0,2,1:T(8,128)(2,1)} %bitcast.200), calls=%async_computation.1 | async-start | bytes 8388608 | tf_op jit(solution)/shard_map/all_to_all | solution.py:61
  63.7 414.0 %reduce-scatter.2.cloned.1.call-start = ((), (), s32[]{:S(2)}) async-start(), calls=%async_computation.3 | async-start | bytes 4718592 | tf_op jit(solution)/shard_map/reduce_scatter | solution.py:80
  359.2 3.7 copy-start.4
  440.3 1.6 copy-start.5
  440.3 1.9 copy-start.7
  440.3 38.6 %copy-start.8 = (f32[4,512]{1,0:T(4,128)S(1)}, f32[4,512]{1,0:T(4,128)}, u32[]{:S(2)}) copy-start(f32[4,512]{1,0:T(4,128)} %param.21) | copy-start | bytes 24580
  441.8 40.4 %copy-start.1 = (bf16[256,2080]{0,1:T(8,128)(2,1)S(1)}, bf16[256,2080]{0,1:T(8,128)(2,1)}, u32[]{:S(2)}) copy-start(bf16[256,2080]{0,1:T(8,128)(2,1)} %param.18) | copy-start | bytes 3194884
Sparse Core Ops, SparseCore 0:
  440.4 37.2 reduce-scatter.1
where the time goes:
time: 499 us; the launch traced here: 490 us
  matrix products  253 us (51%)
  waiting for transfers between devices  94 us (19%)
  local copies, waits for them, and re-layouts  83 us (17%)
  other arithmetic  27.2 us (5%)
  starting transfers between devices  15.8 us (3%)
  between operations  14.8 us (3%)
    dot_general x32, matrix products, one_block(): return jnp.dot(counts, grads_table, preferred_element_type=jnp.float32)  238 us
    all_to_all x1, waiting for transfers between devices, local(): lax.all_to_all(bag_grads.reshape(samples, wide_count, per_owner * width),...  59.1 us
    reduce_scatter x1, waiting for transfers between devices, local(): lax.psum_scatter(summed.transpose(1, 0, 2).reshape(row_block * lax.axis_s...  34.9 us
    add x32, other arithmetic, one_block(): positions = start + jnp.arange(block_rows, dtype=jnp.int32)  19.8 us
    dynamic_slice x32, local copies, waits for them, and re-layouts, window_sums(): summed = lax.map(one_block, starts)  19 us
    dot_general x1, matrix products, local(): jnp.dot(pair_cot, selector, preferred_element_type=jnp.float32)  11.9 us
  transfers between devices with their start and end apart: 3, of which 2 were waited for; matrix products, arithmetic and copies ran while one was open for 9% of the time, Pallas kernels for 0%

commit v1 on v0

v1 whole, which is shorter than its diff:
```python
import functools

import jax
import jax.numpy as jnp
from jax import lax
from jax.experimental import pallas as pl
from jax.experimental.pallas import tpu as pltpu
from jax.sharding import PartitionSpec as P

LEARN_RATE = 0.5
EPSILON = 1e-08
LANES = 128
HALF = 64
FIELD = 4
VMEM = 48 << 20
SEND_CHUNKS = ((0, 1, 2, 3),)
SUM_CHUNKS = ((0, 1), (2, 3))
BF16 = jnp.bfloat16
F32 = jnp.float32


def cost(micros):
    return pl.CostEstimate(flops=int(micros * 1.15e9), bytes_accessed=1 << 20, transcendentals=0)


def params():
    return pltpu.CompilerParams(vmem_limit_bytes=VMEM)


def interact_kernel(
    chunks, dense_ref, pooled_ref, cot_ref, pair_ref, d_dense_ref, *rest
):
    send_refs = rest[: len(chunks)]
    wide_pairs, lower, feats, grads = rest[len(chunks) :]
    block = dense_ref.shape[0]
    half = block // 2
    tables = pooled_ref.shape[1] // LANES
    per_owner = sum(len(chunk) for chunk in chunks)
    rows = lower.shape[1]

    @pl.when(pl.program_id(0) == 0)
    def _():
        lower[...] = jnp.zeros_like(lower)
        feats[...] = jnp.zeros_like(feats)

    wide_pairs[:, 0 : pair_ref.shape[1]] = pair_ref[...].astype(F32)
    lane = lax.broadcasted_iota(jnp.int32, (half, LANES), 1)
    for i in range(1, tables + 1):
        start = i * (i - 1) // 2
        base = start // LANES * LANES
        shift = start - base
        to_low = (LANES - shift) % LANES
        to_high = (HALF - shift) % LANES

        def rolled(first, amount, at):
            piece = wide_pairs[first : first + half, at : at + LANES]
            return pltpu.roll(piece, amount, 1) if amount else piece

        low = rolled(0, to_low, base)
        high = rolled(half, to_high, base)
        if shift + i > LANES:
            low = jnp.where(lane < LANES - shift, low, rolled(0, to_low, base + LANES))
            high = jnp.where(
                lane < HALF + LANES - shift, high, rolled(half, to_high, base + LANES)
            )
        if i < HALF:
            low = jnp.where(lane < i, low, 0.0)
            high = jnp.where(lane < HALF + i, high, 0.0)
        lower[:, i, :] = jnp.where(lane < HALF, low, high)

    feats[:, 0, :] = dense_ref[...].astype(F32)
    for t in range(tables):
        feats[:, t + 1, :] = pooled_ref[:, t * LANES : (t + 1) * LANES].astype(F32)

    row_lane = lax.broadcasted_iota(jnp.int32, (rows, LANES), 1)
    below = jnp.zeros((rows - HALF, LANES), F32)

    def two_samples(b, carry):
        both = lower[b]
        turned = jnp.concatenate([both.T, jnp.zeros((LANES, LANES - rows), F32)], 1)
        first = jnp.where(row_lane < HALF, both, 0.0)
        second = jnp.where(row_lane < HALF, pltpu.roll(both, HALF, 1), 0.0)
        first = first + jnp.concatenate([turned[:HALF], below], 0)
        second = second + jnp.concatenate([turned[HALF:], below], 0)
        for pairs, sample in ((first, b), (second, b + half)):
            out = jnp.dot(
                pairs[:, :rows].astype(BF16),
                feats[sample].astype(BF16),
                preferred_element_type=F32,
            )
            grads[:, pl.ds(sample, 1), :] = out.reshape(rows, 1, LANES)
        return carry

    lax.fori_loop(0, half, two_samples, 0, unroll=8)

    d_dense_ref[...] = (grads[0, 0:block] + cot_ref[...].astype(F32)).astype(BF16)
    for send_ref, chunk in zip(send_refs, chunks):
        for place, t in enumerate(chunk):
            for owner in range(tables // per_owner):
                send_ref[owner, :, place * LANES : (place + 1) * LANES] = grads[
                    owner * per_owner + t + 1, 0:block
                ].astype(BF16)


def interact(dense_out, pooled, dense_cot, pair_cot, owners, chunks):
    samples = dense_out.shape[0]
    tables = pooled.shape[1] // LANES
    pairs = pair_cot.shape[1]
    block = 64
    rows = (tables + 1 + 7) // 8 * 8
    padded = (pairs // LANES + 1) * LANES
    return pl.pallas_call(
        functools.partial(interact_kernel, chunks),
        grid=(samples // block,),
        in_specs=[
            pl.BlockSpec((block, LANES), lambda s: (s, 0)),
            pl.BlockSpec((block, tables * LANES), lambda s: (s, 0)),
            pl.BlockSpec((block, LANES), lambda s: (s, 0)),
            pl.BlockSpec((block, pairs), lambda s: (s, 0)),
        ],
        out_specs=[pl.BlockSpec((block, LANES), lambda s: (s, 0))]
        + [
            pl.BlockSpec((owners, block, len(chunk) * LANES), lambda s: (0, s, 0))
            for chunk in chunks
        ],
        out_shape=[jax.ShapeDtypeStruct((samples, LANES), BF16)]
        + [
            jax.ShapeDtypeStruct((owners, samples, len(chunk) * LANES), BF16) for chunk in chunks
        ],
        scratch_shapes=[
            pltpu.VMEM((block, padded), F32),
            pltpu.VMEM((block // 2, rows, LANES), F32),
            pltpu.VMEM((block, rows, LANES), F32),
            pltpu.VMEM((rows, block + 8, LANES), F32),
        ],
        compiler_params=params(),
        cost_estimate=cost(25),
    )(dense_out, pooled, dense_cot, pair_cot)


def count_kernel(ids_ref, out_ref):
    sources, _, slots, samples = ids_ref.shape
    words = out_ref.shape[1]
    step = 64

    @pl.loop(0, sources)
    def _(source):
        ids = ids_ref[source, 0]
        word = ids & (words - 1)
        one = jnp.left_shift(1, FIELD * (ids // words))
        columns = pl.ds(pl.multiple_of(source * samples, samples), samples)

        @pl.loop(0, words // step)
        def _(part):
            start = pl.multiple_of(part * step, step)
            place = lax.broadcasted_iota(jnp.int32, (step, samples), 0) + start
            total = jnp.zeros((step, samples), jnp.int32)
            for slot in range(slots):
                total = total + jnp.where(
                    word[slot : slot + 1] == place, one[slot : slot + 1], 0
                )
            out_ref[0, pl.ds(start, step), columns] = total


def bag_counts(ids, words):
    sources, tables, slots, samples = ids.shape
    return pl.pallas_call(
        count_kernel,
        grid=(tables,),
        in_specs=[pl.BlockSpec((sources, 1, slots, samples), lambda t: (0, t, 0, 0))],
        out_specs=pl.BlockSpec((1, words, sources * samples), lambda t: (t, 0, 0)),
        out_shape=jax.ShapeDtypeStruct((tables, words, sources * samples), jnp.int32),
        compiler_params=params(),
        cost_estimate=cost(35),
    )(ids)


def sum_kernel(hst_ref, counts_ref, grads_ref, out_ref, total):
    samples = counts_ref.shape[2]
    cores, _, chips = out_ref.shape[:3]
    step = 1024
    here, core = hst_ref[0] // cores, lax.rem(hst_ref[0], cores)
    for at in range(0, samples, step):
        grads = grads_ref[at : at + step, :]
        counts = counts_ref[0, :, at : at + step]
        for c in range(cores):
            for d in range(chips):
                field = cores * lax.rem(here + d, chips) + lax.rem(core + c, cores)
                picked = (counts >> (FIELD * field)) & ((1 << FIELD) - 1)
                part = jnp.dot(
                    picked.astype(F32).astype(BF16), grads, preferred_element_type=F32
                )
                if at == 0:
                    total[c, d] = part
                else:
                    total[c, d] += part
    for c in range(cores):
        for d in range(chips):
            out_ref[c, 0, d] = total[c, d].astype(BF16)


def row_sums(hst, counts, grads, chunk, columns, cores):
    _, words, samples = counts.shape
    step = 256
    chips = 32 // FIELD // cores
    first, column = chunk[0], columns[0]
    return pl.pallas_call(
        sum_kernel,
        grid_spec=pltpu.PrefetchScalarGridSpec(
            num_scalar_prefetch=1,
            grid=(len(chunk), words // step),
            in_specs=[
                pl.BlockSpec((1, step, samples), lambda t, w, hst: (first + t, w, 0)),
                pl.BlockSpec((samples, LANES), lambda t, w, hst: (0, column + t)),
            ],
            out_specs=pl.BlockSpec(
                (cores, 1, chips, step, LANES), lambda t, w, hst: (0, t, 0, w, 0)
            ),
            scratch_shapes=[pltpu.VMEM((cores, chips, step, LANES), F32)],
        ),
        out_shape=jax.ShapeDtypeStruct((cores, len(chunk), chips, words, LANES), BF16),
        compiler_params=params(),
        cost_estimate=cost(11 * len(chunk)),
    )(hst, counts, grads)


def add_kernel(mine_ref, other_ref, *out_refs):
    for d, out_ref in enumerate(out_refs):
        out_ref[0] = (mine_ref[0, 0, d].astype(F32) + other_ref[0, d].astype(F32)).astype(BF16)


def exchange(sums, cores):
    _, tables, chips, words, lanes = sums.shape
    devices = cores * chips
    got = lax.ppermute(sums[1], "hst", [(i, i ^ 1) for i in range(devices)])
    pieces = pl.pallas_call(
        add_kernel,
        grid=(tables,),
        in_specs=[
            pl.BlockSpec((1, 1, chips, words, lanes), lambda t: (0, t, 0, 0, 0)),
            pl.BlockSpec((1, chips, words, lanes), lambda t: (t, 0, 0, 0)),
        ],
        out_specs=[pl.BlockSpec((1, words, lanes), lambda t: (t, 0, 0))] * chips,
        out_shape=[jax.ShapeDtypeStruct((tables, words, lanes), BF16)] * chips,
        compiler_params=params(),
        cost_estimate=cost(1.5),
    )(sums, got)
    out = [pieces[0]]
    for d in range(1, chips):
        ring = [(i, (i + cores * d) % devices) for i in range(devices)]
        out.append(lax.ppermute(pieces[d], "hst", ring))
    return out


def update_kernel(weights_ref, accum_ref, *rest):
    *grad_refs, new_weights_ref, new_accum_ref = rest
    words, lanes = weights_ref.shape[1:]
    grads = grad_refs[0][0].astype(F32)
    for grad_ref in grad_refs[1:]:
        grads = grads + grad_ref[0].astype(F32)
    mean = jnp.sum(grads * grads, 1, keepdims=True) * (1.0 / lanes)
    accum = jnp.broadcast_to(accum_ref[0], (lanes, words)).T + mean
    new_weights_ref[0] = weights_ref[0] - LEARN_RATE * grads / (jnp.sqrt(accum) + EPSILON)
    new_accum_ref[0] = accum.T[0:1]


def update(weights, accum, grads, chunk):
    tables, words, lanes = weights.shape
    first = chunk[0]
    here = pl.BlockSpec((1, words, lanes), lambda t: (first + t, 0, 0))
    part = pl.BlockSpec((1, words, lanes), lambda t: (t, 0, 0))
    return pl.pallas_call(
        update_kernel,
        grid=(len(chunk),),
        in_specs=[here, pl.BlockSpec((1, 1, words), lambda t: (first + t, 0, 0))]
        + [part] * len(grads),
        out_specs=[part, pl.BlockSpec((1, 1, words), lambda t: (t, 0, 0))],
        out_shape=[
            jax.ShapeDtypeStruct((len(chunk), words, lanes), F32),
            jax.ShapeDtypeStruct((len(chunk), 1, words), F32),
        ],
        compiler_params=params(),
        cost_estimate=cost(2),
    )(weights, accum.reshape(tables, 1, words), *grads)


def local(dense_out, pooled, dense_cot, pair_cot, bag_ids, weights, accum):
    samples = dense_out.shape[0]
    slots = bag_ids.shape[1]
    per_owner, words, _ = weights.shape
    owners = lax.axis_size("wide")
    cores = 2
    hst = lax.axis_index("hst").reshape(1)
    ids = bag_ids.reshape(owners, per_owner, slots, samples)
    ids = lax.all_to_all(ids, "wide", split_axis=0, concat_axis=0, tiled=True)
    d_dense, *sends = interact(dense_out, pooled, dense_cot, pair_cot, owners, SEND_CHUNKS)
    counts = bag_counts(ids, words)
    received = [
        lax.all_to_all(send, "wide", split_axis=0, concat_axis=0, tiled=True).reshape(
            owners * samples, -1
        )
        for send in sends
    ]
    weights_out, accum_out = [], []
    for chunk in SUM_CHUNKS:
        for number, carried in enumerate(SEND_CHUNKS):
            if chunk[0] in carried:
                columns = [carried.index(t) for t in chunk]
                sums = row_sums(hst, counts, received[number], chunk, columns, cores)
        w, a = update(weights, accum, exchange(sums, cores), chunk)
        weights_out.append(w)
        accum_out.append(a)
    new_weights = jnp.concatenate(weights_out, 0)
    new_accum = jnp.concatenate(accum_out, 0).reshape(per_owner, words)
    return d_dense, new_weights, new_accum


def solution(mesh):
    in_specs = (
        P(("hst", "wide"), None),
        P(("hst", "wide"), None),
        P(("hst", "wide"), None),
        P(("hst", "wide"), None),
        P(None, None, ("hst", "wide")),
        P("wide", "hst", None),
        P("wide", "hst"),
    )
    out_specs = (P(("hst", "wide"), None), P("wide", "hst", None), P("wide", "hst"))
    return jax.shard_map(local, mesh=mesh, in_specs=in_specs, out_specs=out_specs, check_vma=False)
```

time: 499 us -> 181 us (0.36); the launches traced: 490 us -> 180 us
  matrix products: 253 us -> 0 us
  Pallas kernels: 0 us -> 103 us
  local copies, waits for them, and re-layouts: 83 us -> 4.4 us
  waiting for transfers between devices: 94 us -> 46.3 us
  other arithmetic: 27.2 us -> 1.08 us
  between operations: 14.8 us -> 0.79 us
  starting transfers between devices: 15.8 us -> 25.3 us
    dot_general x34 -> x0, matrix products: 253 us -> none  [the longest x32 238 us: one_block(): return jnp.dot(counts, grads_table, preferred_element_type=jnp.float32)]
    pallas_call x0 -> x8, Pallas kernels: none -> 103 us  [the longest x2 45.7 us: row_sums(): pl.pallas_call(sum_kernel, grid_spec=pltpu.PrefetchScalarGridSpec(num_sca...]
    reduce_scatter x1 -> x0, waiting for transfers between devices: 34.9 us -> none  [local(): lax.psum_scatter(summed.transpose(1, 0, 2).reshape(row_block * lax.axis_s...]
    all_to_all x2, waiting for transfers between devices: 59.1 us -> 26.8 us  [the longest x1 26.8 us: local(): lax.all_to_all(send, 'wide', split_axis=0, concat_axis=0, tiled=True)]
    reshape x5 -> x1, local copies, waits for them, and re-layouts: 22.9 us -> 0.01 us  [update(): accum.reshape(tables, 1, words)]
    add x34 -> x0, other arithmetic: 20.4 us -> none  [the longest x32 19.8 us: one_block(): positions = start + jnp.arange(block_rows, dtype=jnp.int32)]
    ppermute x0 -> x8, waiting for transfers between devices: none -> 19.5 us  [the longest x6 17.5 us: exchange(): out.append(lax.ppermute(pieces[d], 'hst', ring))]
    dynamic_slice x32 -> x0, local copies, waits for them, and re-layouts: 19 us -> none  [window_sums(): summed = lax.map(one_block, starts)]
  transfers between devices with their start and end apart: 3 -> 10, of which waited for: 2 -> 6; matrix products, arithmetic and copies ran while one was open for 9% -> 1% of each run, Pallas kernels for 0% -> 31%
where the time goes in v1:
time: 181 us; the launch traced here: 180 us
  Pallas kernels  103 us (57%)
  waiting for transfers between devices  46.3 us (26%)
  starting transfers between devices  25.3 us (14%)
  local copies, waits for them, and re-layouts  4.4 us (2%)
    pallas_call x2, Pallas kernels, row_sums(): pl.pallas_call(sum_kernel, grid_spec=pltpu.PrefetchScalarGridSpec(num_sca...  45.7 us
    pallas_call x1, Pallas kernels, bag_counts(): pl.pallas_call(count_kernel, grid=(tables,), in_specs=[pl.BlockSpec((sour...  34.7 us
    all_to_all x1, waiting for transfers between devices, local(): lax.all_to_all(send, 'wide', split_axis=0, concat_axis=0, tiled=True)  26.8 us
    pallas_call x1, Pallas kernels, interact(): pl.pallas_call(functools.partial(interact_kernel, chunks), grid=(samples...  20.3 us
    ppermute x6, waiting for transfers between devices, exchange(): out.append(lax.ppermute(pieces[d], 'hst', ring))  17.5 us
    ppermute x6, starting transfers between devices, exchange(): out.append(lax.ppermute(pieces[d], 'hst', ring))  9.07 us
    all_to_all x1, starting transfers between devices, local(): ids = lax.all_to_all(ids, 'wide', split_axis=0, concat_axis=0, tiled=True)  8.28 us
    all_to_all x1, starting transfers between devices, local(): lax.all_to_all(send, 'wide', split_axis=0, concat_axis=0, tiled=True)  7.27 us
  transfers between devices with their start and end apart: 10, of which 6 were waited for; matrix products, arithmetic and copies ran while one was open for 1% of the time, Pallas kernels for 31%

profile of v1, /device:TPU:0, one launch (start us, length us, event | category | flops | bytes accessed | tf_op | source)
XLA Modules:
  0.0 180.3 jit_solution(11119064282506464929)
XLA Ops:
  0.6 0.0 copy-start.3
  0.6 0.0 copy-start.2
  0.6 8.3 %all-to-all-start = ((s32[16,4,8,256]{3,2,1,0:T(8,128)}), s32[16,4,8,256]{3,2,1,0:T(8,128)S(1)}, u32[]{:S(2)}, u32[]{:S(2)}) async-start(s32[16,4,8,256]{3,2,1,0:T(8,128)} %bitcast.10), calls=%async_computation | async-start | bytes 1048576 | tf_op jit(solution)/shard_map/all_to_all | solution.py:295
  8.9 1.7 copy.10.pair_ref
  10.6 0.0 copy-done.3
  10.6 0.0 copy-done.2
  10.6 20.3 %shard_map.94 = (bf16[256,128]{1,0:T(8,128)(2,1)}, bf16[16,256,512]{2,1,0:T(8,128)(2,1)S(1)}) custom-call(bf16[256,128]{1,0:T(8,128)(2,1)S(1)} %copy-done.2, bf16[256,8192]{1,0:T(8,128)(2,1)} %pooled_ref.1, bf16[256,128]{1,0:T(8,128)(2,1)S(1)} %copy-done.3, bf16[256,2080]{1,0:T(8,128)(2,1)S(1)} %copy.10.pair_ref), custom_call_target="tpu_custom_call" | custom-call | flops 28750000128 | bytes 1048576 | tf_op jit(solution)/shard_map/pallas_call | solution.py:112
  30.9 0.0 copy-start
  30.9 2.0 %copy-done = bf16[16,256,512]{2,1,0:T(8,128)(2,1)} copy-done((bf16[16,256,512]{2,1,0:T(8,128)(2,1)}, bf16[16,256,512]{2,1,0:T(8,128)(2,1)S(1)}, u32[]{:S(2)}) %copy-start) | copy-done | bytes 4194328
  32.9 0.0 all-to-all-done.ids_ref
  32.9 7.3 %all-to-all-start.1 = ((bf16[16,256,512]{2,1,0:T(8,128)(2,1)}), bf16[16,256,512]{2,1,0:T(8,128)(2,1)}, u32[]{:S(2)}, u32[]{:S(2)}) async-start(bf16[16,256,512]{2,1,0:T(8,128)(2,1)} %copy-done), calls=%async_computation.1 | async-start | bytes 8388608 | tf_op jit(solution)/shard_map/all_to_all | solution.py:299
  40.2 34.7 %shard_map.95.counts_ref = s32[4,512,4096]{2,1,0:T(8,128)} custom-call(s32[16,4,8,256]{3,2,1,0:T(8,128)S(1)} %all-to-all-done.ids_ref), custom_call_target="tpu_custom_call" | custom-call | flops 40249999360 | bytes 1048576 | tf_op jit(solution)/shard_map/pallas_call | solution.py:167
  74.9 26.8 %all-to-all-done.1 = bf16[16,256,512]{2,1,0:T(8,128)(2,1)} async-done(((bf16[16,256,512]{2,1,0:T(8,128)(2,1)}), bf16[16,256,512]{2,1,0:T(8,128)(2,1)}, u32[]{:S(2)}, u32[]{:S(2)}) %all-to-all-start.1) | async-done | bytes 4194336 | tf_op jit(solution)/shard_map/all_to_all | solution.py:299
  101.7 22.9 %shard_map.99.mine_ref = bf16[2,2,4,512,128]{4,3,2,1,0:T(8,128)(2,1)S(1)} custom-call(s32[1]{0:T(128)} %bitcast.hst_ref, s32[4,512,4096]{2,1,0:T(8,128)} %shard_map.95.counts_ref, bf16[4096,512]{1,0:T(8,128)(2,1)} %bitcast.2.grads_ref), custom_call_target="tpu_custom_call" | custom-call | flops 25300000768 | bytes 1048576 | tf_op jit(solution)/shard_map/pallas_call | solution.py:207
  124.5 22.9 %shard_map.96.mine_ref = bf16[2,2,4,512,128]{4,3,2,1,0:T(8,128)(2,1)S(1)} custom-call(s32[1]{0:T(128)} %bitcast.hst_ref, s32[4,512,4096]{2,1,0:T(8,128)} %shard_map.95.counts_ref, bf16[4096,512]{1,0:T(8,128)(2,1)} %bitcast.2.grads_ref), custom_call_target="tpu_custom_call" | custom-call | flops 25300000768 | bytes 1048576 | tf_op jit(solution)/shard_map/pallas_call | solution.py:207
  147.4 0.1 slice_bitcast_fusion
  147.5 0.1 collective-permute-start.4
  147.6 0.1 slice_bitcast_fusion.1
  147.6 0.6 collective-permute-start
  148.2 2.0 %collective-permute-done.4.other_ref = bf16[2,4,512,128]{3,2,1,0:T(8,128)(2,1)S(1)} collective-permute-done((bf16[2,4,512,128]{3,2,1,0:T(8,128)(2,1)S(1)}, bf16[2,4,512,128]{3,2,1,0:T(8,128)(2,1)S(1)}, u32[]{:S(2)}, u32[]{:S(2)}) %collective-permute-start.4) | collective-permute-done | bytes 1048608 | tf_op jit(solution)/shard_map/ppermute | solution.py:235
  150.2 0.3 shard_map.100
  150.5 1.6 collective-permute-start.5
  152.1 2.7 %collective-permute-start.6 = (bf16[2,512,128]{2,1,0:T(8,128)(2,1)S(1)}, bf16[2,512,128]{2,1,0:T(8,128)(2,1)S(1)}, u32[]{:S(2)}, u32[]{:S(2)}) collective-permute-start(bf16[2,512,128]{2,1,0:T(8,128)(2,1)S(1)} %get-tuple-element.26), channel_id=1, source_target_pairs={{0,64},{16,80},{32,96},{48,112},{64,0},{80,16},{96,32},{112,48},{1... | collective-permute-start | bytes 786440 | tf_op jit(solution)/shard_map/ppermute | solution.py:251
  154.8 0.0 copy-start.4
  154.8 0.0 copy-start.1
  154.8 1.4 collective-permute-start.7
  156.2 0.0 collective-permute-done.other_ref
  156.2 0.3 shard_map.97
  156.5 0.7 collective-permute-start.1
  157.2 0.9 collective-permute-start.2
  158.1 2.6 %collective-permute-done.5.rest_1_ = bf16[2,512,128]{2,1,0:T(8,128)(2,1)S(1)} collective-permute-done((bf16[2,512,128]{2,1,0:T(8,128)(2,1)S(1)}, bf16[2,512,128]{2,1,0:T(8,128)(2,1)S(1)}, u32[]{:S(2)}, u32[]{:S(2)}) %collective-permute-start.5) | collective-permute-done | bytes 262176 | tf_op jit(solution)/shard_map/ppermute | solution.py:251
  160.7 1.8 collective-permute-start.3
  162.5 0.0 copy-done.4
  162.5 5.1 %collective-permute-done.6.rest_2_ = bf16[2,512,128]{2,1,0:T(8,128)(2,1)S(1)} collective-permute-done((bf16[2,512,128]{2,1,0:T(8,128)(2,1)S(1)}, bf16[2,512,128]{2,1,0:T(8,128)(2,1)S(1)}, u32[]{:S(2)}, u32[]{:S(2)}) %collective-permute-start.6) | collective-permute-done | bytes 262176 | tf_op jit(solution)/shard_map/ppermute | solution.py:251
  167.6 0.0 collective-permute-done.7.rest_3_
  167.6 0.0 copy-done.1
  167.6 0.6 shard_map.101
  168.2 3.1 %collective-permute-done.1.rest_1_ = bf16[2,512,128]{2,1,0:T(8,128)(2,1)S(1)} collective-permute-done((bf16[2,512,128]{2,1,0:T(8,128)(2,1)S(1)}, bf16[2,512,128]{2,1,0:T(8,128)(2,1)S(1)}, u32[]{:S(2)}, u32[]{:S(2)}) %collective-permute-start.1) | collective-permute-done | bytes 262176 | tf_op jit(solution)/shard_map/ppermute | solution.py:251
  171.3 6.6 %collective-permute-done.2.rest_2_ = bf16[2,512,128]{2,1,0:T(8,128)(2,1)S(1)} collective-permute-done((bf16[2,512,128]{2,1,0:T(8,128)(2,1)S(1)}, bf16[2,512,128]{2,1,0:T(8,128)(2,1)S(1)}, u32[]{:S(2)}, u32[]{:S(2)}) %collective-permute-start.2) | collective-permute-done | bytes 262176 | tf_op jit(solution)/shard_map/ppermute | solution.py:251
  178.0 0.0 collective-permute-done.3.rest_3_
  178.0 0.6 shard_map.98
  178.7 0.6 copy.13
  179.3 1.1 pad_maximum_fusion
  (2 shorter events, 0.0 us)
Async XLA Ops:
  0.6 10.0 %copy-start.3 = (bf16[256,128]{1,0:T(8,128)(2,1)S(1)}, bf16[256,128]{1,0:T(8,128)(2,1)}, u32[]{:S(2)}) copy-start(bf16[256,128]{1,0:T(8,128)(2,1)} %cot_ref.1) | copy-start | bytes 196612
  0.6 10.0 %copy-start.2 = (bf16[256,128]{1,0:T(8,128)(2,1)S(1)}, bf16[256,128]{1,0:T(8,128)(2,1)}, u32[]{:S(2)}) copy-start(bf16[256,128]{1,0:T(8,128)(2,1)} %dense_ref.1) | copy-start | bytes 196612
  0.6 32.2 %all-to-all-start = ((s32[16,4,8,256]{3,2,1,0:T(8,128)}), s32[16,4,8,256]{3,2,1,0:T(8,128)S(1)}, u32[]{:S(2)}, u32[]{:S(2)}) async-start(s32[16,4,8,256]{3,2,1,0:T(8,128)} %bitcast.10), calls=%async_computation | async-start | bytes 1048576 | tf_op jit(solution)/shard_map/all_to_all | solution.py:295
  30.9 2.0 %copy-start = (bf16[16,256,512]{2,1,0:T(8,128)(2,1)}, bf16[16,256,512]{2,1,0:T(8,128)(2,1)S(1)}, u32[]{:S(2)}) copy-start(bf16[16,256,512]{2,1,0:T(8,128)(2,1)S(1)} %get-tuple-element.18) | copy-start | bytes 12582916
  32.9 68.8 %all-to-all-start.1 = ((bf16[16,256,512]{2,1,0:T(8,128)(2,1)}), bf16[16,256,512]{2,1,0:T(8,128)(2,1)}, u32[]{:S(2)}, u32[]{:S(2)}) async-start(bf16[16,256,512]{2,1,0:T(8,128)(2,1)} %copy-done), calls=%async_computation.1 | async-start | bytes 8388608 | tf_op jit(solution)/shard_map/all_to_all | solution.py:299
  147.5 2.7 %collective-permute-start.4 = (bf16[2,4,512,128]{3,2,1,0:T(8,128)(2,1)S(1)}, bf16[2,4,512,128]{3,2,1,0:T(8,128)(2,1)S(1)}, u32[]{:S(2)}, u32[]{:S(2)}) collective-permute-start(bf16[2,4,512,128]{3,2,1,0:T(8,128)(2,1)S(1)} %slice_bitcast_fusion), channel_id=1, source_target_pairs={{0,16},{16,0},{32,48},{48,32},{64,80},{80,64},{96,112},{112,96},{1... | collective-permute-start | bytes 3145736 | tf_op jit(solution)/shard_map/ppermute | solution.py:235
  147.6 8.6 %collective-permute-start = (bf16[2,4,512,128]{3,2,1,0:T(8,128)(2,1)S(1)}, bf16[2,4,512,128]{3,2,1,0:T(8,128)(2,1)S(1)}, u32[]{:S(2)}, u32[]{:S(2)}) collective-permute-start(bf16[2,4,512,128]{3,2,1,0:T(8,128)(2,1)S(1)} %slice_bitcast_fusion.1), channel_id=1, source_target_pairs={{0,16},{16,0},{32,48},{48,32},{64,80},{80,64},{96,112},{112,96},{1... | collective-permute-start | bytes 3145736 | tf_op jit(solution)/shard_map/ppermute | solution.py:235
  150.5 10.2 %collective-permute-start.5 = (bf16[2,512,128]{2,1,0:T(8,128)(2,1)S(1)}, bf16[2,512,128]{2,1,0:T(8,128)(2,1)S(1)}, u32[]{:S(2)}, u32[]{:S(2)}) collective-permute-start(bf16[2,512,128]{2,1,0:T(8,128)(2,1)S(1)} %get-tuple-element.25), channel_id=1, source_target_pairs={{0,32},{16,48},{32,64},{48,80},{64,96},{80,112},{96,0},{112,16},{1... | collective-permute-start | bytes 786440 | tf_op jit(solution)/shard_map/ppermute | solution.py:251
  152.1 15.5 %collective-permute-start.6 = (bf16[2,512,128]{2,1,0:T(8,128)(2,1)S(1)}, bf16[2,512,128]{2,1,0:T(8,128)(2,1)S(1)}, u32[]{:S(2)}, u32[]{:S(2)}) collective-permute-start(bf16[2,512,128]{2,1,0:T(8,128)(2,1)S(1)} %get-tuple-element.26), channel_id=1, source_target_pairs={{0,64},{16,80},{32,96},{48,112},{64,0},{80,16},{96,32},{112,48},{1... | collective-permute-start | bytes 786440 | tf_op jit(solution)/shard_map/ppermute | solution.py:251
  154.8 7.7 %copy-start.4 = (f32[4,512]{1,0:T(4,128)S(1)}, f32[4,512]{1,0:T(4,128)}, u32[]{:S(2)}) copy-start(f32[4,512]{1,0:T(4,128)} %param.13) | copy-start | bytes 24580
  154.8 12.8 %copy-start.1 = (f32[4,512,128]{2,1,0:T(8,128)S(1)}, f32[4,512,128]{2,1,0:T(8,128)}, u32[]{:S(2)}) copy-start(f32[4,512,128]{2,1,0:T(8,128)} %weights_ref.3) | copy-start | bytes 3145732
  154.8 12.8 %collective-permute-start.7 = (bf16[2,512,128]{2,1,0:T(8,128)(2,1)S(1)}, bf16[2,512,128]{2,1,0:T(8,128)(2,1)S(1)}, u32[]{:S(2)}, u32[]{:S(2)}) collective-permute-start(bf16[2,512,128]{2,1,0:T(8,128)(2,1)S(1)} %get-tuple-element.27), channel_id=1, source_target_pairs={{0,96},{16,112},{32,0},{48,16},{64,32},{80,48},{96,64},{112,80},{1... | collective-permute-start | bytes 786440 | tf_op jit(solution)/shard_map/ppermute | solution.py:251
  156.5 14.8 %collective-permute-start.1 = (bf16[2,512,128]{2,1,0:T(8,128)(2,1)S(1)}, bf16[2,512,128]{2,1,0:T(8,128)(2,1)S(1)}, u32[]{:S(2)}, u32[]{:S(2)}) collective-permute-start(bf16[2,512,128]{2,1,0:T(8,128)(2,1)S(1)} %get-tuple-element.20), channel_id=1, source_target_pairs={{0,32},{16,48},{32,64},{48,80},{64,96},{80,112},{96,0},{112,16},{1... | collective-permute-start | bytes 786440 | tf_op jit(solution)/shard_map/ppermute | solution.py:251
  157.2 20.8 %collective-permute-start.2 = (bf16[2,512,128]{2,1,0:T(8,128)(2,1)S(1)}, bf16[2,512,128]{2,1,0:T(8,128)(2,1)S(1)}, u32[]{:S(2)}, u32[]{:S(2)}) collective-permute-start(bf16[2,512,128]{2,1,0:T(8,128)(2,1)S(1)} %get-tuple-element.21), channel_id=1, source_target_pairs={{0,64},{16,80},{32,96},{48,112},{64,0},{80,16},{96,32},{112,48},{1... | collective-permute-start | bytes 786440 | tf_op jit(solution)/shard_map/ppermute | solution.py:251
  160.7 17.3 %collective-permute-start.3 = (bf16[2,512,128]{2,1,0:T(8,128)(2,1)S(1)}, bf16[2,512,128]{2,1,0:T(8,128)(2,1)S(1)}, u32[]{:S(2)}, u32[]{:S(2)}) collective-permute-start(bf16[2,512,128]{2,1,0:T(8,128)(2,1)S(1)} %get-tuple-element.22), channel_id=1, source_target_pairs={{0,96},{16,112},{32,0},{48,16},{64,32},{80,48},{96,64},{112,80},{1... | collective-permute-start | bytes 786440 | tf_op jit(solution)/shard_map/ppermute | solution.py:251

commit v2 on v0

v2 whole, which is shorter than its diff:
```python
import functools

import jax
import jax.numpy as jnp
from jax import lax
from jax.experimental import pallas as pl
from jax.experimental.pallas import tpu as pltpu
from jax.sharding import Mesh
from jax.sharding import PartitionSpec as P

LEARN_RATE = 0.5
EPSILON = 1e-08
LANES = 128
HALF = 64
FIELD = 4
BLOCK = 32
CORES = 2
CODE = 7
VMEM = 62 << 20
SMALL = 12 << 20
EARLY = 64
LATE_GROUP = 8
BF16 = jnp.bfloat16
F32 = jnp.float32


def cost(micros):
    return pl.CostEstimate(flops=int(micros * 2e8), bytes_accessed=1 << 16, transcendentals=0)


def params(size=VMEM):
    return pltpu.CompilerParams(vmem_limit_bytes=size)


def encode(ids):
    high = lax.shift_right_logical(ids, CODE)
    value = ((1 << CODE) + (ids & ((1 << CODE) - 1))).astype(F32)
    for bit in range(5):
        value = jnp.where((high >> bit) & 1 == 1, value * 2.0 ** (1 << bit), value)
    return value.astype(BF16)


def decode(codes):
    value = codes.astype(F32)
    high = jnp.zeros(value.shape, jnp.int32)
    for bit in range(4, -1, -1):
        large = value >= 2.0 ** (CODE + (1 << bit))
        value = jnp.where(large, value * 2.0 ** -(1 << bit), value)
        high = jnp.where(large, high + (1 << bit), high)
    return (high << CODE) + value.astype(jnp.int32) - (1 << CODE)


def interact_kernel(steps, with_ids, dense_ref, pooled_ref, cot_ref, pair_ref, *rest):
    if with_ids:
        ids_ref, *rest = rest
    d_dense_ref, send_ref, *scratch = rest
    tables = pooled_ref.shape[1] // LANES
    held = tables // send_ref.shape[0]

    @pl.when(pl.program_id(0) == 0)
    def _():
        for ref in scratch[1:3]:
            ref[...] = jnp.zeros_like(ref)

    if not with_ids:
        interact_block(dense_ref, pooled_ref, cot_ref, pair_ref, d_dense_ref, send_ref, *scratch)
        return

    @pl.when(pl.program_id(0) < steps)
    def _():
        interact_block(dense_ref, pooled_ref, cot_ref, pair_ref, d_dense_ref, send_ref, *scratch)

    @pl.when(pl.program_id(0) == steps)
    def _():
        slots = ids_ref.shape[1]
        for owner in range(tables // held):
            ids = ids_ref[owner * held : (owner + 1) * held]
            send_ref[owner, 0 : held * slots, :] = encode(ids.reshape(held * slots, -1))


def interact_block(
    dense_ref, pooled_ref, cot_ref, pair_ref, d_dense_ref, send_ref, wide_pairs, lower, feats, grads
):
    block = dense_ref.shape[0]
    half = block // 2
    tables = pooled_ref.shape[1] // LANES
    rows = lower.shape[1]

    wide_pairs[:, 0 : pair_ref.shape[1]] = pair_ref[...].astype(F32)
    lane = lax.broadcasted_iota(jnp.int32, (half, LANES), 1)
    for i in range(1, tables + 1):
        start = i * (i - 1) // 2
        base = start // LANES * LANES
        shift = start - base
        to_low = (LANES - shift) % LANES
        to_high = (HALF - shift) % LANES

        def rolled(first, amount, at):
            piece = wide_pairs[first : first + half, at : at + LANES]
            return pltpu.roll(piece, amount, 1) if amount else piece

        low = rolled(0, to_low, base)
        high = rolled(half, to_high, base)
        if shift + i > LANES:
            low = jnp.where(lane < LANES - shift, low, rolled(0, to_low, base + LANES))
            high = jnp.where(
                lane < HALF + LANES - shift, high, rolled(half, to_high, base + LANES)
            )
        if i < HALF:
            low = jnp.where(lane < i, low, 0.0)
            high = jnp.where(lane < HALF + i, high, 0.0)
        lower[:, i, :] = jnp.where(lane < HALF, low, high)

    feats[:, 0, :] = dense_ref[...].astype(F32)
    for t in range(tables):
        feats[:, t + 1, :] = pooled_ref[:, t * LANES : (t + 1) * LANES].astype(F32)

    row_lane = lax.broadcasted_iota(jnp.int32, (rows, LANES), 1)
    below = jnp.zeros((rows - HALF, LANES), F32)

    def two_samples(b, carry):
        both = lower[b]
        turned = jnp.concatenate([both.T, jnp.zeros((LANES, LANES - rows), F32)], 1)
        first = jnp.where(row_lane < HALF, both, 0.0)
        second = jnp.where(row_lane < HALF, pltpu.roll(both, HALF, 1), 0.0)
        first = first + jnp.concatenate([turned[:HALF], below], 0)
        second = second + jnp.concatenate([turned[HALF:], below], 0)
        for pairs, sample in ((first, b), (second, b + half)):
            out = jnp.dot(
                pairs[:, :rows].astype(BF16),
                feats[sample].astype(BF16),
                preferred_element_type=F32,
            )
            grads[:, pl.ds(sample, 1), :] = out.reshape(rows, 1, LANES)
        return carry

    lax.fori_loop(0, half, two_samples, 0, unroll=8)

    d_dense_ref[...] = (grads[0, 0:block] + cot_ref[...].astype(F32)).astype(BF16)
    owners = send_ref.shape[0]
    held = tables // owners
    for t in range(tables):
        place = t % held * LANES
        send_ref[t // held, :, place : place + LANES] = grads[t + 1, 0:block].astype(BF16)


def interact(dense_out, pooled, dense_cot, pair_cot, ids, owners, first, samples):
    tables = pooled.shape[1] // LANES
    pairs = pair_cot.shape[1]
    held = tables // owners
    rows = (tables + 1 + 7) // 8 * 8
    padded = (pairs // LANES + 1) * LANES
    skip, steps = first // BLOCK, samples // BLOCK
    with_ids = ids is not None
    slots = ids.shape[1] if with_ids else 0

    def at(s):
        return (skip + jnp.minimum(s, steps - 1), 0)

    specs = [
        pl.BlockSpec((BLOCK, LANES), at),
        pl.BlockSpec((BLOCK, tables * LANES), at),
        pl.BlockSpec((BLOCK, LANES), at),
        pl.BlockSpec((BLOCK, pairs), at),
    ]
    operands = [dense_out, pooled, dense_cot, pair_cot]
    if with_ids:
        specs.append(pl.BlockSpec(ids.shape, lambda s: (0, 0, 0)))
        operands.append(ids)
    extra = 1 if with_ids else 0
    return pl.pallas_call(
        functools.partial(interact_kernel, steps, with_ids),
        grid=(steps + extra,),
        in_specs=specs,
        out_specs=[
            pl.BlockSpec((BLOCK, LANES), lambda s: (jnp.minimum(s, steps - 1), 0)),
            pl.BlockSpec((owners, BLOCK, held * LANES), lambda s: (0, s, 0)),
        ],
        out_shape=[
            jax.ShapeDtypeStruct((samples, LANES), BF16),
            jax.ShapeDtypeStruct((owners, samples + extra * held * slots, held * LANES), BF16),
        ],
        scratch_shapes=[
            pltpu.VMEM((BLOCK, padded), F32),
            pltpu.VMEM((BLOCK // 2, rows, LANES), F32),
            pltpu.VMEM((BLOCK, rows, LANES), F32),
            pltpu.VMEM((rows, BLOCK + 8, LANES), F32),
        ],
        compiler_params=params(),
        cost_estimate=cost(20 * samples / 256),
    )(*operands)


def count_kernel(first, samples, codes_ref, out_ref):
    sources, rows, _ = codes_ref.shape
    words, columns = out_ref.shape[2:]
    slots = 32 // FIELD
    bits = words.bit_length() - 1
    strip = 64
    table = pl.program_id(0)
    codes = jnp.concatenate(
        [codes_ref[source, :, first : first + samples] for source in range(sources)], 1
    ).astype(F32)
    mine = codes[:slots]
    for other in range(1, rows // slots):
        mine = jnp.where(table == other, codes[other * slots : (other + 1) * slots], mine)
    ids = decode(mine)
    word = ids & (words - 1)
    one = jnp.left_shift(1, FIELD * lax.shift_right_logical(ids, bits))
    total = one
    for by in range(1, slots):
        total = total + jnp.where(word == pltpu.roll(word, by, 0), pltpu.roll(one, by, 0), 0)
    place = lax.broadcasted_iota(jnp.int32, (strip, LANES), 0)
    for at in range(0, columns, LANES):
        words_at = [word[slot : slot + 1, at : at + LANES] for slot in range(slots)]
        totals_at = [total[slot : slot + 1, at : at + LANES] for slot in range(slots)]
        for start in range(0, words, strip):
            out = jnp.zeros((strip, LANES), jnp.int32)
            for slot in range(slots):
                out = jnp.where(words_at[slot] == place + start, totals_at[slot], out)
            out_ref[0, 0, start : start + strip, at : at + LANES] = out


def bag_counts(received, held, slots, words, first, samples, group):
    sources, rows, lanes = received.shape
    last = rows // (held * slots) - 1
    return pl.pallas_call(
        functools.partial(count_kernel, first, samples),
        grid=(held, sources // group),
        in_specs=[pl.BlockSpec((group, held * slots, lanes), lambda t, g: (g, last, 0))],
        out_specs=pl.BlockSpec((1, 1, words, group * samples), lambda t, g: (t, g, 0, 0)),
        out_shape=jax.ShapeDtypeStruct(
            (held, sources // group, words, group * samples), jnp.int32
        ),
        compiler_params=params(),
        cost_estimate=cost(24 * samples / 256),
    )(received)


def sum_kernel(plan, first, hst_ref, counts_ref, grads_ref, *rest):
    befores = () if first else rest[: len(plan)]
    outs = rest[0 if first else len(plan) :]
    totals = outs if first else outs[-len(plan) :]
    chips = 32 // FIELD // CORES
    here, core = hst_ref[0] // CORES, lax.rem(hst_ref[0], CORES)

    @pl.when(pl.program_id(1) == 0)
    def _():
        for number, total in enumerate(totals):
            total[...] = jnp.zeros_like(total) if first else befores[number][...]

    group, samples, _ = grads_ref.shape
    grads = grads_ref[...].reshape(group * samples, LANES)
    counts = counts_ref[0, 0]
    for number, ds in enumerate(plan):
        for k, d in enumerate(ds):
            for c in range(CORES):
                field = CORES * lax.rem(here + d, chips) + lax.rem(core + c, CORES)
                picked = (counts >> (FIELD * field)) & ((1 << FIELD) - 1)
                totals[number][0, k, c] += jnp.dot(
                    picked.astype(F32).astype(BF16), grads, preferred_element_type=F32
                )
    if first:
        return

    @pl.when(pl.program_id(1) == pl.num_programs(1) - 1)
    def _():
        at = 0
        for number, ds in enumerate(plan):
            for k in range(len(ds)):
                outs[at][...] = totals[number][0, k].astype(outs[at].dtype)
                at += 1


def row_sums(hst, counts, grads, befores, plan, table):
    tables, groups, words, columns = counts.shape
    group = grads.shape[0] // groups
    samples = columns // group
    begin = 0 if table is None else table
    count = tables if table is None else 1
    specs = [
        pl.BlockSpec((1, 1, words, columns), lambda t, g, hst: (begin + t, g, 0, 0)),
        pl.BlockSpec((group, samples, LANES), lambda t, g, hst: (g, 0, begin + t)),
    ]
    blocks = [
        pl.BlockSpec(
            (1, len(ds), CORES, words, LANES), lambda t, g, hst: (begin + t, 0, 0, 0, 0)
        )
        for ds in plan
    ]
    specs += blocks if befores else []
    scratch = []
    if table is None:
        out_specs = blocks
        out_shape = [
            jax.ShapeDtypeStruct((tables, len(ds), CORES, words, LANES), F32) for ds in plan
        ]
    else:
        every = [d for ds in plan for d in ds]
        out_specs = [
            pl.BlockSpec((CORES, words, LANES), lambda t, g, hst: (0, 0, 0)) for d in every
        ]
        out_shape = [
            jax.ShapeDtypeStruct((CORES, words, LANES), BF16 if d else F32) for d in every
        ]
        scratch = [pltpu.VMEM((1, len(ds), CORES, words, LANES), F32) for ds in plan]
    used = sum(len(ds) for ds in plan)
    return pl.pallas_call(
        functools.partial(sum_kernel, plan, not befores),
        grid_spec=pltpu.PrefetchScalarGridSpec(
            num_scalar_prefetch=1,
            grid=(count, groups),
            in_specs=specs,
            out_specs=out_specs,
            scratch_shapes=scratch,
        ),
        out_shape=out_shape,
        compiler_params=params(),
        cost_estimate=cost(count * groups * columns * used / 1600),
    )(hst, counts, grads, *befores)


def adagrad(number, grads, weights_ref, accum, new_weights_ref):
    rows, lanes = grads.shape
    mean = jnp.sum(grads * grads, 1, keepdims=True) * (1.0 / lanes)
    accum = jnp.broadcast_to(accum, (lanes, rows)).T + mean
    new_weights_ref[number] = weights_ref[number] - LEARN_RATE * grads / (
        jnp.sqrt(accum) + EPSILON
    )
    return accum.T[0:1]


def own_kernel(pieces, core_ref, weights_ref, accum_ref, *rest):
    piece_refs, (new_weights_ref, new_accum_ref, send_ref) = rest[:-3], rest[-3:]
    held = weights_ref.shape[0]
    mine = core_ref[0] == 0
    rows = []
    for t in range(held):
        total = piece_refs[t * pieces][...]
        for piece_ref in piece_refs[t * pieces + 1 : (t + 1) * pieces]:
            total = total + piece_ref[...].astype(F32)
        send_ref[t] = total[1].astype(BF16)
        accum = jnp.where(mine, accum_ref[t : t + 1], accum_ref[held + t : held + t + 1])
        rows.append(adagrad(t, total[0], weights_ref, accum, new_weights_ref))
    new_accum_ref[...] = jnp.concatenate(rows, 0)


def other_kernel(core_ref, weights_ref, accum_ref, grads_ref, own_accum_ref, *rest):
    new_weights_ref, new_accum_ref = rest[-2:]
    held = weights_ref.shape[0]
    mine = core_ref[0] == 0
    rows = []
    for t in range(held):
        accum = jnp.where(mine, accum_ref[held + t : held + t + 1], accum_ref[t : t + 1])
        grads = grads_ref[t].astype(F32)
        rows.append(adagrad(t, grads, weights_ref, accum, new_weights_ref))
    other, own = jnp.concatenate(rows, 0), own_accum_ref[...]
    new_accum_ref[...] = jnp.concatenate(
        [jnp.where(mine, own, other), jnp.where(mine, other, own)], 0
    )


def update(core, weights, accum, pieces):
    tables, words, lanes = weights.shape
    held = tables // CORES
    part = 256
    mine = pl.BlockSpec((held, part, lanes), lambda q, core: (core[0], q, 0))
    others = pl.BlockSpec((held, part, lanes), lambda q, core: (1 - core[0], q, 0))
    moved = pl.BlockSpec((held, part, lanes), lambda q, core: (0, q, 0))
    row = pl.BlockSpec((tables, part), lambda q, core: (0, q))
    half = pl.BlockSpec((held, part), lambda q, core: (0, q))
    piece = pl.BlockSpec((CORES, part, lanes), lambda q, core: (0, q, 0))
    flat = [array for table in pieces for array in table]
    new_weights, own_accum, send = pl.pallas_call(
        functools.partial(own_kernel, len(pieces[0])),
        grid_spec=pltpu.PrefetchScalarGridSpec(
            num_scalar_prefetch=1,
            grid=(words // part,),
            in_specs=[mine, row] + [piece] * len(flat),
            out_specs=[mine, half, moved],
        ),
        out_shape=[
            jax.ShapeDtypeStruct(weights.shape, F32),
            jax.ShapeDtypeStruct((held, words), F32),
            jax.ShapeDtypeStruct((held, words, lanes), BF16),
        ],
        compiler_params=params(SMALL),
        cost_estimate=cost(3),
    )(core, weights, accum, *flat)
    grads = lax.ppermute(send, "core", [(0, 1), (1, 0)])
    return pl.pallas_call(
        other_kernel,
        grid_spec=pltpu.PrefetchScalarGridSpec(
            num_scalar_prefetch=1,
            grid=(words // part,),
            in_specs=[others, row, moved, half, pl.BlockSpec(memory_space=pl.ANY)],
            out_specs=[others, row],
        ),
        out_shape=[
            jax.ShapeDtypeStruct(weights.shape, F32),
            jax.ShapeDtypeStruct(accum.shape, F32),
        ],
        input_output_aliases={5: 0},
        compiler_params=params(SMALL),
        cost_estimate=cost(2),
    )(core, weights, accum, grads, own_accum, new_weights)


def local(dense_out, pooled, dense_cot, pair_cot, bag_ids, weights, accum):
    samples = dense_out.shape[0]
    tables, slots, _ = bag_ids.shape
    words = weights.shape[1]
    chips = lax.axis_size("chip")
    devices = chips * CORES
    owners = lax.axis_size("wide") * CORES
    held = tables // owners
    core = lax.axis_index("core")
    hst = (lax.axis_index("chip") * CORES + core).reshape(1)

    def spread(x):
        return lax.all_to_all(x, ("wide", "core"), split_axis=0, concat_axis=0, tiled=True)

    args = (dense_out, pooled, dense_cot, pair_cot)
    late = samples - EARLY
    early_dense, send = interact(*args, bag_ids, owners, 0, EARLY)
    received = spread(send)
    late_dense, send = interact(*args, None, owners, EARLY, late)
    d_dense = jnp.concatenate([early_dense, late_dense], 0)
    early_counts = bag_counts(received, held, slots, words, 0, EARLY, 16)
    late_counts = bag_counts(received, held, slots, words, EARLY, late, LATE_GROUP)
    away, stay = tuple(range(1, chips)), (0,)
    leaving, staying = row_sums(hst, early_counts, received, (), (away, stay), None)
    received = spread(send)
    pieces = []
    for t in range(held):
        if t < held - 1:
            plan, befores = (away, stay), (leaving, staying)
        else:
            plan, befores = (away,), (leaving,)
        sums = row_sums(hst, late_counts, received, befores, plan, t)
        moved = []
        for d in away:
            ring = [(i, (i + d) % chips) for i in range(chips)]
            moved.append(lax.ppermute(sums[d - 1], "chip", ring))
        pieces.append([sums[-1]] + moved)
    pieces[-1][0] = row_sums(hst, late_counts, received, (staying,), (stay,), held - 1)[0]
    new_weights, new_accum = update(core.reshape(1), weights, accum, pieces)
    return d_dense, new_weights, new_accum


def solution(mesh):
    hst, wide = mesh.devices.shape
    split = Mesh(mesh.devices.reshape(hst // CORES, CORES, wide), ("chip", "core", "wide"))
    every = ("chip", "core", "wide")
    rows = ("chip", "core")
    in_specs = (
        P(every, None),
        P(every, None),
        P(every, None),
        P(every, None),
        P(None, None, every),
        P("wide", rows, None),
        P("wide", rows),
    )
    out_specs = (P(every, None), P("wide", rows, None), P("wide", rows))
    return jax.shard_map(local, mesh=split, in_specs=in_specs, out_specs=out_specs, check_vma=False)
```

time: 499 us -> 147 us (0.29); the launches traced: 490 us -> 146 us
  matrix products: 253 us -> 0 us
  Pallas kernels: 0 us -> 108 us
  waiting for transfers between devices: 94 us -> 9.04 us
  local copies, waits for them, and re-layouts: 83 us -> 4.47 us
  other arithmetic: 27.2 us -> 0.64 us
  between operations: 14.8 us -> 0.7 us
  starting transfers between devices: 15.8 us -> 22.4 us
    dot_general x34 -> x0, matrix products: 253 us -> none  [the longest x32 238 us: one_block(): return jnp.dot(counts, grads_table, preferred_element_type=jnp.float32)]
    pallas_call x0 -> x10, Pallas kernels: none -> 108 us  [the longest x4 53.7 us: row_sums(): pl.pallas_call(functools.partial(sum_kernel, plan, not befores), grid_spe...]
    all_to_all x2, waiting for transfers between devices: 59.1 us -> 6.95 us  [spread(): lax.all_to_all(x, ('wide', 'core'), split_axis=0, concat_axis=0, tiled=True)]
    reduce_scatter x1 -> x0, waiting for transfers between devices: 34.9 us -> none  [local(): lax.psum_scatter(summed.transpose(1, 0, 2).reshape(row_block * lax.axis_s...]
    reshape x5 -> x0, local copies, waits for them, and re-layouts: 22.9 us -> none  [the longest x2 8.5 us: local(): pair_grad = pair_grad.reshape(samples, num_feat, num_feat)]
    add x34 -> x0, other arithmetic: 20.4 us -> none  [the longest x32 19.8 us: one_block(): positions = start + jnp.arange(block_rows, dtype=jnp.int32)]
    dynamic_slice x32 -> x0, local copies, waits for them, and re-layouts: 19 us -> none  [window_sums(): summed = lax.map(one_block, starts)]
    ppermute x0 -> x7, starting transfers between devices: none -> 8.99 us  [the longest x6 8.99 us: local(): moved.append(lax.ppermute(sums[d - 1], 'chip', ring))]
  transfers between devices with their start and end apart: 3 -> 9, of which waited for: 2 -> 5; matrix products, arithmetic and copies ran while one was open for 9% -> 0% of each run, Pallas kernels for 0% -> 54%
where the time goes in v2:
time: 147 us; the launch traced here: 146 us
  Pallas kernels  108 us (73%)
  starting transfers between devices  22.4 us (15%)
  waiting for transfers between devices  9.04 us (6%)
  local copies, waits for them, and re-layouts  4.47 us (3%)
    pallas_call x4, Pallas kernels, row_sums(): pl.pallas_call(functools.partial(sum_kernel, plan, not befores), grid_spe...  53.7 us
    pallas_call x2, Pallas kernels, bag_counts(): pl.pallas_call(functools.partial(count_kernel, first, samples), grid=(hel...  26.7 us
    pallas_call x2, Pallas kernels, interact(): pl.pallas_call(functools.partial(interact_kernel, steps, with_ids), grid=...  23.6 us
    all_to_all x2, starting transfers between devices, spread(): lax.all_to_all(x, ('wide', 'core'), split_axis=0, concat_axis=0, tiled=True)  13.4 us
    ppermute x6, starting transfers between devices, local(): moved.append(lax.ppermute(sums[d - 1], 'chip', ring))  8.99 us
    all_to_all x2, waiting for transfers between devices, spread(): lax.all_to_all(x, ('wide', 'core'), split_axis=0, concat_axis=0, tiled=True)  6.95 us
    unnamed x15, local copies, waits for them, and re-layouts  4.47 us
  transfers between devices with their start and end apart: 9, of which 5 were waited for; matrix products, arithmetic and copies ran while one was open for 0% of the time, Pallas kernels for 54%

profile of v2, /device:TPU:0, one launch (start us, length us, event | category | flops | bytes accessed | tf_op | source)
XLA Modules:
  0.0 145.7 jit_solution(17124020962035510462)
XLA Ops:
  0.6 2.4 %copy.11.pair_ref = bf16[256,2080]{1,0:T(8,128)(2,1)} copy(bf16[256,2080]{0,1:T(8,128)(2,1)} %param.10) | data formatting | bytes 2129920 | tf_op args[3]
  3.0 7.5 %shard_map.94 = (bf16[64,128]{1,0:T(8,128)(2,1)}, bf16[32,80,256]{2,1,0:T(8,128)(2,1)}) custom-call(bf16[256,128]{1,0:T(8,128)(2,1)} %dense_ref.3, bf16[256,8192]{1,0:T(8,128)(2,1)} %pooled_ref.3, bf16[256,128]{1,0:T(8,128)(2,1)} %cot_ref.3, bf16[256,2080]{1,0:T(8,128)(2,1)} %copy.11.pair_ref, s32[64,8,256]{2,1,0:T(8,128)} %rest_0_.1), custom_call_target="tpu_custom_call" | custom-call | flops 1000000000 | bytes 65536 | tf_op jit(solution)/shard_map/pallas_call | solution.py:171
  10.5 8.4 %all-to-all-start = ((bf16[32,80,256]{2,1,0:T(8,128)(2,1)}), bf16[32,80,256]{2,1,0:T(8,128)(2,1)S(1)}, u32[]{:S(2)}, u32[]{:S(2)}) async-start(bf16[32,80,256]{2,1,0:T(8,128)(2,1)} %get-tuple-element.23), calls=%async_computation | async-start | bytes 2621440 | tf_op jit(solution)/shard_map/all_to_all | solution.py:421
  19.0 16.0 %shard_map.95 = (bf16[192,128]{1,0:T(8,128)(2,1)}, bf16[32,192,256]{2,1,0:T(8,128)(2,1)}) custom-call(bf16[256,128]{1,0:T(8,128)(2,1)} %dense_ref.3, bf16[256,8192]{1,0:T(8,128)(2,1)} %pooled_ref.3, bf16[256,128]{1,0:T(8,128)(2,1)} %cot_ref.3, bf16[256,2080]{1,0:T(8,128)(2,1)} %copy.11.pair_ref), custom_call_target="tpu_custom_call" | custom-call | flops 3000000000 | bytes 65536 | tf_op jit(solution)/shard_map/pallas_call | solution.py:171
  35.0 4.8 %all-to-all-done.codes_ref.grads_ref = bf16[32,80,256]{2,1,0:T(8,128)(2,1)S(1)} async-done(((bf16[32,80,256]{2,1,0:T(8,128)(2,1)}), bf16[32,80,256]{2,1,0:T(8,128)(2,1)S(1)}, u32[]{:S(2)}, u32[]{:S(2)}) %all-to-all-start) | async-done | bytes 1310752 | tf_op jit(solution)/shard_map/all_to_all | solution.py:421
  39.7 0.0 copy-start.4
  39.8 1.1 copy-done.4
  40.8 5.0 %all-to-all-start.1 = ((bf16[32,192,256]{2,1,0:T(8,128)(2,1)}), bf16[32,192,256]{2,1,0:T(8,128)(2,1)}, u32[]{:S(2)}, u32[]{:S(2)}) async-start(bf16[32,192,256]{2,1,0:T(8,128)(2,1)} %get-tuple-element.24), calls=%async_computation.1 | async-start | bytes 6291456 | tf_op jit(solution)/shard_map/all_to_all | solution.py:421
  45.8 7.9 %shard_map.97.counts_ref = s32[2,2,512,1024]{3,2,1,0:T(8,128)} custom-call(bf16[32,80,256]{2,1,0:T(8,128)(2,1)} %copy-done.4), custom_call_target="tpu_custom_call" | custom-call | flops 1200000000 | bytes 65536 | tf_op jit(solution)/shard_map/pallas_call | solution.py:227
  53.7 12.7 %shard_map.98 = (f32[2,3,2,512,128]{4,3,2,1,0:T(8,128)}, f32[2,1,2,512,128]{4,3,2,1,0:T(8,128)}) custom-call(s32[1]{0:T(128)} %bitcast.1.hst_ref, s32[2,2,512,1024]{3,2,1,0:T(8,128)} %shard_map.97.counts_ref, bf16[32,80,256]{2,1,0:T(8,128)(2,1)} %copy-done.4), custom_call_target="tpu_custom_call" | custom-call | flops 2048000000 | bytes 65536 | tf_op jit(solution)/shard_map/pallas_call | solution.py:308
  66.4 18.8 %shard_map.96.counts_ref = s32[2,4,512,1536]{3,2,1,0:T(8,128)} custom-call(bf16[32,80,256]{2,1,0:T(8,128)(2,1)} %copy-done.4), custom_call_target="tpu_custom_call" | custom-call | flops 3600000000 | bytes 65536 | tf_op jit(solution)/shard_map/pallas_call | solution.py:227
  85.2 2.2 %all-to-all-done.1.grads_ref = bf16[32,192,256]{2,1,0:T(8,128)(2,1)} async-done(((bf16[32,192,256]{2,1,0:T(8,128)(2,1)}), bf16[32,192,256]{2,1,0:T(8,128)(2,1)}, u32[]{:S(2)}, u32[]{:S(2)}) %all-to-all-start.1) | async-done | bytes 3145760 | tf_op jit(solution)/shard_map/all_to_all | solution.py:421
  87.4 17.9 %shard_map.99 = (bf16[2,512,128]{2,1,0:T(8,128)(2,1)}, bf16[2,512,128]{2,1,0:T(8,128)(2,1)}, bf16[2,512,128]{2,1,0:T(8,128)(2,1)}, f32[2,512,128]{2,1,0:T(8,128)}) custom-call(s32[1]{0:T(128)} %bitcast.1.hst_ref, s32[2,4,512,1536]{3,2,1,0:T(8,128)} %shard_map.96.counts_ref, bf16[32,192,256]{2,1,0:T(8,128)(2,1)} %all-to-all-done.1.grads_ref, ...), custom_call_target="tpu_custom_call" | custom-call | flops 3072000000 | bytes 65536 | tf_op jit(solution)/shard_map/pallas_call | solution.py:308
  105.3 1.5 %collective-permute-start = (bf16[2,512,128]{2,1,0:T(8,128)(2,1)}, bf16[2,512,128]{2,1,0:T(8,128)(2,1)S(1)}, u32[]{:S(2)}, u32[]{:S(2)}) collective-permute-start(bf16[2,512,128]{2,1,0:T(8,128)(2,1)} %get-tuple-element.28), channel_id=1, source_target_pairs={{0,32},{32,64},{64,96},{96,0},{1,33},{33,65},{65,97},{97,1},{2,34}... | collective-permute-start | bytes 786440 | tf_op jit(solution)/shard_map/ppermute | solution.py:444
  106.7 2.7 %collective-permute-start.1 = (bf16[2,512,128]{2,1,0:T(8,128)(2,1)}, bf16[2,512,128]{2,1,0:T(8,128)(2,1)}, u32[]{:S(2)}, u32[]{:S(2)}) collective-permute-start(bf16[2,512,128]{2,1,0:T(8,128)(2,1)} %get-tuple-element.29), channel_id=1, source_target_pairs={{0,64},{32,96},{64,0},{96,32},{1,65},{33,97},{65,1},{97,33},{2,66}... | collective-permute-start | bytes 786440 | tf_op jit(solution)/shard_map/ppermute | solution.py:444
  109.5 1.4 collective-permute-start.2
  110.9 14.8 %shard_map.101 = (bf16[2,512,128]{2,1,0:T(8,128)(2,1)}, bf16[2,512,128]{2,1,0:T(8,128)(2,1)}, bf16[2,512,128]{2,1,0:T(8,128)(2,1)}) custom-call(s32[1]{0:T(128)} %bitcast.1.hst_ref, s32[2,4,512,1536]{3,2,1,0:T(8,128)} %shard_map.96.counts_ref, bf16[32,192,256]{2,1,0:T(8,128)(2,1)} %all-to-all-done.1.grads_ref, f32[2,3,2,512,128]{4,3,2,1,0:T(8,128)} %get-tuple-element.25.rest_0_), custom_call_target="tpu_custom_call" | custom-call | flops 2304000000 | bytes 65536 | tf_op jit(solution)/shard_map/pallas_call | solution.py:308
  125.7 0.6 collective-permute-start.3
  126.3 0.9 collective-permute-start.4
  127.2 0.0 collective-permute-done.rest_1_
  127.2 0.0 copy-start
  127.2 0.0 copy-start.2
  127.2 0.0 copy-start.3
  127.2 1.9 %collective-permute-start.5 = (bf16[2,512,128]{2,1,0:T(8,128)(2,1)}, bf16[2,512,128]{2,1,0:T(8,128)(2,1)}, u32[]{:S(2)}, u32[]{:S(2)}) collective-permute-start(bf16[2,512,128]{2,1,0:T(8,128)(2,1)} %get-tuple-element.33), channel_id=1, source_target_pairs={{0,96},{32,0},{64,32},{96,64},{1,97},{33,1},{65,33},{97,65},{2,98}... | collective-permute-start | bytes 786440 | tf_op jit(solution)/shard_map/ppermute | solution.py:444
  129.1 0.0 copy-start.5
  129.1 0.0 copy-start.6
  129.1 8.4 %shard_map.100.rest_4_ = f32[2,512,128]{2,1,0:T(8,128)} custom-call(s32[1]{0:T(128)} %bitcast.1.hst_ref, s32[2,4,512,1536]{3,2,1,0:T(8,128)} %shard_map.96.counts_ref, bf16[32,192,256]{2,1,0:T(8,128)(2,1)} %all-to-all-done.1.grads_ref, f32[2,1,2,512,128]{4,3,2,1,0:T(8,128)} %get-tuple-element.26.rest_1_.rest_0_), custom_call_target="tpu_custom_call" | custom-call | flops 768000000 | bytes 65536 | tf_op jit(solution)/shard_map/pallas_call | solution.py:308
  137.5 0.0 collective-permute-done.1.rest_2_
  137.5 0.0 collective-permute-done.2.rest_3_
  137.5 0.5 collective-permute-done.3.rest_5_
  138.0 0.0 collective-permute-done.4.rest_6_
  138.0 0.7 collective-permute-done.5.rest_7_
  138.7 0.0 copy-done
  138.7 0.0 copy-done.2
  138.7 0.0 copy-done.3
  138.7 0.0 copy-start.1
  138.7 1.0 copy-done.1
  139.7 2.9 %shard_map.102 = (f32[4,512,128]{2,1,0:T(8,128)}, f32[2,512]{1,0:T(2,128)S(1)}, bf16[2,512,128]{2,1,0:T(8,128)(2,1)S(1)}) custom-call(s32[1]{0:T(128)} %bitcast.core_ref, f32[4,512,128]{2,1,0:T(8,128)S(1)} %copy-done, f32[4,512]{1,0:T(4,128)S(1)} %copy-done.3, f32[2,512,128]{2,1,0:T(8,128)S(1)} %copy-done.2, ...), custom_call_target="tpu_custom_call" | custom-call | flops 600000000 | bytes 65536 | tf_op jit(solution)/shard_map/pallas_call | solution.py:374
  142.6 0.0 collective-permute-start.6
  142.6 0.0 copy-done.5
  142.6 0.0 copy-done.6
  142.6 0.6 pad_maximum_fusion
  143.2 0.9 collective-permute-done.6.grads_ref
  144.1 1.6 %shard_map.103 = (f32[4,512,128]{2,1,0:T(8,128)}, f32[4,512]{1,0:T(4,128)}) custom-call(s32[1]{0:T(128)} %bitcast.core_ref, f32[4,512,128]{2,1,0:T(8,128)S(1)} %copy-done, f32[4,512]{1,0:T(4,128)S(1)} %copy-done.3, bf16[2,512,128]{2,1,0:T(8,128)(2,1)S(1)} %collective-permute-done.6.grads_ref, ...), custom_call_target="tpu_custom_call", output_to_operand_aliasing={{0}: (5, {})} | custom-call | flops 400000000 | bytes 65536 | tf_op jit(solution)/shard_map/pallas_call | solution.py:391
Async XLA Ops:
  10.5 29.2 %all-to-all-start = ((bf16[32,80,256]{2,1,0:T(8,128)(2,1)}), bf16[32,80,256]{2,1,0:T(8,128)(2,1)S(1)}, u32[]{:S(2)}, u32[]{:S(2)}) async-start(bf16[32,80,256]{2,1,0:T(8,128)(2,1)} %get-tuple-element.23), calls=%async_computation | async-start | bytes 2621440 | tf_op jit(solution)/shard_map/all_to_all | solution.py:421
  39.7 1.1 copy-start.4
  40.8 46.6 %all-to-all-start.1 = ((bf16[32,192,256]{2,1,0:T(8,128)(2,1)}), bf16[32,192,256]{2,1,0:T(8,128)(2,1)}, u32[]{:S(2)}, u32[]{:S(2)}) async-start(bf16[32,192,256]{2,1,0:T(8,128)(2,1)} %get-tuple-element.24), calls=%async_computation.1 | async-start | bytes 6291456 | tf_op jit(solution)/shard_map/all_to_all | solution.py:421
  105.3 22.0 %collective-permute-start = (bf16[2,512,128]{2,1,0:T(8,128)(2,1)}, bf16[2,512,128]{2,1,0:T(8,128)(2,1)S(1)}, u32[]{:S(2)}, u32[]{:S(2)}) collective-permute-start(bf16[2,512,128]{2,1,0:T(8,128)(2,1)} %get-tuple-element.28), channel_id=1, source_target_pairs={{0,32},{32,64},{64,96},{96,0},{1,33},{33,65},{65,97},{97,1},{2,34}... | collective-permute-start | bytes 786440 | tf_op jit(solution)/shard_map/ppermute | solution.py:444
  106.7 30.7 %collective-permute-start.1 = (bf16[2,512,128]{2,1,0:T(8,128)(2,1)}, bf16[2,512,128]{2,1,0:T(8,128)(2,1)}, u32[]{:S(2)}, u32[]{:S(2)}) collective-permute-start(bf16[2,512,128]{2,1,0:T(8,128)(2,1)} %get-tuple-element.29), channel_id=1, source_target_pairs={{0,64},{32,96},{64,0},{96,32},{1,65},{33,97},{65,1},{97,33},{2,66}... | collective-permute-start | bytes 786440 | tf_op jit(solution)/shard_map/ppermute | solution.py:444
  109.5 28.0 %collective-permute-start.2 = (bf16[2,512,128]{2,1,0:T(8,128)(2,1)}, bf16[2,512,128]{2,1,0:T(8,128)(2,1)}, u32[]{:S(2)}, u32[]{:S(2)}) collective-permute-start(bf16[2,512,128]{2,1,0:T(8,128)(2,1)} %get-tuple-element.30), channel_id=1, source_target_pairs={{0,96},{32,0},{64,32},{96,64},{1,97},{33,1},{65,33},{97,65},{2,98}... | collective-permute-start | bytes 786440 | tf_op jit(solution)/shard_map/ppermute | solution.py:444
  125.7 12.3 %collective-permute-start.3 = (bf16[2,512,128]{2,1,0:T(8,128)(2,1)}, bf16[2,512,128]{2,1,0:T(8,128)(2,1)}, u32[]{:S(2)}, u32[]{:S(2)}) collective-permute-start(bf16[2,512,128]{2,1,0:T(8,128)(2,1)} %get-tuple-element.31), channel_id=1, source_target_pairs={{0,32},{32,64},{64,96},{96,0},{1,33},{33,65},{65,97},{97,1},{2,34}... | collective-permute-start | bytes 786440 | tf_op jit(solution)/shard_map/ppermute | solution.py:444
  126.3 11.7 %collective-permute-start.4 = (bf16[2,512,128]{2,1,0:T(8,128)(2,1)}, bf16[2,512,128]{2,1,0:T(8,128)(2,1)}, u32[]{:S(2)}, u32[]{:S(2)}) collective-permute-start(bf16[2,512,128]{2,1,0:T(8,128)(2,1)} %get-tuple-element.32), channel_id=1, source_target_pairs={{0,64},{32,96},{64,0},{96,32},{1,65},{33,97},{65,1},{97,33},{2,66}... | collective-permute-start | bytes 786440 | tf_op jit(solution)/shard_map/ppermute | solution.py:444
  127.2 11.5 %copy-start = (f32[4,512,128]{2,1,0:T(8,128)S(1)}, f32[4,512,128]{2,1,0:T(8,128)}, u32[]{:S(2)}) copy-start(f32[4,512,128]{2,1,0:T(8,128)} %weights_ref.3) | copy-start | bytes 3145732
  127.2 11.5 %copy-start.2 = (f32[2,512,128]{2,1,0:T(8,128)S(1)}, f32[2,512,128]{2,1,0:T(8,128)}, u32[]{:S(2)}) copy-start(f32[2,512,128]{2,1,0:T(8,128)} %get-tuple-element.27.rest_0_) | copy-start | bytes 1572868
  127.2 11.5 %copy-start.3 = (f32[4,512]{1,0:T(4,128)S(1)}, f32[4,512]{1,0:T(4,128)}, u32[]{:S(2)}) copy-start(f32[4,512]{1,0:T(4,128)} %accum_ref.3) | copy-start | bytes 24580
  127.2 11.4 %collective-permute-start.5 = (bf16[2,512,128]{2,1,0:T(8,128)(2,1)}, bf16[2,512,128]{2,1,0:T(8,128)(2,1)}, u32[]{:S(2)}, u32[]{:S(2)}) collective-permute-start(bf16[2,512,128]{2,1,0:T(8,128)(2,1)} %get-tuple-element.33), channel_id=1, source_target_pairs={{0,96},{32,0},{64,32},{96,64},{1,97},{33,1},{65,33},{97,65},{2,98}... | collective-permute-start | bytes 786440 | tf_op jit(solution)/shard_map/ppermute | solution.py:444
  129.1 13.5 %copy-start.5 = (bf16[192,128]{1,0:T(8,128)(2,1)S(1)}, bf16[192,128]{1,0:T(8,128)(2,1)}, u32[]{:S(2)}) copy-start(bf16[192,128]{1,0:T(8,128)(2,1)} %get-tuple-element.22) | copy-start | bytes 147460
  129.1 13.5 %copy-start.6 = (bf16[64,128]{1,0:T(8,128)(2,1)S(1)}, bf16[64,128]{1,0:T(8,128)(2,1)}, u32[]{:S(2)}) copy-start(bf16[64,128]{1,0:T(8,128)(2,1)} %get-tuple-element.21) | copy-start | bytes 49156
  138.7 1.0 copy-start.1
  142.6 1.5 %collective-permute-start.6 = (bf16[2,512,128]{2,1,0:T(8,128)(2,1)S(1)}, bf16[2,512,128]{2,1,0:T(8,128)(2,1)S(1)}, u32[]{:S(2)}, u32[]{:S(2)}) collective-permute-start(bf16[2,512,128]{2,1,0:T(8,128)(2,1)S(1)} %get-tuple-element.34), channel_id=1, source_target_pairs={{0,16},{16,0},{1,17},{17,1},{2,18},{18,2},{3,19},{19,3},{4,20},{20... | collective-permute-start | bytes 786440 | tf_op jit(solution)/shard_map/ppermute | solution.py:390

commit v3 on v2

--- a/solution.py
+++ b/solution.py
@@ -16,16 +16,23 @@
 BLOCK = 32
 CORES = 2
 CODE = 7
-VMEM = 62 << 20
+STRIP = 64
+VMEM = 40 << 20
+FULL = 62 << 20
 SMALL = 12 << 20
 EARLY = 64
-LATE_GROUP = 8
+GROUP = 8
+AWAY = (1, 2, 3)
 BF16 = jnp.bfloat16
 F32 = jnp.float32
 
 
 def cost(micros):
     return pl.CostEstimate(flops=int(micros * 2e8), bytes_accessed=1 << 16, transcendentals=0)
+
+
+def in_hbm(x):
+    return pltpu.with_memory_space_constraint(x, pltpu.HBM)
 
 
 def params(size=VMEM):
@@ -120,7 +127,8 @@
 
     def two_samples(b, carry):
         both = lower[b]
-        turned = jnp.concatenate([both.T, jnp.zeros((LANES, LANES - rows), F32)], 1)
+        turned = both.astype(BF16).T.astype(F32)
+        turned = jnp.concatenate([turned, jnp.zeros((LANES, LANES - rows), F32)], 1)
         first = jnp.where(row_lane < HALF, both, 0.0)
         second = jnp.where(row_lane < HALF, pltpu.roll(both, HALF, 1), 0.0)
         first = first + jnp.concatenate([turned[:HALF], below], 0)
@@ -144,9 +152,9 @@
         send_ref[t // held, :, place : place + LANES] = grads[t + 1, 0:block].astype(BF16)
 
 
-def interact(dense_out, pooled, dense_cot, pair_cot, ids, owners, first, samples):
+def interact(dense_out, pooled, dense_cot, pair_cot, ids, owners, first):
     tables = pooled.shape[1] // LANES
-    pairs = pair_cot.shape[1]
+    samples, pairs = pair_cot.shape
     held = tables // owners
     rows = (tables + 1 + 7) // 8 * 8
     padded = (pairs // LANES + 1) * LANES
@@ -161,12 +169,12 @@
         pl.BlockSpec((BLOCK, LANES), at),
         pl.BlockSpec((BLOCK, tables * LANES), at),
         pl.BlockSpec((BLOCK, LANES), at),
-        pl.BlockSpec((BLOCK, pairs), at),
+        pl.BlockSpec((BLOCK, pairs), lambda s: (jnp.minimum(s, steps - 1), 0)),
     ]
-    operands = [dense_out, pooled, dense_cot, pair_cot]
+    operands = [in_hbm(x) for x in (dense_out, pooled, dense_cot, pair_cot)]
     if with_ids:
         specs.append(pl.BlockSpec(ids.shape, lambda s: (0, 0, 0)))
-        operands.append(ids)
+        operands.append(in_hbm(ids))
     extra = 1 if with_ids else 0
     return pl.pallas_call(
         functools.partial(interact_kernel, steps, with_ids),
@@ -178,7 +186,7 @@
         ],
         out_shape=[
             jax.ShapeDtypeStruct((samples, LANES), BF16),
-            jax.ShapeDtypeStruct((owners, samples + extra * held * slots, held * LANES), BF16),
+            pltpu.HBM((owners, samples + extra * held * slots, held * LANES), BF16),
         ],
         scratch_shapes=[
             pltpu.VMEM((BLOCK, padded), F32),
@@ -186,18 +194,15 @@
             pltpu.VMEM((BLOCK, rows, LANES), F32),
             pltpu.VMEM((rows, BLOCK + 8, LANES), F32),
         ],
-        compiler_params=params(),
+        compiler_params=params(FULL),
         cost_estimate=cost(20 * samples / 256),
     )(*operands)
 
 
-def count_kernel(first, samples, codes_ref, out_ref):
+def slot_words(first, samples, words, table, codes_ref):
     sources, rows, _ = codes_ref.shape
-    words, columns = out_ref.shape[2:]
     slots = 32 // FIELD
     bits = words.bit_length() - 1
-    strip = 64
-    table = pl.program_id(0)
     codes = jnp.concatenate(
         [codes_ref[source, :, first : first + samples] for source in range(sources)], 1
     ).astype(F32)
@@ -210,114 +215,142 @@
     total = one
     for by in range(1, slots):
         total = total + jnp.where(word == pltpu.roll(word, by, 0), pltpu.roll(one, by, 0), 0)
-    place = lax.broadcasted_iota(jnp.int32, (strip, LANES), 0)
-    for at in range(0, columns, LANES):
-        words_at = [word[slot : slot + 1, at : at + LANES] for slot in range(slots)]
-        totals_at = [total[slot : slot + 1, at : at + LANES] for slot in range(slots)]
-        for start in range(0, words, strip):
-            out = jnp.zeros((strip, LANES), jnp.int32)
-            for slot in range(slots):
-                out = jnp.where(words_at[slot] == place + start, totals_at[slot], out)
-            out_ref[0, 0, start : start + strip, at : at + LANES] = out
-
-
-def bag_counts(received, held, slots, words, first, samples, group):
+    return word, total
+
+
+def count_column(word, total, at, out_ref):
+    words = out_ref.shape[0]
+    slots = word.shape[0]
+    place = lax.broadcasted_iota(jnp.int32, (STRIP, LANES), 0)
+    words_at = [word[slot : slot + 1, at : at + LANES] for slot in range(slots)]
+    totals_at = [total[slot : slot + 1, at : at + LANES] for slot in range(slots)]
+    for start in range(0, words, STRIP):
+        out = jnp.zeros((STRIP, LANES), jnp.int32)
+        for slot in range(slots):
+            out = jnp.where(words_at[slot] == place + start, totals_at[slot], out)
+        out_ref[start : start + STRIP, at : at + LANES] = out
+
+
+def early_kernel(late, hst_ref, grads_ref, codes_ref, total_ref, late_ref, counts_ref):
+    @pl.when(pl.program_id(1) == 0)
+    def _():
+        total_ref[...] = jnp.zeros_like(total_ref)
+
+    group, samples, _ = grads_ref.shape
+    chips = total_ref.shape[1]
+    fields = chips * CORES
+    words = counts_ref.shape[0]
+    table = pl.program_id(0)
+    word, total = slot_words(0, samples, words, table, codes_ref)
+    for at in range(0, counts_ref.shape[1], LANES):
+        count_column(word, total, at, counts_ref)
+    grads = grads_ref[...].reshape(group * samples, LANES)
+    word, total = slot_words(samples, late, words, table, codes_ref)
+    lanes = list(range(0, late_ref.shape[3], LANES))
+    here, core = hst_ref[0] // CORES, lax.rem(hst_ref[0], CORES)
+    for field in range(fields):
+        if field < fields - 1:
+            taken, scale = counts_ref[...] & (((1 << FIELD) - 1) << (FIELD * field)), FIELD * field
+        else:
+            taken, scale = lax.shift_right_logical(counts_ref[...], FIELD * field), 0
+        part = jnp.dot(
+            taken.astype(F32).astype(BF16), grads, preferred_element_type=F32
+        )
+        chip = lax.rem(field // CORES + 2 * chips - 1 - here, chips)
+        c = lax.rem(field + core, CORES)
+        total_ref[0, chip, c] += part * 2.0**-scale
+        begin, end = (len(lanes) * n // fields for n in (field, field + 1))
+        for at in lanes[begin:end]:
+            count_column(word, total, at, late_ref.at[0, 0])
+
+
+def early_sums(hst, received, held, slots, words, early, late, chips):
     sources, rows, lanes = received.shape
-    last = rows // (held * slots) - 1
+    groups = sources // GROUP
+    codes = held * slots
+    last = rows // codes - 1
+    totals = (chips, CORES, words, LANES)
     return pl.pallas_call(
-        functools.partial(count_kernel, first, samples),
-        grid=(held, sources // group),
-        in_specs=[pl.BlockSpec((group, held * slots, lanes), lambda t, g: (g, last, 0))],
-        out_specs=pl.BlockSpec((1, 1, words, group * samples), lambda t, g: (t, g, 0, 0)),
-        out_shape=jax.ShapeDtypeStruct(
-            (held, sources // group, words, group * samples), jnp.int32
+        functools.partial(early_kernel, late),
+        grid_spec=pltpu.PrefetchScalarGridSpec(
+            num_scalar_prefetch=1,
+            grid=(held, groups),
+            in_specs=[
+                pl.BlockSpec((GROUP, early, LANES), lambda t, g, hst: (g, 0, t)),
+                pl.BlockSpec((GROUP, codes, lanes), lambda t, g, hst: (g, last, 0)),
+            ],
+            out_specs=[
+                pl.BlockSpec((1,) + totals, lambda t, g, hst: (t, 0, 0, 0, 0)),
+                pl.BlockSpec((1, 1, words, GROUP * late), lambda t, g, hst: (t, g, 0, 0)),
+            ],
+            scratch_shapes=[pltpu.VMEM((words, GROUP * early), jnp.int32)],
         ),
-        compiler_params=params(),
-        cost_estimate=cost(24 * samples / 256),
-    )(received)
-
-
-def sum_kernel(plan, first, hst_ref, counts_ref, grads_ref, *rest):
-    befores = () if first else rest[: len(plan)]
-    outs = rest[0 if first else len(plan) :]
-    totals = outs if first else outs[-len(plan) :]
+        out_shape=[
+            jax.ShapeDtypeStruct((held,) + totals, F32),
+            pltpu.HBM((held, groups, words, GROUP * late), jnp.int32),
+        ],
+        compiler_params=params(FULL),
+        cost_estimate=cost(25),
+    )(hst, in_hbm(received), in_hbm(received))
+
+
+def picked(counts, hst_ref, d, c):
     chips = 32 // FIELD // CORES
     here, core = hst_ref[0] // CORES, lax.rem(hst_ref[0], CORES)
-
-    @pl.when(pl.program_id(1) == 0)
-    def _():
-        for number, total in enumerate(totals):
-            total[...] = jnp.zeros_like(total) if first else befores[number][...]
+    field = CORES * lax.rem(here + d, chips) + lax.rem(core + c, CORES)
+    return ((counts >> (FIELD * field)) & ((1 << FIELD) - 1)).astype(F32).astype(BF16)
+
+
+def sum_kernel(ds, hst_ref, counts_ref, grads_ref, before_ref, *rest):
+    outs, total = rest[:-1], rest[-1]
+
+    @pl.when(pl.program_id(0) == 0)
+    def _():
+        total[...] = before_ref[0]
 
     group, samples, _ = grads_ref.shape
     grads = grads_ref[...].reshape(group * samples, LANES)
     counts = counts_ref[0, 0]
-    for number, ds in enumerate(plan):
-        for k, d in enumerate(ds):
-            for c in range(CORES):
-                field = CORES * lax.rem(here + d, chips) + lax.rem(core + c, CORES)
-                picked = (counts >> (FIELD * field)) & ((1 << FIELD) - 1)
-                totals[number][0, k, c] += jnp.dot(
-                    picked.astype(F32).astype(BF16), grads, preferred_element_type=F32
-                )
-    if first:
-        return
-
-    @pl.when(pl.program_id(1) == pl.num_programs(1) - 1)
-    def _():
-        at = 0
-        for number, ds in enumerate(plan):
-            for k in range(len(ds)):
-                outs[at][...] = totals[number][0, k].astype(outs[at].dtype)
-                at += 1
-
-
-def row_sums(hst, counts, grads, befores, plan, table):
-    tables, groups, words, columns = counts.shape
+    for k, d in enumerate(ds):
+        for c in range(CORES):
+            total[k, c] += jnp.dot(
+                picked(counts, hst_ref, d, c), grads, preferred_element_type=F32
+            )
+
+    @pl.when(pl.program_id(0) == pl.num_programs(0) - 1)
+    def _():
+        for k, out in enumerate(outs):
+            out[...] = total[k].astype(out.dtype)
+
+
+def row_sums(hst, counts, grads, before, ds, table):
+    _, groups, words, columns = counts.shape
     group = grads.shape[0] // groups
     samples = columns // group
-    begin = 0 if table is None else table
-    count = tables if table is None else 1
-    specs = [
-        pl.BlockSpec((1, 1, words, columns), lambda t, g, hst: (begin + t, g, 0, 0)),
-        pl.BlockSpec((group, samples, LANES), lambda t, g, hst: (g, 0, begin + t)),
-    ]
-    blocks = [
-        pl.BlockSpec(
-            (1, len(ds), CORES, words, LANES), lambda t, g, hst: (begin + t, 0, 0, 0, 0)
-        )
-        for ds in plan
-    ]
-    specs += blocks if befores else []
-    scratch = []
-    if table is None:
-        out_specs = blocks
-        out_shape = [
-            jax.ShapeDtypeStruct((tables, len(ds), CORES, words, LANES), F32) for ds in plan
-        ]
-    else:
-        every = [d for ds in plan for d in ds]
-        out_specs = [
-            pl.BlockSpec((CORES, words, LANES), lambda t, g, hst: (0, 0, 0)) for d in every
-        ]
-        out_shape = [
-            jax.ShapeDtypeStruct((CORES, words, LANES), BF16 if d else F32) for d in every
-        ]
-        scratch = [pltpu.VMEM((1, len(ds), CORES, words, LANES), F32) for ds in plan]
-    used = sum(len(ds) for ds in plan)
+    at = (ds[0] - 1) % before.shape[1] // len(ds)
     return pl.pallas_call(
-        functools.partial(sum_kernel, plan, not befores),
+        functools.partial(sum_kernel, ds),
         grid_spec=pltpu.PrefetchScalarGridSpec(
             num_scalar_prefetch=1,
-            grid=(count, groups),
-            in_specs=specs,
-            out_specs=out_specs,
-            scratch_shapes=scratch,
+            grid=(groups,),
+            in_specs=[
+                pl.BlockSpec((1, 1, words, columns), lambda g, hst: (table, g, 0, 0)),
+                pl.BlockSpec((group, samples, LANES), lambda g, hst: (g, 0, table)),
+                pl.BlockSpec(
+                    (1, len(ds), CORES, words, LANES), lambda g, hst: (table, at, 0, 0, 0)
+                ),
+            ],
+            out_specs=[
+                pl.BlockSpec((CORES, words, LANES), lambda g, hst: (0, 0, 0)) for d in ds
+            ],
+            scratch_shapes=[pltpu.VMEM((len(ds), CORES, words, LANES), F32)],
         ),
-        out_shape=out_shape,
+        out_shape=[
+            jax.ShapeDtypeStruct((CORES, words, LANES), BF16 if d else F32) for d in ds
+        ],
         compiler_params=params(),
-        cost_estimate=cost(count * groups * columns * used / 1600),
-    )(hst, counts, grads, *befores)
+        cost_estimate=cost(2 * len(ds)),
+    )(hst, in_hbm(counts), in_hbm(grads), before)
 
 
 def adagrad(number, grads, weights_ref, accum, new_weights_ref):
@@ -420,30 +453,26 @@
     def spread(x):
         return lax.all_to_all(x, ("wide", "core"), split_axis=0, concat_axis=0, tiled=True)
 
-    args = (dense_out, pooled, dense_cot, pair_cot)
     late = samples - EARLY
-    early_dense, send = interact(*args, bag_ids, owners, 0, EARLY)
+    early_pairs, late_pairs = pair_cot[:EARLY], pair_cot[EARLY:]
+    early_dense, send = interact(dense_out, pooled, dense_cot, early_pairs, bag_ids, owners, 0)
     received = spread(send)
-    late_dense, send = interact(*args, None, owners, EARLY, late)
+    late_dense, send = interact(dense_out, pooled, dense_cot, late_pairs, None, owners, EARLY)
     d_dense = jnp.concatenate([early_dense, late_dense], 0)
-    early_counts = bag_counts(received, held, slots, words, 0, EARLY, 16)
-    late_counts = bag_counts(received, held, slots, words, EARLY, late, LATE_GROUP)
-    away, stay = tuple(range(1, chips)), (0,)
-    leaving, staying = row_sums(hst, early_counts, received, (), (away, stay), None)
+    before, counts = early_sums(hst, received, held, slots, words, EARLY, late, chips)
     received = spread(send)
     pieces = []
     for t in range(held):
-        if t < held - 1:
-            plan, befores = (away, stay), (leaving, staying)
-        else:
-            plan, befores = (away,), (leaving,)
-        sums = row_sums(hst, late_counts, received, befores, plan, t)
+        everything = t < held - 1
+        prior = before if t else in_hbm(before)
+        sums = list(row_sums(hst, counts, received, prior, AWAY + (0,) * everything, t))
+        before, sums[0] = lax.optimization_barrier((before, sums[0]))
         moved = []
-        for d in away:
+        for d in AWAY:
             ring = [(i, (i + d) % chips) for i in range(chips)]
             moved.append(lax.ppermute(sums[d - 1], "chip", ring))
-        pieces.append([sums[-1]] + moved)
-    pieces[-1][0] = row_sums(hst, late_counts, received, (staying,), (stay,), held - 1)[0]
+        pieces.append(sums[len(AWAY) :] + moved)
+    pieces[-1] = list(row_sums(hst, counts, received, before, (0,), held - 1)) + pieces[-1]
     new_weights, new_accum = update(core.reshape(1), weights, accum, pieces)
     return d_dense, new_weights, new_accum
 

time: 147 us -> 142 us (0.966)
  Pallas kernels: 108 us -> 98.9 us
  waiting for transfers between devices: 9.04 us -> 13.3 us
    pallas_call x6 -> x4, Pallas kernels: 80.4 us -> 72.7 us  [the longest x3 38.7 us: row_sums(): pl.pallas_call(functools.partial(sum_kernel, ds), grid_spec=pltpu.Prefetc...]
    all_to_all x2, waiting for transfers between devices: 6.95 us -> 10.9 us  [spread(): lax.all_to_all(x, ('wide', 'core'), split_axis=0, concat_axis=0, tiled=True)]
    unnamed x15 -> x14, local copies, waits for them, and re-layouts: 4.47 us -> 2.63 us
    slice x0 -> x2, local copies, waits for them, and re-layouts: none -> 1.52 us  [local(): early_pairs, late_pairs = (pair_cot[:EARLY], pair_cot[EARLY:])]
  transfers between devices with their start and end apart: 9 -> 9, of which waited for: 5 -> 5; matrix products, arithmetic and copies ran while one was open for 0% -> 2% of each run, Pallas kernels for 54% -> 50%
where the time goes in v3:
time: 142 us; the launch traced here: 141 us
  Pallas kernels  98.9 us (70%)
  starting transfers between devices  22.9 us (16%)
  waiting for transfers between devices  13.3 us (9%)
  local copies, waits for them, and re-layouts  4.15 us (3%)
    pallas_call x3, Pallas kernels, row_sums(): pl.pallas_call(functools.partial(sum_kernel, ds), grid_spec=pltpu.Prefetc...  38.7 us
    pallas_call x1, Pallas kernels, early_sums(): pl.pallas_call(functools.partial(early_kernel, late), grid_spec=pltpu.Pre...  34 us
    pallas_call x2, Pallas kernels, interact(): pl.pallas_call(functools.partial(interact_kernel, steps, with_ids), grid=...  22.6 us
    all_to_all x2, starting transfers between devices, spread(): lax.all_to_all(x, ('wide', 'core'), split_axis=0, concat_axis=0, tiled=True)  13.5 us
    all_to_all x2, waiting for transfers between devices, spread(): lax.all_to_all(x, ('wide', 'core'), split_axis=0, concat_axis=0, tiled=True)  10.9 us
    ppermute x6, starting transfers between devices, local(): moved.append(lax.ppermute(sums[d - 1], 'chip', ring))  9.41 us
  transfers between devices with their start and end apart: 9, of which 5 were waited for; matrix products, arithmetic and copies ran while one was open for 2% of the time, Pallas kernels for 50%

profile of v3, /device:TPU:0, one launch (start us, length us, event | category | flops | bytes accessed | tf_op | source)
XLA Modules:
  0.0 140.7 jit_solution(4912577554251017079)
XLA Ops:
  0.6 1.1 slice.6
  1.7 0.9 copy.13.pair_ref
  2.7 0.0 copy-start.3
  2.7 7.3 %shard_map.94 = (bf16[64,128]{1,0:T(8,128)(2,1)}, bf16[32,80,256]{2,1,0:T(8,128)(2,1)}) custom-call(bf16[256,128]{1,0:T(8,128)(2,1)} %dense_ref.3, bf16[256,8192]{1,0:T(8,128)(2,1)} %pooled_ref.3, bf16[256,128]{1,0:T(8,128)(2,1)} %cot_ref.3, bf16[64,2080]{1,0:T(8,128)(2,1)} %copy.13.pair_ref, s32[64,8,256]{2,1,0:T(8,128)} %rest_0_.1), custom_call_target="tpu_custom_call" | custom-call | flops 1000000000 | bytes 65536 | tf_op jit(solution)/shard_map/pallas_call | solution.py:179
  10.0 8.5 %all-to-all-start = ((bf16[32,80,256]{2,1,0:T(8,128)(2,1)}), bf16[32,80,256]{2,1,0:T(8,128)(2,1)}, u32[]{:S(2)}, u32[]{:S(2)}) async-start(bf16[32,80,256]{2,1,0:T(8,128)(2,1)} %get-tuple-element.27), calls=%async_computation | async-start | bytes 2621440 | tf_op jit(solution)/shard_map/all_to_all | solution.py:454
  18.5 0.0 copy-done.3
  18.6 0.4 slice.7
  19.0 1.7 %copy.14.pair_ref = bf16[192,2080]{1,0:T(8,128)(2,1)} copy(bf16[192,2080]{0,1:T(8,128)(2,1)S(1)} %slice.7) | data formatting | bytes 1597440
  20.7 15.3 %shard_map.95 = (bf16[192,128]{1,0:T(8,128)(2,1)}, bf16[32,192,256]{2,1,0:T(8,128)(2,1)}) custom-call(bf16[256,128]{1,0:T(8,128)(2,1)} %dense_ref.3, bf16[256,8192]{1,0:T(8,128)(2,1)} %pooled_ref.3, bf16[256,128]{1,0:T(8,128)(2,1)} %cot_ref.3, bf16[192,2080]{1,0:T(8,128)(2,1)} %copy.14.pair_ref), custom_call_target="tpu_custom_call" | custom-call | flops 3000000000 | bytes 65536 | tf_op jit(solution)/shard_map/pallas_call | solution.py:179
  36.0 3.4 %all-to-all-done.grads_ref.codes_ref = bf16[32,80,256]{2,1,0:T(8,128)(2,1)} async-done(((bf16[32,80,256]{2,1,0:T(8,128)(2,1)}), bf16[32,80,256]{2,1,0:T(8,128)(2,1)}, u32[]{:S(2)}, u32[]{:S(2)}) %all-to-all-start) | async-done | bytes 1310752 | tf_op jit(solution)/shard_map/all_to_all | solution.py:454
  39.3 5.0 %all-to-all-start.1 = ((bf16[32,192,256]{2,1,0:T(8,128)(2,1)}), bf16[32,192,256]{2,1,0:T(8,128)(2,1)}, u32[]{:S(2)}, u32[]{:S(2)}) async-start(bf16[32,192,256]{2,1,0:T(8,128)(2,1)} %get-tuple-element.29), calls=%async_computation.1 | async-start | bytes 6291456 | tf_op jit(solution)/shard_map/all_to_all | solution.py:454
  44.3 34.0 %shard_map.96 = (f32[2,4,2,512,128]{4,3,2,1,0:T(8,128)}, s32[2,4,512,1536]{3,2,1,0:T(8,128)}) custom-call(s32[1]{0:T(128)} %bitcast.1.hst_ref, bf16[32,80,256]{2,1,0:T(8,128)(2,1)} %all-to-all-done.grads_ref.codes_ref, bf16[32,80,256]{2,1,0:T(8,128)(2,1)} %all-to-all-done.grads_ref.codes_ref), custom_call_target="tpu_custom_call" | custom-call | flops 5000000000 | bytes 65536 | tf_op jit(solution)/shard_map/pallas_call | solution.py:273
  78.4 7.5 %all-to-all-done.1.grads_ref = bf16[32,192,256]{2,1,0:T(8,128)(2,1)} async-done(((bf16[32,192,256]{2,1,0:T(8,128)(2,1)}), bf16[32,192,256]{2,1,0:T(8,128)(2,1)}, u32[]{:S(2)}, u32[]{:S(2)}) %all-to-all-start.1) | async-done | bytes 3145760 | tf_op jit(solution)/shard_map/all_to_all | solution.py:454
  85.9 0.0 copy-start
  85.9 17.9 %shard_map.97 = (bf16[2,512,128]{2,1,0:T(8,128)(2,1)S(1)}, bf16[2,512,128]{2,1,0:T(8,128)(2,1)S(1)}, bf16[2,512,128]{2,1,0:T(8,128)(2,1)S(1)}, f32[2,512,128]{2,1,0:T(8,128)S(1)}) custom-call(s32[1]{0:T(128)} %bitcast.1.hst_ref, s32[2,4,512,1536]{3,2,1,0:T(8,128)} %get-tuple-element.28.counts_ref, bf16[32,192,256]{2,1,0:T(8,128)(2,1)} %all-to-all-done.1.grads_ref, ...), custom_call_target="tpu_custom_call" | custom-call | flops 1600000000 | bytes 65536 | tf_op jit(solution)/shard_map/pallas_call | solution.py:331
  103.9 1.6 %collective-permute-start = (bf16[2,512,128]{2,1,0:T(8,128)(2,1)S(1)}, bf16[2,512,128]{2,1,0:T(8,128)(2,1)S(1)}, u32[]{:S(2)}, u32[]{:S(2)}) collective-permute-start(bf16[2,512,128]{2,1,0:T(8,128)(2,1)S(1)} %get-tuple-element.33), channel_id=1, source_target_pairs={{0,32},{32,64},{64,96},{96,0},{1,33},{33,65},{65,97},{97,1},{2,34}... | collective-permute-start | bytes 786440 | tf_op jit(solution)/shard_map/ppermute | solution.py:473
  105.4 2.7 %collective-permute-start.1 = (bf16[2,512,128]{2,1,0:T(8,128)(2,1)S(1)}, bf16[2,512,128]{2,1,0:T(8,128)(2,1)S(1)}, u32[]{:S(2)}, u32[]{:S(2)}) collective-permute-start(bf16[2,512,128]{2,1,0:T(8,128)(2,1)S(1)} %get-tuple-element.34), channel_id=1, source_target_pairs={{0,64},{32,96},{64,0},{96,32},{1,65},{33,97},{65,1},{97,33},{2,66}... | collective-permute-start | bytes 786440 | tf_op jit(solution)/shard_map/ppermute | solution.py:473
  108.2 1.4 %collective-permute-start.2 = (bf16[2,512,128]{2,1,0:T(8,128)(2,1)S(1)}, bf16[2,512,128]{2,1,0:T(8,128)(2,1)S(1)}, u32[]{:S(2)}, u32[]{:S(2)}) collective-permute-start(bf16[2,512,128]{2,1,0:T(8,128)(2,1)S(1)} %get-tuple-element.35), channel_id=1, source_target_pairs={{0,96},{32,0},{64,32},{96,64},{1,97},{33,1},{65,33},{97,65},{2,98}... | collective-permute-start | bytes 786440 | tf_op jit(solution)/shard_map/ppermute | solution.py:473
  109.6 0.0 copy-done
  109.6 13.4 %shard_map.98 = (bf16[2,512,128]{2,1,0:T(8,128)(2,1)S(1)}, bf16[2,512,128]{2,1,0:T(8,128)(2,1)S(1)}, bf16[2,512,128]{2,1,0:T(8,128)(2,1)S(1)}) custom-call(s32[1]{0:T(128)} %bitcast.1.hst_ref, s32[2,4,512,1536]{3,2,1,0:T(8,128)} %get-tuple-element.28.counts_ref, bf16[32,192,256]{2,1,0:T(8,128)(2,1)} %all-to-all-done.1.grads_ref, ...), custom_call_target="tpu_custom_call" | custom-call | flops 1200000000 | bytes 65536 | tf_op jit(solution)/shard_map/pallas_call | solution.py:331
  123.0 0.9 collective-permute-start.3
  123.9 0.9 collective-permute-start.4
  124.7 0.0 collective-permute-done.rest_1_
  124.7 0.0 copy-start.1
  124.7 0.0 copy-start.2
  124.7 1.9 %collective-permute-start.5 = (bf16[2,512,128]{2,1,0:T(8,128)(2,1)S(1)}, bf16[2,512,128]{2,1,0:T(8,128)(2,1)S(1)}, u32[]{:S(2)}, u32[]{:S(2)}) collective-permute-start(bf16[2,512,128]{2,1,0:T(8,128)(2,1)S(1)} %get-tuple-element.41), channel_id=1, source_target_pairs={{0,96},{32,0},{64,32},{96,64},{1,97},{33,1},{65,33},{97,65},{2,98}... | collective-permute-start | bytes 786440 | tf_op jit(solution)/shard_map/ppermute | solution.py:473
  126.7 7.4 %shard_map.99.rest_4_ = f32[2,512,128]{2,1,0:T(8,128)S(1)} custom-call(s32[1]{0:T(128)} %bitcast.1.hst_ref, s32[2,4,512,1536]{3,2,1,0:T(8,128)} %get-tuple-element.28.counts_ref, bf16[32,192,256]{2,1,0:T(8,128)(2,1)} %all-to-all-done.1.grads_ref, f32[2,4,2,512,128]{4,3,2,1,0:T(8,128)S(1)} %copy-done), custom_call_target="tpu_custom_call" | custom-call | flops 400000000 | bytes 65536 | tf_op jit(solution)/shard_map/pallas_call | solution.py:331
  134.1 0.0 copy-start.4
  134.1 0.0 copy-start.5
  134.1 0.0 collective-permute-done.1.rest_2_
  134.1 0.0 collective-permute-done.2.rest_3_
  134.1 0.9 collective-permute-done.3.rest_5_
  135.0 0.0 collective-permute-done.4.rest_6_
  135.0 0.7 collective-permute-done.5.rest_7_
  135.7 0.0 copy-done.1
  135.7 0.0 copy-done.2
  135.7 1.9 %shard_map.100 = (f32[4,512,128]{2,1,0:T(8,128)}, f32[2,512]{1,0:T(2,128)S(1)}, bf16[2,512,128]{2,1,0:T(8,128)(2,1)S(1)}) custom-call(s32[1]{0:T(128)} %bitcast.core_ref, f32[4,512,128]{2,1,0:T(8,128)S(1)} %copy-done.1, f32[4,512]{1,0:T(4,128)S(1)} %copy-done.2, f32[2,512,128]{2,1,0:T(8,128)S(1)} %get-tuple-element.31.rest_0_, ...), custom_call_target="tpu_custom_call" | custom-call | flops 600000000 | bytes 65536 | tf_op jit(solution)/shard_map/pallas_call | solution.py:407
  137.6 0.0 collective-permute-start.6
  137.6 0.0 copy-done.4
  137.6 0.0 copy-done.5
  137.6 0.6 pad_maximum_fusion
  138.2 0.9 collective-permute-done.6.grads_ref
  139.1 1.6 %shard_map.101 = (f32[4,512,128]{2,1,0:T(8,128)}, f32[4,512]{1,0:T(4,128)}) custom-call(s32[1]{0:T(128)} %bitcast.core_ref, f32[4,512,128]{2,1,0:T(8,128)S(1)} %copy-done.1, f32[4,512]{1,0:T(4,128)S(1)} %copy-done.2, bf16[2,512,128]{2,1,0:T(8,128)(2,1)S(1)} %collective-permute-done.6.grads_ref, ...), custom_call_target="tpu_custom_call", output_to_operand_aliasing={{0}: (5, {})} | custom-call | flops 400000000 | bytes 65536 | tf_op jit(solution)/shard_map/pallas_call | solution.py:424
Async XLA Ops:
  2.7 15.9 %copy-start.3 = (bf16[256,2080]{0,1:T(8,128)(2,1)S(1)}, bf16[256,2080]{0,1:T(8,128)(2,1)}, u32[]{:S(2)}) copy-start(bf16[256,2080]{0,1:T(8,128)(2,1)} %param.10) | copy-start | bytes 3194884
  10.0 29.3 %all-to-all-start = ((bf16[32,80,256]{2,1,0:T(8,128)(2,1)}), bf16[32,80,256]{2,1,0:T(8,128)(2,1)}, u32[]{:S(2)}, u32[]{:S(2)}) async-start(bf16[32,80,256]{2,1,0:T(8,128)(2,1)} %get-tuple-element.27), calls=%async_computation | async-start | bytes 2621440 | tf_op jit(solution)/shard_map/all_to_all | solution.py:454
  39.3 46.6 %all-to-all-start.1 = ((bf16[32,192,256]{2,1,0:T(8,128)(2,1)}), bf16[32,192,256]{2,1,0:T(8,128)(2,1)}, u32[]{:S(2)}, u32[]{:S(2)}) async-start(bf16[32,192,256]{2,1,0:T(8,128)(2,1)} %get-tuple-element.29), calls=%async_computation.1 | async-start | bytes 6291456 | tf_op jit(solution)/shard_map/all_to_all | solution.py:454
  85.9 23.7 %copy-start = (f32[2,4,2,512,128]{4,3,2,1,0:T(8,128)S(1)}, f32[2,4,2,512,128]{4,3,2,1,0:T(8,128)}, u32[]{:S(2)}) copy-start(f32[2,4,2,512,128]{4,3,2,1,0:T(8,128)} %get-tuple-element.38.before_ref) | copy-start | bytes 12582916
  103.9 20.9 %collective-permute-start = (bf16[2,512,128]{2,1,0:T(8,128)(2,1)S(1)}, bf16[2,512,128]{2,1,0:T(8,128)(2,1)S(1)}, u32[]{:S(2)}, u32[]{:S(2)}) collective-permute-start(bf16[2,512,128]{2,1,0:T(8,128)(2,1)S(1)} %get-tuple-element.33), channel_id=1, source_target_pairs={{0,32},{32,64},{64,96},{96,0},{1,33},{33,65},{65,97},{97,1},{2,34}... | collective-permute-start | bytes 786440 | tf_op jit(solution)/shard_map/ppermute | solution.py:473
  105.4 28.7 %collective-permute-start.1 = (bf16[2,512,128]{2,1,0:T(8,128)(2,1)S(1)}, bf16[2,512,128]{2,1,0:T(8,128)(2,1)S(1)}, u32[]{:S(2)}, u32[]{:S(2)}) collective-permute-start(bf16[2,512,128]{2,1,0:T(8,128)(2,1)S(1)} %get-tuple-element.34), channel_id=1, source_target_pairs={{0,64},{32,96},{64,0},{96,32},{1,65},{33,97},{65,1},{97,33},{2,66}... | collective-permute-start | bytes 786440 | tf_op jit(solution)/shard_map/ppermute | solution.py:473
  108.2 26.0 %collective-permute-start.2 = (bf16[2,512,128]{2,1,0:T(8,128)(2,1)S(1)}, bf16[2,512,128]{2,1,0:T(8,128)(2,1)S(1)}, u32[]{:S(2)}, u32[]{:S(2)}) collective-permute-start(bf16[2,512,128]{2,1,0:T(8,128)(2,1)S(1)} %get-tuple-element.35), channel_id=1, source_target_pairs={{0,96},{32,0},{64,32},{96,64},{1,97},{33,1},{65,33},{97,65},{2,98}... | collective-permute-start | bytes 786440 | tf_op jit(solution)/shard_map/ppermute | solution.py:473
  123.0 12.0 %collective-permute-start.3 = (bf16[2,512,128]{2,1,0:T(8,128)(2,1)S(1)}, bf16[2,512,128]{2,1,0:T(8,128)(2,1)S(1)}, u32[]{:S(2)}, u32[]{:S(2)}) collective-permute-start(bf16[2,512,128]{2,1,0:T(8,128)(2,1)S(1)} %get-tuple-element.39), channel_id=1, source_target_pairs={{0,32},{32,64},{64,96},{96,0},{1,33},{33,65},{65,97},{97,1},{2,34}... | collective-permute-start | bytes 786440 | tf_op jit(solution)/shard_map/ppermute | solution.py:473
  123.9 11.2 %collective-permute-start.4 = (bf16[2,512,128]{2,1,0:T(8,128)(2,1)S(1)}, bf16[2,512,128]{2,1,0:T(8,128)(2,1)S(1)}, u32[]{:S(2)}, u32[]{:S(2)}) collective-permute-start(bf16[2,512,128]{2,1,0:T(8,128)(2,1)S(1)} %get-tuple-element.40), channel_id=1, source_target_pairs={{0,64},{32,96},{64,0},{96,32},{1,65},{33,97},{65,1},{97,33},{2,66}... | collective-permute-start | bytes 786440 | tf_op jit(solution)/shard_map/ppermute | solution.py:473
  124.7 10.9 %copy-start.1 = (f32[4,512,128]{2,1,0:T(8,128)S(1)}, f32[4,512,128]{2,1,0:T(8,128)}, u32[]{:S(2)}) copy-start(f32[4,512,128]{2,1,0:T(8,128)} %weights_ref.3) | copy-start | bytes 3145732
  124.7 10.9 %copy-start.2 = (f32[4,512]{1,0:T(4,128)S(1)}, f32[4,512]{1,0:T(4,128)}, u32[]{:S(2)}) copy-start(f32[4,512]{1,0:T(4,128)} %accum_ref.3) | copy-start | bytes 24580
  124.7 10.9 %collective-permute-start.5 = (bf16[2,512,128]{2,1,0:T(8,128)(2,1)S(1)}, bf16[2,512,128]{2,1,0:T(8,128)(2,1)S(1)}, u32[]{:S(2)}, u32[]{:S(2)}) collective-permute-start(bf16[2,512,128]{2,1,0:T(8,128)(2,1)S(1)} %get-tuple-element.41), channel_id=1, source_target_pairs={{0,96},{32,0},{64,32},{96,64},{1,97},{33,1},{65,33},{97,65},{2,98}... | collective-permute-start | bytes 786440 | tf_op jit(solution)/shard_map/ppermute | solution.py:473
  134.1 3.5 %copy-start.4 = (bf16[192,128]{1,0:T(8,128)(2,1)S(1)}, bf16[192,128]{1,0:T(8,128)(2,1)}, u32[]{:S(2)}) copy-start(bf16[192,128]{1,0:T(8,128)(2,1)} %get-tuple-element.26) | copy-start | bytes 147460
  134.1 3.5 %copy-start.5 = (bf16[64,128]{1,0:T(8,128)(2,1)S(1)}, bf16[64,128]{1,0:T(8,128)(2,1)}, u32[]{:S(2)}) copy-start(bf16[64,128]{1,0:T(8,128)(2,1)} %get-tuple-element.25) | copy-start | bytes 49156
  137.6 1.5 %collective-permute-start.6 = (bf16[2,512,128]{2,1,0:T(8,128)(2,1)S(1)}, bf16[2,512,128]{2,1,0:T(8,128)(2,1)S(1)}, u32[]{:S(2)}, u32[]{:S(2)}) collective-permute-start(bf16[2,512,128]{2,1,0:T(8,128)(2,1)S(1)} %get-tuple-element.42), channel_id=1, source_target_pairs={{0,16},{16,0},{1,17},{17,1},{2,18},{18,2},{3,19},{19,3},{4,20},{20... | collective-permute-start | bytes 786440 | tf_op jit(solution)/shard_map/ppermute | solution.py:423

commit v4 on v3

--- a/solution.py
+++ b/solution.py
@@ -231,7 +231,7 @@
         out_ref[start : start + STRIP, at : at + LANES] = out
 
 
-def early_kernel(late, hst_ref, grads_ref, codes_ref, total_ref, late_ref, counts_ref):
+def early_kernel(late, hst_ref, grads_ref, codes_ref, total_ref, late_ref, own_ref, counts_ref):
     @pl.when(pl.program_id(1) == 0)
     def _():
         total_ref[...] = jnp.zeros_like(total_ref)
@@ -262,6 +262,11 @@
         begin, end = (len(lanes) * n // fields for n in (field, field + 1))
         for at in lanes[begin:end]:
             count_column(word, total, at, late_ref.at[0, 0])
+            columns = slice(at, at + LANES)
+            for c in range(CORES):
+                field = CORES * here + lax.rem(core + c, CORES)
+                own = (late_ref[0, 0, :, columns] >> (FIELD * field)) & ((1 << FIELD) - 1)
+                own_ref[0, 0, c, :, columns] = own.astype(jnp.int8)
 
 
 def early_sums(hst, received, held, slots, words, early, late, chips):
@@ -282,12 +287,14 @@
             out_specs=[
                 pl.BlockSpec((1,) + totals, lambda t, g, hst: (t, 0, 0, 0, 0)),
                 pl.BlockSpec((1, 1, words, GROUP * late), lambda t, g, hst: (t, g, 0, 0)),
+                pl.BlockSpec((1, 1, CORES, words, GROUP * late), lambda t, g, hst: (t, g, 0, 0, 0)),
             ],
             scratch_shapes=[pltpu.VMEM((words, GROUP * early), jnp.int32)],
         ),
         out_shape=[
             jax.ShapeDtypeStruct((held,) + totals, F32),
             pltpu.HBM((held, groups, words, GROUP * late), jnp.int32),
+            pltpu.HBM((held, groups, CORES, words, GROUP * late), jnp.int8),
         ],
         compiler_params=params(FULL),
         cost_estimate=cost(25),
@@ -304,52 +311,54 @@
 def sum_kernel(ds, hst_ref, counts_ref, grads_ref, before_ref, *rest):
     outs, total = rest[:-1], rest[-1]
 
-    @pl.when(pl.program_id(0) == 0)
+    @pl.when(pl.program_id(1) == 0)
     def _():
         total[...] = before_ref[0]
 
     group, samples, _ = grads_ref.shape
     grads = grads_ref[...].reshape(group * samples, LANES)
-    counts = counts_ref[0, 0]
     for k, d in enumerate(ds):
         for c in range(CORES):
-            total[k, c] += jnp.dot(
-                picked(counts, hst_ref, d, c), grads, preferred_element_type=F32
-            )
-
-    @pl.when(pl.program_id(0) == pl.num_programs(0) - 1)
+            if d:
+                counts = picked(counts_ref[0, 0], hst_ref, d, c)
+            else:
+                counts = counts_ref[0, 0, c].astype(BF16)
+            total[k, c] += jnp.dot(counts, grads, preferred_element_type=F32)
+
+    @pl.when(pl.program_id(1) == pl.num_programs(1) - 1)
     def _():
         for k, out in enumerate(outs):
-            out[...] = total[k].astype(out.dtype)
-
-
-def row_sums(hst, counts, grads, before, ds, table):
-    _, groups, words, columns = counts.shape
+            out[0] = total[k].astype(out.dtype)
+
+
+def row_sums(hst, counts, grads, before, ds, first, tables):
+    groups, words, columns = counts.shape[1], counts.shape[-2], counts.shape[-1]
     group = grads.shape[0] // groups
     samples = columns // group
     at = (ds[0] - 1) % before.shape[1] // len(ds)
+    fixed = (0,) * (counts.ndim - 2)
     return pl.pallas_call(
         functools.partial(sum_kernel, ds),
         grid_spec=pltpu.PrefetchScalarGridSpec(
             num_scalar_prefetch=1,
-            grid=(groups,),
+            grid=(tables, groups),
             in_specs=[
-                pl.BlockSpec((1, 1, words, columns), lambda g, hst: (table, g, 0, 0)),
-                pl.BlockSpec((group, samples, LANES), lambda g, hst: (g, 0, table)),
+                pl.BlockSpec((1, 1) + counts.shape[2:], lambda t, g, hst: (first + t, g) + fixed),
+                pl.BlockSpec((group, samples, LANES), lambda t, g, hst: (g, 0, first + t)),
                 pl.BlockSpec(
-                    (1, len(ds), CORES, words, LANES), lambda g, hst: (table, at, 0, 0, 0)
+                    (1, len(ds), CORES, words, LANES), lambda t, g, hst: (first + t, at, 0, 0, 0)
                 ),
             ],
             out_specs=[
-                pl.BlockSpec((CORES, words, LANES), lambda g, hst: (0, 0, 0)) for d in ds
+                pl.BlockSpec((1, CORES, words, LANES), lambda t, g, hst: (t, 0, 0, 0)) for d in ds
             ],
             scratch_shapes=[pltpu.VMEM((len(ds), CORES, words, LANES), F32)],
         ),
         out_shape=[
-            jax.ShapeDtypeStruct((CORES, words, LANES), BF16 if d else F32) for d in ds
+            jax.ShapeDtypeStruct((tables, CORES, words, LANES), BF16 if d else F32) for d in ds
         ],
         compiler_params=params(),
-        cost_estimate=cost(2 * len(ds)),
+        cost_estimate=cost(0.1),
     )(hst, in_hbm(counts), in_hbm(grads), before)
 
 
@@ -369,9 +378,9 @@
     mine = core_ref[0] == 0
     rows = []
     for t in range(held):
-        total = piece_refs[t * pieces][...]
+        total = piece_refs[t * pieces][0]
         for piece_ref in piece_refs[t * pieces + 1 : (t + 1) * pieces]:
-            total = total + piece_ref[...].astype(F32)
+            total = total + piece_ref[0].astype(F32)
         send_ref[t] = total[1].astype(BF16)
         accum = jnp.where(mine, accum_ref[t : t + 1], accum_ref[held + t : held + t + 1])
         rows.append(adagrad(t, total[0], weights_ref, accum, new_weights_ref))
@@ -393,7 +402,7 @@
     )
 
 
-def update(core, weights, accum, pieces):
+def update(core, weights, accum, staying, pieces):
     tables, words, lanes = weights.shape
     held = tables // CORES
     part = 256
@@ -402,14 +411,20 @@
     moved = pl.BlockSpec((held, part, lanes), lambda q, core: (0, q, 0))
     row = pl.BlockSpec((tables, part), lambda q, core: (0, q))
     half = pl.BlockSpec((held, part), lambda q, core: (0, q))
-    piece = pl.BlockSpec((CORES, part, lanes), lambda q, core: (0, q, 0))
-    flat = [array for table in pieces for array in table]
+    flat, specs = [], []
+    for t in range(held):
+        for n, array in enumerate([staying] + pieces[t]):
+            flat.append(array)
+            place = 0 if n else t
+            specs.append(
+                pl.BlockSpec((1, CORES, part, lanes), lambda q, core, n=place: (n, 0, q, 0))
+            )
     new_weights, own_accum, send = pl.pallas_call(
-        functools.partial(own_kernel, len(pieces[0])),
+        functools.partial(own_kernel, 1 + len(pieces[0])),
         grid_spec=pltpu.PrefetchScalarGridSpec(
             num_scalar_prefetch=1,
             grid=(words // part,),
-            in_specs=[mine, row] + [piece] * len(flat),
+            in_specs=[mine, row] + specs,
             out_specs=[mine, half, moved],
         ),
         out_shape=[
@@ -459,21 +474,21 @@
     received = spread(send)
     late_dense, send = interact(dense_out, pooled, dense_cot, late_pairs, None, owners, EARLY)
     d_dense = jnp.concatenate([early_dense, late_dense], 0)
-    before, counts = early_sums(hst, received, held, slots, words, EARLY, late, chips)
+    before, counts, own = early_sums(hst, received, held, slots, words, EARLY, late, chips)
     received = spread(send)
     pieces = []
     for t in range(held):
-        everything = t < held - 1
         prior = before if t else in_hbm(before)
-        sums = list(row_sums(hst, counts, received, prior, AWAY + (0,) * everything, t))
+        sums = list(row_sums(hst, counts, received, prior, AWAY, t, 1))
         before, sums[0] = lax.optimization_barrier((before, sums[0]))
         moved = []
         for d in AWAY:
             ring = [(i, (i + d) % chips) for i in range(chips)]
             moved.append(lax.ppermute(sums[d - 1], "chip", ring))
-        pieces.append(sums[len(AWAY) :] + moved)
-    pieces[-1] = list(row_sums(hst, counts, received, before, (0,), held - 1)) + pieces[-1]
-    new_weights, new_accum = update(core.reshape(1), weights, accum, pieces)
+        pieces.append(moved)
+    before, pieces[0] = lax.optimization_barrier((before, pieces[0]))
+    (staying,) = row_sums(hst, own, received, before, (0,), 0, held)
+    new_weights, new_accum = update(core.reshape(1), weights, accum, staying, pieces)
     return d_dense, new_weights, new_accum
 
 

time: 142 us -> 140 us (0.986)
  waiting for transfers between devices: 13.3 us -> 4.91 us
  Pallas kernels: 98.9 us -> 105 us
    pallas_call x1, Pallas kernels: 34 us -> 40.9 us  [early_sums(): pl.pallas_call(functools.partial(early_kernel, late), grid_spec=pltpu.Pre...]
    all_to_all x2, waiting for transfers between devices: 10.9 us -> 4 us  [spread(): lax.all_to_all(x, ('wide', 'core'), split_axis=0, concat_axis=0, tiled=True)]
    ppermute x6, waiting for transfers between devices: 1.55 us -> 0.02 us  [local(): moved.append(lax.ppermute(sums[d - 1], 'chip', ring))]
  transfers between devices with their start and end apart: 9 -> 9, of which waited for: 5 -> 3; matrix products, arithmetic and copies ran while one was open for 2% -> 2% of each run, Pallas kernels for 50% -> 58%
where the time goes in v4:
time: 140 us; the launch traced here: 139 us
  Pallas kernels  105 us (75%)
  starting transfers between devices  22.9 us (16%)
  waiting for transfers between devices  4.91 us (4%)
  local copies, waits for them, and re-layouts  4.15 us (3%)
    pallas_call x1, Pallas kernels, early_sums(): pl.pallas_call(functools.partial(early_kernel, late), grid_spec=pltpu.Pre...  40.9 us
    pallas_call x3, Pallas kernels, row_sums(): pl.pallas_call(functools.partial(sum_kernel, ds), grid_spec=pltpu.Prefetc...  38.4 us
    pallas_call x2, Pallas kernels, interact(): pl.pallas_call(functools.partial(interact_kernel, steps, with_ids), grid=...  22.6 us
    all_to_all x2, starting transfers between devices, spread(): lax.all_to_all(x, ('wide', 'core'), split_axis=0, concat_axis=0, tiled=True)  13.5 us
    ppermute x6, starting transfers between devices, local(): moved.append(lax.ppermute(sums[d - 1], 'chip', ring))  9.35 us
    all_to_all x2, waiting for transfers between devices, spread(): lax.all_to_all(x, ('wide', 'core'), split_axis=0, concat_axis=0, tiled=True)  4 us
  transfers between devices with their start and end apart: 9, of which 3 were waited for; matrix products, arithmetic and copies ran while one was open for 2% of the time, Pallas kernels for 58%

profile of v4, /device:TPU:0, one launch (start us, length us, event | category | flops | bytes accessed | tf_op | source)
XLA Modules:
  0.0 138.8 jit_solution(13715720395557491359)
XLA Ops:
  0.6 1.1 slice.6
  1.7 0.9 copy.13.pair_ref
  2.7 0.0 copy-start.3
  2.7 7.3 %shard_map.94 = (bf16[64,128]{1,0:T(8,128)(2,1)}, bf16[32,80,256]{2,1,0:T(8,128)(2,1)}) custom-call(bf16[256,128]{1,0:T(8,128)(2,1)} %dense_ref.3, bf16[256,8192]{1,0:T(8,128)(2,1)} %pooled_ref.3, bf16[256,128]{1,0:T(8,128)(2,1)} %cot_ref.3, bf16[64,2080]{1,0:T(8,128)(2,1)} %copy.13.pair_ref, s32[64,8,256]{2,1,0:T(8,128)} %rest_0_.1), custom_call_target="tpu_custom_call" | custom-call | flops 1000000000 | bytes 65536 | tf_op jit(solution)/shard_map/pallas_call | solution.py:179
  10.0 8.5 %all-to-all-start = ((bf16[32,80,256]{2,1,0:T(8,128)(2,1)}), bf16[32,80,256]{2,1,0:T(8,128)(2,1)}, u32[]{:S(2)}, u32[]{:S(2)}) async-start(bf16[32,80,256]{2,1,0:T(8,128)(2,1)} %get-tuple-element.31), calls=%async_computation | async-start | bytes 2621440 | tf_op jit(solution)/shard_map/all_to_all | solution.py:469
  18.5 0.0 copy-done.3
  18.6 0.4 slice.7
  19.0 1.7 %copy.14.pair_ref = bf16[192,2080]{1,0:T(8,128)(2,1)} copy(bf16[192,2080]{0,1:T(8,128)(2,1)S(1)} %slice.7) | data formatting | bytes 1597440
  20.7 15.3 %shard_map.95 = (bf16[192,128]{1,0:T(8,128)(2,1)}, bf16[32,192,256]{2,1,0:T(8,128)(2,1)}) custom-call(bf16[256,128]{1,0:T(8,128)(2,1)} %dense_ref.3, bf16[256,8192]{1,0:T(8,128)(2,1)} %pooled_ref.3, bf16[256,128]{1,0:T(8,128)(2,1)} %cot_ref.3, bf16[192,2080]{1,0:T(8,128)(2,1)} %copy.14.pair_ref), custom_call_target="tpu_custom_call" | custom-call | flops 3000000000 | bytes 65536 | tf_op jit(solution)/shard_map/pallas_call | solution.py:179
  35.9 3.4 %all-to-all-done.grads_ref.codes_ref = bf16[32,80,256]{2,1,0:T(8,128)(2,1)} async-done(((bf16[32,80,256]{2,1,0:T(8,128)(2,1)}), bf16[32,80,256]{2,1,0:T(8,128)(2,1)}, u32[]{:S(2)}, u32[]{:S(2)}) %all-to-all-start) | async-done | bytes 1310752 | tf_op jit(solution)/shard_map/all_to_all | solution.py:469
  39.3 5.0 %all-to-all-start.1 = ((bf16[32,192,256]{2,1,0:T(8,128)(2,1)}), bf16[32,192,256]{2,1,0:T(8,128)(2,1)}, u32[]{:S(2)}, u32[]{:S(2)}) async-start(bf16[32,192,256]{2,1,0:T(8,128)(2,1)} %get-tuple-element.33), calls=%async_computation.1 | async-start | bytes 6291456 | tf_op jit(solution)/shard_map/all_to_all | solution.py:469
  44.3 40.9 %shard_map.96 = (f32[2,4,2,512,128]{4,3,2,1,0:T(8,128)}, s32[2,4,512,1536]{3,2,1,0:T(8,128)}, s8[2,4,2,512,1536]{4,3,2,1,0:T(32,128)(4,1)}) custom-call(s32[1]{0:T(128)} %bitcast.1.hst_ref, bf16[32,80,256]{2,1,0:T(8,128)(2,1)} %all-to-all-done.grads_ref.codes_ref, bf16[32,80,256]{2,1,0:T(8,128)(2,1)} %all-to-all-done.grads_ref.codes_ref), custom_call_target="tpu_custom_call" | custom-call | flops 5000000000 | bytes 65536 | tf_op jit(solution)/shard_map/pallas_call | solution.py:278
  85.3 0.6 all-to-all-done.1.grads_ref
  85.9 0.0 copy-start
  85.9 14.2 %shard_map.97 = (bf16[1,2,512,128]{3,2,1,0:T(8,128)(2,1)S(1)}, bf16[1,2,512,128]{3,2,1,0:T(8,128)(2,1)S(1)}, bf16[1,2,512,128]{3,2,1,0:T(8,128)(2,1)S(1)}) custom-call(s32[1]{0:T(128)} %bitcast.1.hst_ref, s32[2,4,512,1536]{3,2,1,0:T(8,128)} %get-tuple-element.35.counts_ref, bf16[32,192,256]{2,1,0:T(8,128)(2,1)} %all-to-all-done.1.grads_ref, ...), custom_call_target="tpu_custom_call" | custom-call | flops 20000000 | bytes 65536 | tf_op jit(solution)/shard_map/pallas_call | solution.py:340
  100.1 1.6 %collective-permute-start = (bf16[1,2,512,128]{3,2,1,0:T(8,128)(2,1)S(1)}, bf16[1,2,512,128]{3,2,1,0:T(8,128)(2,1)S(1)}, u32[]{:S(2)}, u32[]{:S(2)}) collective-permute-start(bf16[1,2,512,128]{3,2,1,0:T(8,128)(2,1)S(1)} %get-tuple-element.40), channel_id=1, source_target_pairs={{0,32},{32,64},{64,96},{96,0},{1,33},{33,65},{65,97},{97,1},{2,34}... | collective-permute-start | bytes 786440 | tf_op jit(solution)/shard_map/ppermute | solution.py:487
  101.6 2.7 %collective-permute-start.1 = (bf16[1,2,512,128]{3,2,1,0:T(8,128)(2,1)S(1)}, bf16[1,2,512,128]{3,2,1,0:T(8,128)(2,1)S(1)}, u32[]{:S(2)}, u32[]{:S(2)}) collective-permute-start(bf16[1,2,512,128]{3,2,1,0:T(8,128)(2,1)S(1)} %get-tuple-element.41), channel_id=1, source_target_pairs={{0,64},{32,96},{64,0},{96,32},{1,65},{33,97},{65,1},{97,33},{2,66}... | collective-permute-start | bytes 786440 | tf_op jit(solution)/shard_map/ppermute | solution.py:487
  104.4 1.4 %collective-permute-start.2 = (bf16[1,2,512,128]{3,2,1,0:T(8,128)(2,1)S(1)}, bf16[1,2,512,128]{3,2,1,0:T(8,128)(2,1)S(1)}, u32[]{:S(2)}, u32[]{:S(2)}) collective-permute-start(bf16[1,2,512,128]{3,2,1,0:T(8,128)(2,1)S(1)} %get-tuple-element.42), channel_id=1, source_target_pairs={{0,96},{32,0},{64,32},{96,64},{1,97},{33,1},{65,33},{97,65},{2,98}... | collective-permute-start | bytes 786440 | tf_op jit(solution)/shard_map/ppermute | solution.py:487
  105.8 0.0 copy-done
  105.8 12.8 %shard_map.98 = (bf16[1,2,512,128]{3,2,1,0:T(8,128)(2,1)S(1)}, bf16[1,2,512,128]{3,2,1,0:T(8,128)(2,1)S(1)}, bf16[1,2,512,128]{3,2,1,0:T(8,128)(2,1)S(1)}) custom-call(s32[1]{0:T(128)} %bitcast.1.hst_ref, s32[2,4,512,1536]{3,2,1,0:T(8,128)} %get-tuple-element.35.counts_ref, bf16[32,192,256]{2,1,0:T(8,128)(2,1)} %all-to-all-done.1.grads_ref, ...), custom_call_target="tpu_custom_call" | custom-call | flops 20000000 | bytes 65536 | tf_op jit(solution)/shard_map/pallas_call | solution.py:340
  118.6 0.9 collective-permute-start.3
  119.5 0.9 collective-permute-start.4
  120.4 0.0 collective-permute-done.rest_1_
  120.4 1.9 %collective-permute-start.5 = (bf16[1,2,512,128]{3,2,1,0:T(8,128)(2,1)S(1)}, bf16[1,2,512,128]{3,2,1,0:T(8,128)(2,1)S(1)}, u32[]{:S(2)}, u32[]{:S(2)}) collective-permute-start(bf16[1,2,512,128]{3,2,1,0:T(8,128)(2,1)S(1)} %get-tuple-element.49), channel_id=1, source_target_pairs={{0,96},{32,0},{64,32},{96,64},{1,97},{33,1},{65,33},{97,65},{2,98}... | collective-permute-start | bytes 786440 | tf_op jit(solution)/shard_map/ppermute | solution.py:487
  122.3 0.0 collective-permute-done.1.rest_2_
  122.3 0.0 collective-permute-done.2.rest_3_
  122.3 0.0 copy-start.1
  122.3 0.0 copy-start.2
  122.3 11.4 %shard_map.99.rest_0_.rest_4_ = f32[2,2,512,128]{3,2,1,0:T(8,128)S(1)} custom-call(s32[1]{0:T(128)} %bitcast.1.hst_ref, s8[2,4,2,512,1536]{4,3,2,1,0:T(32,128)(4,1)} %get-tuple-element.32.counts_ref, bf16[32,192,256]{2,1,0:T(8,128)(2,1)} %all-to-all-done.1.grads_ref, f32[2,4,2,512,128]{4,3,2,1,0:T(8,128)S(1)} %copy-done), custom_call_target="tpu_custom_call" | custom-call | flops 20000000 | bytes 65536 | tf_op jit(solution)/shard_map/pallas_call | solution.py:340
  133.7 0.0 copy-start.4
  133.7 0.0 copy-start.5
  133.7 0.0 collective-permute-done.3.rest_5_
  133.7 0.0 collective-permute-done.4.rest_6_
  133.7 0.0 collective-permute-done.5.rest_7_
  133.8 0.0 copy-done.1
  133.8 0.0 copy-done.2
  133.8 1.9 %shard_map.100 = (f32[4,512,128]{2,1,0:T(8,128)}, f32[2,512]{1,0:T(2,128)S(1)}, bf16[2,512,128]{2,1,0:T(8,128)(2,1)S(1)}) custom-call(s32[1]{0:T(128)} %bitcast.core_ref, f32[4,512,128]{2,1,0:T(8,128)S(1)} %copy-done.1, f32[4,512]{1,0:T(4,128)S(1)} %copy-done.2, f32[2,2,512,128]{3,2,1,0:T(8,128)S(1)} %shard_map.99.rest_0_.rest_4_, ...), custom_call_target="tpu_custom_call" | custom-call | flops 600000000 | bytes 65536 | tf_op jit(solution)/shard_map/pallas_call | solution.py:422
  135.7 0.0 collective-permute-start.6
  135.7 0.0 copy-done.4
  135.7 0.0 copy-done.5
  135.7 0.6 pad_maximum_fusion
  136.3 0.9 collective-permute-done.6.grads_ref
  137.2 1.6 %shard_map.101 = (f32[4,512,128]{2,1,0:T(8,128)}, f32[4,512]{1,0:T(4,128)}) custom-call(s32[1]{0:T(128)} %bitcast.core_ref, f32[4,512,128]{2,1,0:T(8,128)S(1)} %copy-done.1, f32[4,512]{1,0:T(4,128)S(1)} %copy-done.2, bf16[2,512,128]{2,1,0:T(8,128)(2,1)S(1)} %collective-permute-done.6.grads_ref, ...), custom_call_target="tpu_custom_call", output_to_operand_aliasing={{0}: (5, {})} | custom-call | flops 400000000 | bytes 65536 | tf_op jit(solution)/shard_map/pallas_call | solution.py:439
Async XLA Ops:
  2.7 15.9 %copy-start.3 = (bf16[256,2080]{0,1:T(8,128)(2,1)S(1)}, bf16[256,2080]{0,1:T(8,128)(2,1)}, u32[]{:S(2)}) copy-start(bf16[256,2080]{0,1:T(8,128)(2,1)} %param.10) | copy-start | bytes 3194884
  10.0 29.3 %all-to-all-start = ((bf16[32,80,256]{2,1,0:T(8,128)(2,1)}), bf16[32,80,256]{2,1,0:T(8,128)(2,1)}, u32[]{:S(2)}, u32[]{:S(2)}) async-start(bf16[32,80,256]{2,1,0:T(8,128)(2,1)} %get-tuple-element.31), calls=%async_computation | async-start | bytes 2621440 | tf_op jit(solution)/shard_map/all_to_all | solution.py:469
  39.3 46.6 %all-to-all-start.1 = ((bf16[32,192,256]{2,1,0:T(8,128)(2,1)}), bf16[32,192,256]{2,1,0:T(8,128)(2,1)}, u32[]{:S(2)}, u32[]{:S(2)}) async-start(bf16[32,192,256]{2,1,0:T(8,128)(2,1)} %get-tuple-element.33), calls=%async_computation.1 | async-start | bytes 6291456 | tf_op jit(solution)/shard_map/all_to_all | solution.py:469
  85.9 19.9 %copy-start = (f32[2,4,2,512,128]{4,3,2,1,0:T(8,128)S(1)}, f32[2,4,2,512,128]{4,3,2,1,0:T(8,128)}, u32[]{:S(2)}) copy-start(f32[2,4,2,512,128]{4,3,2,1,0:T(8,128)} %get-tuple-element.43.before_ref) | copy-start | bytes 12582916
  100.1 20.3 %collective-permute-start = (bf16[1,2,512,128]{3,2,1,0:T(8,128)(2,1)S(1)}, bf16[1,2,512,128]{3,2,1,0:T(8,128)(2,1)S(1)}, u32[]{:S(2)}, u32[]{:S(2)}) collective-permute-start(bf16[1,2,512,128]{3,2,1,0:T(8,128)(2,1)S(1)} %get-tuple-element.40), channel_id=1, source_target_pairs={{0,32},{32,64},{64,96},{96,0},{1,33},{33,65},{65,97},{97,1},{2,34}... | collective-permute-start | bytes 786440 | tf_op jit(solution)/shard_map/ppermute | solution.py:487
  101.6 20.6 %collective-permute-start.1 = (bf16[1,2,512,128]{3,2,1,0:T(8,128)(2,1)S(1)}, bf16[1,2,512,128]{3,2,1,0:T(8,128)(2,1)S(1)}, u32[]{:S(2)}, u32[]{:S(2)}) collective-permute-start(bf16[1,2,512,128]{3,2,1,0:T(8,128)(2,1)S(1)} %get-tuple-element.41), channel_id=1, source_target_pairs={{0,64},{32,96},{64,0},{96,32},{1,65},{33,97},{65,1},{97,33},{2,66}... | collective-permute-start | bytes 786440 | tf_op jit(solution)/shard_map/ppermute | solution.py:487
  104.4 17.9 %collective-permute-start.2 = (bf16[1,2,512,128]{3,2,1,0:T(8,128)(2,1)S(1)}, bf16[1,2,512,128]{3,2,1,0:T(8,128)(2,1)S(1)}, u32[]{:S(2)}, u32[]{:S(2)}) collective-permute-start(bf16[1,2,512,128]{3,2,1,0:T(8,128)(2,1)S(1)} %get-tuple-element.42), channel_id=1, source_target_pairs={{0,96},{32,0},{64,32},{96,64},{1,97},{33,1},{65,33},{97,65},{2,98}... | collective-permute-start | bytes 786440 | tf_op jit(solution)/shard_map/ppermute | solution.py:487
  118.6 15.1 %collective-permute-start.3 = (bf16[1,2,512,128]{3,2,1,0:T(8,128)(2,1)S(1)}, bf16[1,2,512,128]{3,2,1,0:T(8,128)(2,1)S(1)}, u32[]{:S(2)}, u32[]{:S(2)}) collective-permute-start(bf16[1,2,512,128]{3,2,1,0:T(8,128)(2,1)S(1)} %get-tuple-element.47), channel_id=1, source_target_pairs={{0,32},{32,64},{64,96},{96,0},{1,33},{33,65},{65,97},{97,1},{2,34}... | collective-permute-start | bytes 786440 | tf_op jit(solution)/shard_map/ppermute | solution.py:487
  119.5 14.2 %collective-permute-start.4 = (bf16[1,2,512,128]{3,2,1,0:T(8,128)(2,1)S(1)}, bf16[1,2,512,128]{3,2,1,0:T(8,128)(2,1)S(1)}, u32[]{:S(2)}, u32[]{:S(2)}) collective-permute-start(bf16[1,2,512,128]{3,2,1,0:T(8,128)(2,1)S(1)} %get-tuple-element.48), channel_id=1, source_target_pairs={{0,64},{32,96},{64,0},{96,32},{1,65},{33,97},{65,1},{97,33},{2,66}... | collective-permute-start | bytes 786440 | tf_op jit(solution)/shard_map/ppermute | solution.py:487
  120.4 13.3 %collective-permute-start.5 = (bf16[1,2,512,128]{3,2,1,0:T(8,128)(2,1)S(1)}, bf16[1,2,512,128]{3,2,1,0:T(8,128)(2,1)S(1)}, u32[]{:S(2)}, u32[]{:S(2)}) collective-permute-start(bf16[1,2,512,128]{3,2,1,0:T(8,128)(2,1)S(1)} %get-tuple-element.49), channel_id=1, source_target_pairs={{0,96},{32,0},{64,32},{96,64},{1,97},{33,1},{65,33},{97,65},{2,98}... | collective-permute-start | bytes 786440 | tf_op jit(solution)/shard_map/ppermute | solution.py:487
  122.3 11.5 %copy-start.1 = (f32[4,512,128]{2,1,0:T(8,128)S(1)}, f32[4,512,128]{2,1,0:T(8,128)}, u32[]{:S(2)}) copy-start(f32[4,512,128]{2,1,0:T(8,128)} %weights_ref.3) | copy-start | bytes 3145732
  122.3 11.5 %copy-start.2 = (f32[4,512]{1,0:T(4,128)S(1)}, f32[4,512]{1,0:T(4,128)}, u32[]{:S(2)}) copy-start(f32[4,512]{1,0:T(4,128)} %accum_ref.3) | copy-start | bytes 24580
  133.7 2.0 %copy-start.4 = (bf16[192,128]{1,0:T(8,128)(2,1)S(1)}, bf16[192,128]{1,0:T(8,128)(2,1)}, u32[]{:S(2)}) copy-start(bf16[192,128]{1,0:T(8,128)(2,1)} %get-tuple-element.30) | copy-start | bytes 147460
  133.7 2.0 %copy-start.5 = (bf16[64,128]{1,0:T(8,128)(2,1)S(1)}, bf16[64,128]{1,0:T(8,128)(2,1)}, u32[]{:S(2)}) copy-start(bf16[64,128]{1,0:T(8,128)(2,1)} %get-tuple-element.29) | copy-start | bytes 49156
  135.7 1.5 %collective-permute-start.6 = (bf16[2,512,128]{2,1,0:T(8,128)(2,1)S(1)}, bf16[2,512,128]{2,1,0:T(8,128)(2,1)S(1)}, u32[]{:S(2)}, u32[]{:S(2)}) collective-permute-start(bf16[2,512,128]{2,1,0:T(8,128)(2,1)S(1)} %get-tuple-element.50), channel_id=1, source_target_pairs={{0,16},{16,0},{1,17},{17,1},{2,18},{18,2},{3,19},{19,3},{4,20},{20... | collective-permute-start | bytes 786440 | tf_op jit(solution)/shard_map/ppermute | solution.py:438

commit v5 on v4

--- a/solution.py
+++ b/solution.py
@@ -73,9 +73,20 @@
         interact_block(dense_ref, pooled_ref, cot_ref, pair_ref, d_dense_ref, send_ref, *scratch)
         return
 
+    *scratch, turned = scratch
+    pairs = pair_ref.shape[0]
+
+    @pl.when(pl.program_id(0) == 0)
+    def _():
+        for at in range(0, pairs, LANES):
+            end = min(at + LANES, pairs)
+            turned[:, at:end] = pair_ref[at:end, :].astype(F32).T
+
     @pl.when(pl.program_id(0) < steps)
     def _():
-        interact_block(dense_ref, pooled_ref, cot_ref, pair_ref, d_dense_ref, send_ref, *scratch)
+        block = pl.ds(pl.multiple_of(pl.program_id(0) * BLOCK, BLOCK), BLOCK)
+        block_pairs = turned.at[block, 0:pairs]
+        interact_block(dense_ref, pooled_ref, cot_ref, block_pairs, d_dense_ref, send_ref, *scratch)
 
     @pl.when(pl.program_id(0) == steps)
     def _():
@@ -152,9 +163,9 @@
         send_ref[t // held, :, place : place + LANES] = grads[t + 1, 0:block].astype(BF16)
 
 
-def interact(dense_out, pooled, dense_cot, pair_cot, ids, owners, first):
+def interact(dense_out, pooled, dense_cot, pair_cot, ids, owners, first, samples):
     tables = pooled.shape[1] // LANES
-    samples, pairs = pair_cot.shape
+    pairs = pair_cot.shape[1 if ids is None else 0]
     held = tables // owners
     rows = (tables + 1 + 7) // 8 * 8
     padded = (pairs // LANES + 1) * LANES
@@ -172,7 +183,15 @@
         pl.BlockSpec((BLOCK, pairs), lambda s: (jnp.minimum(s, steps - 1), 0)),
     ]
     operands = [in_hbm(x) for x in (dense_out, pooled, dense_cot, pair_cot)]
+    scratch = [
+        pltpu.VMEM((BLOCK, padded), F32),
+        pltpu.VMEM((BLOCK // 2, rows, LANES), F32),
+        pltpu.VMEM((BLOCK, rows, LANES), F32),
+        pltpu.VMEM((rows, BLOCK + 8, LANES), F32),
+    ]
     if with_ids:
+        specs[-1] = pl.BlockSpec((pairs, LANES), lambda s: (0, 0))
+        scratch.append(pltpu.VMEM((LANES, padded), F32))
         specs.append(pl.BlockSpec(ids.shape, lambda s: (0, 0, 0)))
         operands.append(in_hbm(ids))
     extra = 1 if with_ids else 0
@@ -188,12 +207,7 @@
             jax.ShapeDtypeStruct((samples, LANES), BF16),
             pltpu.HBM((owners, samples + extra * held * slots, held * LANES), BF16),
         ],
-        scratch_shapes=[
-            pltpu.VMEM((BLOCK, padded), F32),
-            pltpu.VMEM((BLOCK // 2, rows, LANES), F32),
-            pltpu.VMEM((BLOCK, rows, LANES), F32),
-            pltpu.VMEM((rows, BLOCK + 8, LANES), F32),
-        ],
+        scratch_shapes=scratch,
         compiler_params=params(FULL),
         cost_estimate=cost(20 * samples / 256),
     )(*operands)
@@ -469,10 +483,10 @@
         return lax.all_to_all(x, ("wide", "core"), split_axis=0, concat_axis=0, tiled=True)
 
     late = samples - EARLY
-    early_pairs, late_pairs = pair_cot[:EARLY], pair_cot[EARLY:]
-    early_dense, send = interact(dense_out, pooled, dense_cot, early_pairs, bag_ids, owners, 0)
+    shared = (dense_out, pooled, dense_cot)
+    early_dense, send = interact(*shared, pair_cot.T, bag_ids, owners, 0, EARLY)
     received = spread(send)
-    late_dense, send = interact(dense_out, pooled, dense_cot, late_pairs, None, owners, EARLY)
+    late_dense, send = interact(*shared, pair_cot[EARLY:], None, owners, EARLY, late)
     d_dense = jnp.concatenate([early_dense, late_dense], 0)
     before, counts, own = early_sums(hst, received, held, slots, words, EARLY, late, chips)
     received = spread(send)

time: 140 us -> 139 us (level)
  local copies, waits for them, and re-layouts: 4.15 us -> 2.13 us
  transfers between devices with their start and end apart: 9 -> 9, of which waited for: 3 -> 3; matrix products, arithmetic and copies ran while one was open for 2% -> 2% of each run, Pallas kernels for 58% -> 59%
where the time goes in v5:
time: 139 us; the launch traced here: 137 us
  Pallas kernels  106 us (76%)
  starting transfers between devices  22.9 us (16%)
  waiting for transfers between devices  4.91 us (4%)
  local copies, waits for them, and re-layouts  2.13 us (2%)
    pallas_call x1, Pallas kernels, early_sums(): pl.pallas_call(functools.partial(early_kernel, late), grid_spec=pltpu.Pre...  40.9 us
    pallas_call x3, Pallas kernels, row_sums(): pl.pallas_call(functools.partial(sum_kernel, ds), grid_spec=pltpu.Prefetc...  38.4 us
    pallas_call x2, Pallas kernels, interact(): pl.pallas_call(functools.partial(interact_kernel, steps, with_ids), grid=...  22.9 us
    all_to_all x2, starting transfers between devices, spread(): lax.all_to_all(x, ('wide', 'core'), split_axis=0, concat_axis=0, tiled=True)  13.5 us
    ppermute x6, starting transfers between devices, local(): moved.append(lax.ppermute(sums[d - 1], 'chip', ring))  9.38 us
    all_to_all x2, waiting for transfers between devices, spread(): lax.all_to_all(x, ('wide', 'core'), split_axis=0, concat_axis=0, tiled=True)  4.01 us
  transfers between devices with their start and end apart: 9, of which 3 were waited for; matrix products, arithmetic and copies ran while one was open for 2% of the time, Pallas kernels for 59%

profile of v5, /device:TPU:0, one launch (start us, length us, event | category | flops | bytes accessed | tf_op | source)
XLA Modules:
  0.0 137.1 jit_solution(17126154076335309416)
XLA Ops:
  0.6 0.0 copy-start.3
  0.6 7.6 %shard_map.94 = (bf16[64,128]{1,0:T(8,128)(2,1)}, bf16[32,80,256]{2,1,0:T(8,128)(2,1)}) custom-call(bf16[256,128]{1,0:T(8,128)(2,1)} %dense_ref.3, bf16[256,8192]{1,0:T(8,128)(2,1)} %pooled_ref.3, bf16[256,128]{1,0:T(8,128)(2,1)} %cot_ref.3, bf16[2080,256]{1,0:T(8,128)(2,1)} %bitcast.3, s32[64,8,256]{2,1,0:T(8,128)} %rest_0_.1), custom_call_target="tpu_custom_call" | custom-call | flops 1000000000 | bytes 65536 | tf_op jit(solution)/shard_map/pallas_call | solution.py:198
  8.2 8.5 %all-to-all-start = ((bf16[32,80,256]{2,1,0:T(8,128)(2,1)}), bf16[32,80,256]{2,1,0:T(8,128)(2,1)}, u32[]{:S(2)}, u32[]{:S(2)}) async-start(bf16[32,80,256]{2,1,0:T(8,128)(2,1)} %get-tuple-element.31), calls=%async_computation | async-start | bytes 2621440 | tf_op jit(solution)/shard_map/all_to_all | solution.py:483
  16.8 0.0 copy-done.3
  16.8 0.4 slice.3
  17.2 1.7 %copy.12.pair_ref = bf16[192,2080]{1,0:T(8,128)(2,1)} copy(bf16[192,2080]{0,1:T(8,128)(2,1)S(1)} %slice.3) | data formatting | bytes 1597440
  18.9 15.3 %shard_map.95 = (bf16[192,128]{1,0:T(8,128)(2,1)}, bf16[32,192,256]{2,1,0:T(8,128)(2,1)}) custom-call(bf16[256,128]{1,0:T(8,128)(2,1)} %dense_ref.3, bf16[256,8192]{1,0:T(8,128)(2,1)} %pooled_ref.3, bf16[256,128]{1,0:T(8,128)(2,1)} %cot_ref.3, bf16[192,2080]{1,0:T(8,128)(2,1)} %copy.12.pair_ref), custom_call_target="tpu_custom_call" | custom-call | flops 3000000000 | bytes 65536 | tf_op jit(solution)/shard_map/pallas_call | solution.py:198
  34.2 3.4 %all-to-all-done.grads_ref.codes_ref = bf16[32,80,256]{2,1,0:T(8,128)(2,1)} async-done(((bf16[32,80,256]{2,1,0:T(8,128)(2,1)}), bf16[32,80,256]{2,1,0:T(8,128)(2,1)}, u32[]{:S(2)}, u32[]{:S(2)}) %all-to-all-start) | async-done | bytes 1310752 | tf_op jit(solution)/shard_map/all_to_all | solution.py:483
  37.6 5.0 %all-to-all-start.1 = ((bf16[32,192,256]{2,1,0:T(8,128)(2,1)}), bf16[32,192,256]{2,1,0:T(8,128)(2,1)}, u32[]{:S(2)}, u32[]{:S(2)}) async-start(bf16[32,192,256]{2,1,0:T(8,128)(2,1)} %get-tuple-element.33), calls=%async_computation.1 | async-start | bytes 6291456 | tf_op jit(solution)/shard_map/all_to_all | solution.py:483
  42.6 40.9 %shard_map.96 = (f32[2,4,2,512,128]{4,3,2,1,0:T(8,128)}, s32[2,4,512,1536]{3,2,1,0:T(8,128)}, s8[2,4,2,512,1536]{4,3,2,1,0:T(32,128)(4,1)}) custom-call(s32[1]{0:T(128)} %bitcast.2.hst_ref, bf16[32,80,256]{2,1,0:T(8,128)(2,1)} %all-to-all-done.grads_ref.codes_ref, bf16[32,80,256]{2,1,0:T(8,128)(2,1)} %all-to-all-done.grads_ref.codes_ref), custom_call_target="tpu_custom_call" | custom-call | flops 5000000000 | bytes 65536 | tf_op jit(solution)/shard_map/pallas_call | solution.py:292
  83.5 0.6 all-to-all-done.1.grads_ref
  84.2 0.0 copy-start
  84.2 14.2 %shard_map.97 = (bf16[1,2,512,128]{3,2,1,0:T(8,128)(2,1)S(1)}, bf16[1,2,512,128]{3,2,1,0:T(8,128)(2,1)S(1)}, bf16[1,2,512,128]{3,2,1,0:T(8,128)(2,1)S(1)}) custom-call(s32[1]{0:T(128)} %bitcast.2.hst_ref, s32[2,4,512,1536]{3,2,1,0:T(8,128)} %get-tuple-element.35.counts_ref, bf16[32,192,256]{2,1,0:T(8,128)(2,1)} %all-to-all-done.1.grads_ref, ...), custom_call_target="tpu_custom_call" | custom-call | flops 20000000 | bytes 65536 | tf_op jit(solution)/shard_map/pallas_call | solution.py:354
  98.3 1.6 %collective-permute-start = (bf16[1,2,512,128]{3,2,1,0:T(8,128)(2,1)S(1)}, bf16[1,2,512,128]{3,2,1,0:T(8,128)(2,1)S(1)}, u32[]{:S(2)}, u32[]{:S(2)}) collective-permute-start(bf16[1,2,512,128]{3,2,1,0:T(8,128)(2,1)S(1)} %get-tuple-element.40), channel_id=1, source_target_pairs={{0,32},{32,64},{64,96},{96,0},{1,33},{33,65},{65,97},{97,1},{2,34}... | collective-permute-start | bytes 786440 | tf_op jit(solution)/shard_map/ppermute | solution.py:501
  99.9 2.7 %collective-permute-start.1 = (bf16[1,2,512,128]{3,2,1,0:T(8,128)(2,1)S(1)}, bf16[1,2,512,128]{3,2,1,0:T(8,128)(2,1)S(1)}, u32[]{:S(2)}, u32[]{:S(2)}) collective-permute-start(bf16[1,2,512,128]{3,2,1,0:T(8,128)(2,1)S(1)} %get-tuple-element.41), channel_id=1, source_target_pairs={{0,64},{32,96},{64,0},{96,32},{1,65},{33,97},{65,1},{97,33},{2,66}... | collective-permute-start | bytes 786440 | tf_op jit(solution)/shard_map/ppermute | solution.py:501
  102.6 1.4 %collective-permute-start.2 = (bf16[1,2,512,128]{3,2,1,0:T(8,128)(2,1)S(1)}, bf16[1,2,512,128]{3,2,1,0:T(8,128)(2,1)S(1)}, u32[]{:S(2)}, u32[]{:S(2)}) collective-permute-start(bf16[1,2,512,128]{3,2,1,0:T(8,128)(2,1)S(1)} %get-tuple-element.42), channel_id=1, source_target_pairs={{0,96},{32,0},{64,32},{96,64},{1,97},{33,1},{65,33},{97,65},{2,98}... | collective-permute-start | bytes 786440 | tf_op jit(solution)/shard_map/ppermute | solution.py:501
  104.0 0.0 copy-done
  104.0 12.8 %shard_map.98 = (bf16[1,2,512,128]{3,2,1,0:T(8,128)(2,1)S(1)}, bf16[1,2,512,128]{3,2,1,0:T(8,128)(2,1)S(1)}, bf16[1,2,512,128]{3,2,1,0:T(8,128)(2,1)S(1)}) custom-call(s32[1]{0:T(128)} %bitcast.2.hst_ref, s32[2,4,512,1536]{3,2,1,0:T(8,128)} %get-tuple-element.35.counts_ref, bf16[32,192,256]{2,1,0:T(8,128)(2,1)} %all-to-all-done.1.grads_ref, ...), custom_call_target="tpu_custom_call" | custom-call | flops 20000000 | bytes 65536 | tf_op jit(solution)/shard_map/pallas_call | solution.py:354
  116.9 0.9 collective-permute-start.3
  117.7 0.9 collective-permute-start.4
  118.6 0.0 collective-permute-done.rest_1_
  118.6 1.9 %collective-permute-start.5 = (bf16[1,2,512,128]{3,2,1,0:T(8,128)(2,1)S(1)}, bf16[1,2,512,128]{3,2,1,0:T(8,128)(2,1)S(1)}, u32[]{:S(2)}, u32[]{:S(2)}) collective-permute-start(bf16[1,2,512,128]{3,2,1,0:T(8,128)(2,1)S(1)} %get-tuple-element.49), channel_id=1, source_target_pairs={{0,96},{32,0},{64,32},{96,64},{1,97},{33,1},{65,33},{97,65},{2,98}... | collective-permute-start | bytes 786440 | tf_op jit(solution)/shard_map/ppermute | solution.py:501
  120.5 0.0 collective-permute-done.1.rest_2_
  120.5 0.0 collective-permute-done.2.rest_3_
  120.5 0.0 copy-start.1
  120.5 0.0 copy-start.2
  120.5 11.4 %shard_map.99.rest_0_.rest_4_ = f32[2,2,512,128]{3,2,1,0:T(8,128)S(1)} custom-call(s32[1]{0:T(128)} %bitcast.2.hst_ref, s8[2,4,2,512,1536]{4,3,2,1,0:T(32,128)(4,1)} %get-tuple-element.32.counts_ref, bf16[32,192,256]{2,1,0:T(8,128)(2,1)} %all-to-all-done.1.grads_ref, f32[2,4,2,512,128]{4,3,2,1,0:T(8,128)S(1)} %copy-done), custom_call_target="tpu_custom_call" | custom-call | flops 20000000 | bytes 65536 | tf_op jit(solution)/shard_map/pallas_call | solution.py:354
  132.0 0.0 copy-start.4
  132.0 0.0 copy-start.5
  132.0 0.0 collective-permute-done.3.rest_5_
  132.0 0.0 collective-permute-done.4.rest_6_
  132.0 0.0 collective-permute-done.5.rest_7_
  132.0 0.0 copy-done.1
  132.0 0.0 copy-done.2
  132.0 1.9 %shard_map.100 = (f32[4,512,128]{2,1,0:T(8,128)}, f32[2,512]{1,0:T(2,128)S(1)}, bf16[2,512,128]{2,1,0:T(8,128)(2,1)S(1)}) custom-call(s32[1]{0:T(128)} %bitcast.1.core_ref, f32[4,512,128]{2,1,0:T(8,128)S(1)} %copy-done.1, f32[4,512]{1,0:T(4,128)S(1)} %copy-done.2, f32[2,2,512,128]{3,2,1,0:T(8,128)S(1)} %shard_map.99.rest_0_.rest_4_, ...), custom_call_target="tpu_custom_call" | custom-call | flops 600000000 | bytes 65536 | tf_op jit(solution)/shard_map/pallas_call | solution.py:436
  133.9 0.0 collective-permute-start.6
  133.9 0.0 copy-done.4
  133.9 0.0 copy-done.5
  134.0 0.6 pad_maximum_fusion
  134.6 0.9 collective-permute-done.6.grads_ref
  135.5 1.6 %shard_map.101 = (f32[4,512,128]{2,1,0:T(8,128)}, f32[4,512]{1,0:T(4,128)}) custom-call(s32[1]{0:T(128)} %bitcast.1.core_ref, f32[4,512,128]{2,1,0:T(8,128)S(1)} %copy-done.1, f32[4,512]{1,0:T(4,128)S(1)} %copy-done.2, bf16[2,512,128]{2,1,0:T(8,128)(2,1)S(1)} %collective-permute-done.6.grads_ref, ...), custom_call_target="tpu_custom_call", output_to_operand_aliasing={{0}: (5, {})} | custom-call | flops 400000000 | bytes 65536 | tf_op jit(solution)/shard_map/pallas_call | solution.py:453
Async XLA Ops:
  0.6 16.2 %copy-start.3 = (bf16[256,2080]{0,1:T(8,128)(2,1)S(1)}, bf16[256,2080]{0,1:T(8,128)(2,1)}, u32[]{:S(2)}) copy-start(bf16[256,2080]{0,1:T(8,128)(2,1)} %param.10) | copy-start | bytes 3194884
  8.2 29.3 %all-to-all-start = ((bf16[32,80,256]{2,1,0:T(8,128)(2,1)}), bf16[32,80,256]{2,1,0:T(8,128)(2,1)}, u32[]{:S(2)}, u32[]{:S(2)}) async-start(bf16[32,80,256]{2,1,0:T(8,128)(2,1)} %get-tuple-element.31), calls=%async_computation | async-start | bytes 2621440 | tf_op jit(solution)/shard_map/all_to_all | solution.py:483
  37.6 46.6 %all-to-all-start.1 = ((bf16[32,192,256]{2,1,0:T(8,128)(2,1)}), bf16[32,192,256]{2,1,0:T(8,128)(2,1)}, u32[]{:S(2)}, u32[]{:S(2)}) async-start(bf16[32,192,256]{2,1,0:T(8,128)(2,1)} %get-tuple-element.33), calls=%async_computation.1 | async-start | bytes 6291456 | tf_op jit(solution)/shard_map/all_to_all | solution.py:483
  84.2 19.9 %copy-start = (f32[2,4,2,512,128]{4,3,2,1,0:T(8,128)S(1)}, f32[2,4,2,512,128]{4,3,2,1,0:T(8,128)}, u32[]{:S(2)}) copy-start(f32[2,4,2,512,128]{4,3,2,1,0:T(8,128)} %get-tuple-element.43.before_ref) | copy-start | bytes 12582916
  98.3 20.3 %collective-permute-start = (bf16[1,2,512,128]{3,2,1,0:T(8,128)(2,1)S(1)}, bf16[1,2,512,128]{3,2,1,0:T(8,128)(2,1)S(1)}, u32[]{:S(2)}, u32[]{:S(2)}) collective-permute-start(bf16[1,2,512,128]{3,2,1,0:T(8,128)(2,1)S(1)} %get-tuple-element.40), channel_id=1, source_target_pairs={{0,32},{32,64},{64,96},{96,0},{1,33},{33,65},{65,97},{97,1},{2,34}... | collective-permute-start | bytes 786440 | tf_op jit(solution)/shard_map/ppermute | solution.py:501
  99.9 20.6 %collective-permute-start.1 = (bf16[1,2,512,128]{3,2,1,0:T(8,128)(2,1)S(1)}, bf16[1,2,512,128]{3,2,1,0:T(8,128)(2,1)S(1)}, u32[]{:S(2)}, u32[]{:S(2)}) collective-permute-start(bf16[1,2,512,128]{3,2,1,0:T(8,128)(2,1)S(1)} %get-tuple-element.41), channel_id=1, source_target_pairs={{0,64},{32,96},{64,0},{96,32},{1,65},{33,97},{65,1},{97,33},{2,66}... | collective-permute-start | bytes 786440 | tf_op jit(solution)/shard_map/ppermute | solution.py:501
  102.6 17.9 %collective-permute-start.2 = (bf16[1,2,512,128]{3,2,1,0:T(8,128)(2,1)S(1)}, bf16[1,2,512,128]{3,2,1,0:T(8,128)(2,1)S(1)}, u32[]{:S(2)}, u32[]{:S(2)}) collective-permute-start(bf16[1,2,512,128]{3,2,1,0:T(8,128)(2,1)S(1)} %get-tuple-element.42), channel_id=1, source_target_pairs={{0,96},{32,0},{64,32},{96,64},{1,97},{33,1},{65,33},{97,65},{2,98}... | collective-permute-start | bytes 786440 | tf_op jit(solution)/shard_map/ppermute | solution.py:501
  116.9 15.1 %collective-permute-start.3 = (bf16[1,2,512,128]{3,2,1,0:T(8,128)(2,1)S(1)}, bf16[1,2,512,128]{3,2,1,0:T(8,128)(2,1)S(1)}, u32[]{:S(2)}, u32[]{:S(2)}) collective-permute-start(bf16[1,2,512,128]{3,2,1,0:T(8,128)(2,1)S(1)} %get-tuple-element.47), channel_id=1, source_target_pairs={{0,32},{32,64},{64,96},{96,0},{1,33},{33,65},{65,97},{97,1},{2,34}... | collective-permute-start | bytes 786440 | tf_op jit(solution)/shard_map/ppermute | solution.py:501
  117.7 14.2 %collective-permute-start.4 = (bf16[1,2,512,128]{3,2,1,0:T(8,128)(2,1)S(1)}, bf16[1,2,512,128]{3,2,1,0:T(8,128)(2,1)S(1)}, u32[]{:S(2)}, u32[]{:S(2)}) collective-permute-start(bf16[1,2,512,128]{3,2,1,0:T(8,128)(2,1)S(1)} %get-tuple-element.48), channel_id=1, source_target_pairs={{0,64},{32,96},{64,0},{96,32},{1,65},{33,97},{65,1},{97,33},{2,66}... | collective-permute-start | bytes 786440 | tf_op jit(solution)/shard_map/ppermute | solution.py:501
  118.6 13.4 %collective-permute-start.5 = (bf16[1,2,512,128]{3,2,1,0:T(8,128)(2,1)S(1)}, bf16[1,2,512,128]{3,2,1,0:T(8,128)(2,1)S(1)}, u32[]{:S(2)}, u32[]{:S(2)}) collective-permute-start(bf16[1,2,512,128]{3,2,1,0:T(8,128)(2,1)S(1)} %get-tuple-element.49), channel_id=1, source_target_pairs={{0,96},{32,0},{64,32},{96,64},{1,97},{33,1},{65,33},{97,65},{2,98}... | collective-permute-start | bytes 786440 | tf_op jit(solution)/shard_map/ppermute | solution.py:501
  120.5 11.5 %copy-start.1 = (f32[4,512,128]{2,1,0:T(8,128)S(1)}, f32[4,512,128]{2,1,0:T(8,128)}, u32[]{:S(2)}) copy-start(f32[4,512,128]{2,1,0:T(8,128)} %weights_ref.3) | copy-start | bytes 3145732
  120.5 11.5 %copy-start.2 = (f32[4,512]{1,0:T(4,128)S(1)}, f32[4,512]{1,0:T(4,128)}, u32[]{:S(2)}) copy-start(f32[4,512]{1,0:T(4,128)} %accum_ref.3) | copy-start | bytes 24580
  132.0 2.0 %copy-start.4 = (bf16[192,128]{1,0:T(8,128)(2,1)S(1)}, bf16[192,128]{1,0:T(8,128)(2,1)}, u32[]{:S(2)}) copy-start(bf16[192,128]{1,0:T(8,128)(2,1)} %get-tuple-element.30) | copy-start | bytes 147460
  132.0 2.0 %copy-start.5 = (bf16[64,128]{1,0:T(8,128)(2,1)S(1)}, bf16[64,128]{1,0:T(8,128)(2,1)}, u32[]{:S(2)}) copy-start(bf16[64,128]{1,0:T(8,128)(2,1)} %get-tuple-element.29) | copy-start | bytes 49156
  133.9 1.5 %collective-permute-start.6 = (bf16[2,512,128]{2,1,0:T(8,128)(2,1)S(1)}, bf16[2,512,128]{2,1,0:T(8,128)(2,1)S(1)}, u32[]{:S(2)}, u32[]{:S(2)}) collective-permute-start(bf16[2,512,128]{2,1,0:T(8,128)(2,1)S(1)} %get-tuple-element.50), channel_id=1, source_target_pairs={{0,16},{16,0},{1,17},{17,1},{2,18},{18,2},{3,19},{19,3},{4,20},{20... | collective-permute-start | bytes 786440 | tf_op jit(solution)/shard_map/ppermute | solution.py:452

commit v6 on v5

--- a/solution.py
+++ b/solution.py
@@ -419,7 +419,7 @@
 def update(core, weights, accum, staying, pieces):
     tables, words, lanes = weights.shape
     held = tables // CORES
-    part = 256
+    part = 512
     mine = pl.BlockSpec((held, part, lanes), lambda q, core: (core[0], q, 0))
     others = pl.BlockSpec((held, part, lanes), lambda q, core: (1 - core[0], q, 0))
     moved = pl.BlockSpec((held, part, lanes), lambda q, core: (0, q, 0))

time: 139 us -> 138 us (level)
  no operation moved by 1% of the time
where the time goes in v6:
time: 138 us; the launch traced here: 136 us
  Pallas kernels  105 us (76%)
  starting transfers between devices  22.9 us (17%)
  waiting for transfers between devices  4.91 us (4%)
  local copies, waits for them, and re-layouts  2.13 us (2%)
    pallas_call x1, Pallas kernels, early_sums(): pl.pallas_call(functools.partial(early_kernel, late), grid_spec=pltpu.Pre...  40.9 us
    pallas_call x3, Pallas kernels, row_sums(): pl.pallas_call(functools.partial(sum_kernel, ds), grid_spec=pltpu.Prefetc...  38.4 us
    pallas_call x2, Pallas kernels, interact(): pl.pallas_call(functools.partial(interact_kernel, steps, with_ids), grid=...  22.9 us
    all_to_all x2, starting transfers between devices, spread(): lax.all_to_all(x, ('wide', 'core'), split_axis=0, concat_axis=0, tiled=True)  13.5 us
    ppermute x6, starting transfers between devices, local(): moved.append(lax.ppermute(sums[d - 1], 'chip', ring))  9.38 us
    all_to_all x2, waiting for transfers between devices, spread(): lax.all_to_all(x, ('wide', 'core'), split_axis=0, concat_axis=0, tiled=True)  4.01 us
  transfers between devices with their start and end apart: 9, of which 3 were waited for; matrix products, arithmetic and copies ran while one was open for 2% of the time, Pallas kernels for 59%

profile of v6, /device:TPU:0, one launch (start us, length us, event | category | flops | bytes accessed | tf_op | source)
XLA Modules:
  0.0 136.3 jit_solution(17893183347199307469)
XLA Ops:
  0.6 0.0 copy-start.3
  0.6 7.6 %shard_map.94 = (bf16[64,128]{1,0:T(8,128)(2,1)}, bf16[32,80,256]{2,1,0:T(8,128)(2,1)}) custom-call(bf16[256,128]{1,0:T(8,128)(2,1)} %dense_ref.3, bf16[256,8192]{1,0:T(8,128)(2,1)} %pooled_ref.3, bf16[256,128]{1,0:T(8,128)(2,1)} %cot_ref.3, bf16[2080,256]{1,0:T(8,128)(2,1)} %bitcast.3, s32[64,8,256]{2,1,0:T(8,128)} %rest_0_.1), custom_call_target="tpu_custom_call" | custom-call | flops 1000000000 | bytes 65536 | tf_op jit(solution)/shard_map/pallas_call | solution.py:198
  8.2 8.5 %all-to-all-start = ((bf16[32,80,256]{2,1,0:T(8,128)(2,1)}), bf16[32,80,256]{2,1,0:T(8,128)(2,1)}, u32[]{:S(2)}, u32[]{:S(2)}) async-start(bf16[32,80,256]{2,1,0:T(8,128)(2,1)} %get-tuple-element.31), calls=%async_computation | async-start | bytes 2621440 | tf_op jit(solution)/shard_map/all_to_all | solution.py:483
  16.8 0.0 copy-done.3
  16.8 0.4 slice.3
  17.2 1.7 %copy.12.pair_ref = bf16[192,2080]{1,0:T(8,128)(2,1)} copy(bf16[192,2080]{0,1:T(8,128)(2,1)S(1)} %slice.3) | data formatting | bytes 1597440
  18.9 15.3 %shard_map.95 = (bf16[192,128]{1,0:T(8,128)(2,1)}, bf16[32,192,256]{2,1,0:T(8,128)(2,1)}) custom-call(bf16[256,128]{1,0:T(8,128)(2,1)} %dense_ref.3, bf16[256,8192]{1,0:T(8,128)(2,1)} %pooled_ref.3, bf16[256,128]{1,0:T(8,128)(2,1)} %cot_ref.3, bf16[192,2080]{1,0:T(8,128)(2,1)} %copy.12.pair_ref), custom_call_target="tpu_custom_call" | custom-call | flops 3000000000 | bytes 65536 | tf_op jit(solution)/shard_map/pallas_call | solution.py:198
  34.2 3.4 %all-to-all-done.grads_ref.codes_ref = bf16[32,80,256]{2,1,0:T(8,128)(2,1)} async-done(((bf16[32,80,256]{2,1,0:T(8,128)(2,1)}), bf16[32,80,256]{2,1,0:T(8,128)(2,1)}, u32[]{:S(2)}, u32[]{:S(2)}) %all-to-all-start) | async-done | bytes 1310752 | tf_op jit(solution)/shard_map/all_to_all | solution.py:483
  37.6 5.0 %all-to-all-start.1 = ((bf16[32,192,256]{2,1,0:T(8,128)(2,1)}), bf16[32,192,256]{2,1,0:T(8,128)(2,1)}, u32[]{:S(2)}, u32[]{:S(2)}) async-start(bf16[32,192,256]{2,1,0:T(8,128)(2,1)} %get-tuple-element.33), calls=%async_computation.1 | async-start | bytes 6291456 | tf_op jit(solution)/shard_map/all_to_all | solution.py:483
  42.6 40.9 %shard_map.96 = (f32[2,4,2,512,128]{4,3,2,1,0:T(8,128)}, s32[2,4,512,1536]{3,2,1,0:T(8,128)}, s8[2,4,2,512,1536]{4,3,2,1,0:T(32,128)(4,1)}) custom-call(s32[1]{0:T(128)} %bitcast.2.hst_ref, bf16[32,80,256]{2,1,0:T(8,128)(2,1)} %all-to-all-done.grads_ref.codes_ref, bf16[32,80,256]{2,1,0:T(8,128)(2,1)} %all-to-all-done.grads_ref.codes_ref), custom_call_target="tpu_custom_call" | custom-call | flops 5000000000 | bytes 65536 | tf_op jit(solution)/shard_map/pallas_call | solution.py:292
  83.5 0.6 all-to-all-done.1.grads_ref
  84.2 0.0 copy-start
  84.2 14.2 %shard_map.97 = (bf16[1,2,512,128]{3,2,1,0:T(8,128)(2,1)S(1)}, bf16[1,2,512,128]{3,2,1,0:T(8,128)(2,1)S(1)}, bf16[1,2,512,128]{3,2,1,0:T(8,128)(2,1)S(1)}) custom-call(s32[1]{0:T(128)} %bitcast.2.hst_ref, s32[2,4,512,1536]{3,2,1,0:T(8,128)} %get-tuple-element.35.counts_ref, bf16[32,192,256]{2,1,0:T(8,128)(2,1)} %all-to-all-done.1.grads_ref, ...), custom_call_target="tpu_custom_call" | custom-call | flops 20000000 | bytes 65536 | tf_op jit(solution)/shard_map/pallas_call | solution.py:354
  98.3 1.6 %collective-permute-start = (bf16[1,2,512,128]{3,2,1,0:T(8,128)(2,1)S(1)}, bf16[1,2,512,128]{3,2,1,0:T(8,128)(2,1)S(1)}, u32[]{:S(2)}, u32[]{:S(2)}) collective-permute-start(bf16[1,2,512,128]{3,2,1,0:T(8,128)(2,1)S(1)} %get-tuple-element.40), channel_id=1, source_target_pairs={{0,32},{32,64},{64,96},{96,0},{1,33},{33,65},{65,97},{97,1},{2,34}... | collective-permute-start | bytes 786440 | tf_op jit(solution)/shard_map/ppermute | solution.py:501
  99.9 2.7 %collective-permute-start.1 = (bf16[1,2,512,128]{3,2,1,0:T(8,128)(2,1)S(1)}, bf16[1,2,512,128]{3,2,1,0:T(8,128)(2,1)S(1)}, u32[]{:S(2)}, u32[]{:S(2)}) collective-permute-start(bf16[1,2,512,128]{3,2,1,0:T(8,128)(2,1)S(1)} %get-tuple-element.41), channel_id=1, source_target_pairs={{0,64},{32,96},{64,0},{96,32},{1,65},{33,97},{65,1},{97,33},{2,66}... | collective-permute-start | bytes 786440 | tf_op jit(solution)/shard_map/ppermute | solution.py:501
  102.6 1.4 %collective-permute-start.2 = (bf16[1,2,512,128]{3,2,1,0:T(8,128)(2,1)S(1)}, bf16[1,2,512,128]{3,2,1,0:T(8,128)(2,1)S(1)}, u32[]{:S(2)}, u32[]{:S(2)}) collective-permute-start(bf16[1,2,512,128]{3,2,1,0:T(8,128)(2,1)S(1)} %get-tuple-element.42), channel_id=1, source_target_pairs={{0,96},{32,0},{64,32},{96,64},{1,97},{33,1},{65,33},{97,65},{2,98}... | collective-permute-start | bytes 786440 | tf_op jit(solution)/shard_map/ppermute | solution.py:501
  104.0 0.0 copy-done
  104.0 12.8 %shard_map.98 = (bf16[1,2,512,128]{3,2,1,0:T(8,128)(2,1)S(1)}, bf16[1,2,512,128]{3,2,1,0:T(8,128)(2,1)S(1)}, bf16[1,2,512,128]{3,2,1,0:T(8,128)(2,1)S(1)}) custom-call(s32[1]{0:T(128)} %bitcast.2.hst_ref, s32[2,4,512,1536]{3,2,1,0:T(8,128)} %get-tuple-element.35.counts_ref, bf16[32,192,256]{2,1,0:T(8,128)(2,1)} %all-to-all-done.1.grads_ref, ...), custom_call_target="tpu_custom_call" | custom-call | flops 20000000 | bytes 65536 | tf_op jit(solution)/shard_map/pallas_call | solution.py:354
  116.9 0.9 collective-permute-start.3
  117.7 0.9 collective-permute-start.4
  118.6 0.0 collective-permute-done.rest_1_
  118.6 1.9 %collective-permute-start.5 = (bf16[1,2,512,128]{3,2,1,0:T(8,128)(2,1)S(1)}, bf16[1,2,512,128]{3,2,1,0:T(8,128)(2,1)S(1)}, u32[]{:S(2)}, u32[]{:S(2)}) collective-permute-start(bf16[1,2,512,128]{3,2,1,0:T(8,128)(2,1)S(1)} %get-tuple-element.49), channel_id=1, source_target_pairs={{0,96},{32,0},{64,32},{96,64},{1,97},{33,1},{65,33},{97,65},{2,98}... | collective-permute-start | bytes 786440 | tf_op jit(solution)/shard_map/ppermute | solution.py:501
  120.5 0.0 collective-permute-done.1.rest_2_
  120.5 0.0 collective-permute-done.2.rest_3_
  120.5 0.0 copy-start.1
  120.5 0.0 copy-start.2
  120.5 11.4 %shard_map.99.rest_0_.rest_4_ = f32[2,2,512,128]{3,2,1,0:T(8,128)S(1)} custom-call(s32[1]{0:T(128)} %bitcast.2.hst_ref, s8[2,4,2,512,1536]{4,3,2,1,0:T(32,128)(4,1)} %get-tuple-element.32.counts_ref, bf16[32,192,256]{2,1,0:T(8,128)(2,1)} %all-to-all-done.1.grads_ref, f32[2,4,2,512,128]{4,3,2,1,0:T(8,128)S(1)} %copy-done), custom_call_target="tpu_custom_call" | custom-call | flops 20000000 | bytes 65536 | tf_op jit(solution)/shard_map/pallas_call | solution.py:354
  132.0 0.0 copy-start.4
  132.0 0.0 copy-start.5
  132.0 0.0 collective-permute-done.3.rest_5_
  132.0 0.0 collective-permute-done.4.rest_6_
  132.0 0.0 collective-permute-done.5.rest_7_
  132.0 0.0 copy-done.1
  132.0 0.0 copy-done.2
  132.0 1.4 %shard_map.100 = (f32[4,512,128]{2,1,0:T(8,128)}, f32[2,512]{1,0:T(2,128)S(1)}, bf16[2,512,128]{2,1,0:T(8,128)(2,1)S(1)}) custom-call(s32[1]{0:T(128)} %bitcast.1.core_ref, f32[4,512,128]{2,1,0:T(8,128)S(1)} %copy-done.1, f32[4,512]{1,0:T(4,128)S(1)} %copy-done.2, f32[2,2,512,128]{3,2,1,0:T(8,128)S(1)} %shard_map.99.rest_0_.rest_4_, ...), custom_call_target="tpu_custom_call" | custom-call | flops 600000000 | bytes 65536 | tf_op jit(solution)/shard_map/pallas_call | solution.py:436
  133.4 0.0 collective-permute-start.6
  133.4 0.0 copy-done.4
  133.4 0.0 copy-done.5
  133.4 0.6 pad_maximum_fusion
  134.1 0.9 collective-permute-done.6.grads_ref
  134.9 1.3 shard_map.101
Async XLA Ops:
  0.6 16.2 %copy-start.3 = (bf16[256,2080]{0,1:T(8,128)(2,1)S(1)}, bf16[256,2080]{0,1:T(8,128)(2,1)}, u32[]{:S(2)}) copy-start(bf16[256,2080]{0,1:T(8,128)(2,1)} %param.10) | copy-start | bytes 3194884
  8.2 29.3 %all-to-all-start = ((bf16[32,80,256]{2,1,0:T(8,128)(2,1)}), bf16[32,80,256]{2,1,0:T(8,128)(2,1)}, u32[]{:S(2)}, u32[]{:S(2)}) async-start(bf16[32,80,256]{2,1,0:T(8,128)(2,1)} %get-tuple-element.31), calls=%async_computation | async-start | bytes 2621440 | tf_op jit(solution)/shard_map/all_to_all | solution.py:483
  37.6 46.6 %all-to-all-start.1 = ((bf16[32,192,256]{2,1,0:T(8,128)(2,1)}), bf16[32,192,256]{2,1,0:T(8,128)(2,1)}, u32[]{:S(2)}, u32[]{:S(2)}) async-start(bf16[32,192,256]{2,1,0:T(8,128)(2,1)} %get-tuple-element.33), calls=%async_computation.1 | async-start | bytes 6291456 | tf_op jit(solution)/shard_map/all_to_all | solution.py:483
  84.2 19.9 %copy-start = (f32[2,4,2,512,128]{4,3,2,1,0:T(8,128)S(1)}, f32[2,4,2,512,128]{4,3,2,1,0:T(8,128)}, u32[]{:S(2)}) copy-start(f32[2,4,2,512,128]{4,3,2,1,0:T(8,128)} %get-tuple-element.43.before_ref) | copy-start | bytes 12582916
  98.3 20.3 %collective-permute-start = (bf16[1,2,512,128]{3,2,1,0:T(8,128)(2,1)S(1)}, bf16[1,2,512,128]{3,2,1,0:T(8,128)(2,1)S(1)}, u32[]{:S(2)}, u32[]{:S(2)}) collective-permute-start(bf16[1,2,512,128]{3,2,1,0:T(8,128)(2,1)S(1)} %get-tuple-element.40), channel_id=1, source_target_pairs={{0,32},{32,64},{64,96},{96,0},{1,33},{33,65},{65,97},{97,1},{2,34}... | collective-permute-start | bytes 786440 | tf_op jit(solution)/shard_map/ppermute | solution.py:501
  99.9 20.6 %collective-permute-start.1 = (bf16[1,2,512,128]{3,2,1,0:T(8,128)(2,1)S(1)}, bf16[1,2,512,128]{3,2,1,0:T(8,128)(2,1)S(1)}, u32[]{:S(2)}, u32[]{:S(2)}) collective-permute-start(bf16[1,2,512,128]{3,2,1,0:T(8,128)(2,1)S(1)} %get-tuple-element.41), channel_id=1, source_target_pairs={{0,64},{32,96},{64,0},{96,32},{1,65},{33,97},{65,1},{97,33},{2,66}... | collective-permute-start | bytes 786440 | tf_op jit(solution)/shard_map/ppermute | solution.py:501
  102.6 17.9 %collective-permute-start.2 = (bf16[1,2,512,128]{3,2,1,0:T(8,128)(2,1)S(1)}, bf16[1,2,512,128]{3,2,1,0:T(8,128)(2,1)S(1)}, u32[]{:S(2)}, u32[]{:S(2)}) collective-permute-start(bf16[1,2,512,128]{3,2,1,0:T(8,128)(2,1)S(1)} %get-tuple-element.42), channel_id=1, source_target_pairs={{0,96},{32,0},{64,32},{96,64},{1,97},{33,1},{65,33},{97,65},{2,98}... | collective-permute-start | bytes 786440 | tf_op jit(solution)/shard_map/ppermute | solution.py:501
  116.9 15.1 %collective-permute-start.3 = (bf16[1,2,512,128]{3,2,1,0:T(8,128)(2,1)S(1)}, bf16[1,2,512,128]{3,2,1,0:T(8,128)(2,1)S(1)}, u32[]{:S(2)}, u32[]{:S(2)}) collective-permute-start(bf16[1,2,512,128]{3,2,1,0:T(8,128)(2,1)S(1)} %get-tuple-element.47), channel_id=1, source_target_pairs={{0,32},{32,64},{64,96},{96,0},{1,33},{33,65},{65,97},{97,1},{2,34}... | collective-permute-start | bytes 786440 | tf_op jit(solution)/shard_map/ppermute | solution.py:501
  117.7 14.2 %collective-permute-start.4 = (bf16[1,2,512,128]{3,2,1,0:T(8,128)(2,1)S(1)}, bf16[1,2,512,128]{3,2,1,0:T(8,128)(2,1)S(1)}, u32[]{:S(2)}, u32[]{:S(2)}) collective-permute-start(bf16[1,2,512,128]{3,2,1,0:T(8,128)(2,1)S(1)} %get-tuple-element.48), channel_id=1, source_target_pairs={{0,64},{32,96},{64,0},{96,32},{1,65},{33,97},{65,1},{97,33},{2,66}... | collective-permute-start | bytes 786440 | tf_op jit(solution)/shard_map/ppermute | solution.py:501
  118.6 13.4 %collective-permute-start.5 = (bf16[1,2,512,128]{3,2,1,0:T(8,128)(2,1)S(1)}, bf16[1,2,512,128]{3,2,1,0:T(8,128)(2,1)S(1)}, u32[]{:S(2)}, u32[]{:S(2)}) collective-permute-start(bf16[1,2,512,128]{3,2,1,0:T(8,128)(2,1)S(1)} %get-tuple-element.49), channel_id=1, source_target_pairs={{0,96},{32,0},{64,32},{96,64},{1,97},{33,1},{65,33},{97,65},{2,98}... | collective-permute-start | bytes 786440 | tf_op jit(solution)/shard_map/ppermute | solution.py:501
  120.5 11.5 %copy-start.1 = (f32[4,512,128]{2,1,0:T(8,128)S(1)}, f32[4,512,128]{2,1,0:T(8,128)}, u32[]{:S(2)}) copy-start(f32[4,512,128]{2,1,0:T(8,128)} %weights_ref.3) | copy-start | bytes 3145732
  120.5 11.5 %copy-start.2 = (f32[4,512]{1,0:T(4,128)S(1)}, f32[4,512]{1,0:T(4,128)}, u32[]{:S(2)}) copy-start(f32[4,512]{1,0:T(4,128)} %accum_ref.3) | copy-start | bytes 24580
  132.0 1.5 %copy-start.4 = (bf16[192,128]{1,0:T(8,128)(2,1)S(1)}, bf16[192,128]{1,0:T(8,128)(2,1)}, u32[]{:S(2)}) copy-start(bf16[192,128]{1,0:T(8,128)(2,1)} %get-tuple-element.30) | copy-start | bytes 147460
  132.0 1.5 %copy-start.5 = (bf16[64,128]{1,0:T(8,128)(2,1)S(1)}, bf16[64,128]{1,0:T(8,128)(2,1)}, u32[]{:S(2)}) copy-start(bf16[64,128]{1,0:T(8,128)(2,1)} %get-tuple-element.29) | copy-start | bytes 49156
  133.4 1.5 %collective-permute-start.6 = (bf16[2,512,128]{2,1,0:T(8,128)(2,1)S(1)}, bf16[2,512,128]{2,1,0:T(8,128)(2,1)S(1)}, u32[]{:S(2)}, u32[]{:S(2)}) collective-permute-start(bf16[2,512,128]{2,1,0:T(8,128)(2,1)S(1)} %get-tuple-element.50), channel_id=1, source_target_pairs={{0,16},{16,0},{1,17},{17,1},{2,18},{18,2},{3,19},{19,3},{4,20},{20... | collective-permute-start | bytes 786440 | tf_op jit(solution)/shard_map/ppermute | solution.py:452
